TPU v7x, 32 devices: a whole 2x2x4 slice. The times are simulated.
32 devices in a mesh: groups: 2 (over y), edge: 16 (over z, x, core).
Axes of the slice: x: 2, y: 2, z: 4, core: 2. Of those that a mesh axis runs over, the one named last changes fastest.
Arguments:
- features: bfloat16 [64, 256, 128], P(('groups', 'edge')), parts along dimension 0, may hold values from -6 to 6
- context: bfloat16 [64, 256, 128], P(('groups', 'edge')), parts along dimension 0, may hold values from -6 to 6
- states: bfloat16 [64, 12, 256, 128], P(('groups', 'edge')), parts along dimension 0, may hold values from -3 to 3
- neighbours: int32 [64, 12], P(('groups', 'edge')), parts along dimension 0, may hold values from 0 to 31, as said below
- depths: float32 [64, 256], P(('groups', 'edge')), parts along dimension 0, may hold values from 0.5 to 2
- damping: float32 [64, 256], P(('groups', 'edge')), parts along dimension 0, may hold values from 0.5 to 32
- w_corr: bfloat16 [49, 128], replicated, may hold values from -0.875 to 0.875
- w_gates: bfloat16 [256, 256], replicated, may hold values from -0.375 to 0.375
- w_cand: bfloat16 [9, 128, 128], replicated, may hold values from -0.1875 to 0.1875
- w_motion: bfloat16 [128, 128], replicated, may hold values from -0.5 to 0.5
- w_heads: bfloat16 [2, 128], replicated, may hold values from -0.5 to 0.5
Outputs:
- new_states: bfloat16 [64, 12, 256, 128], P(('groups', 'edge')), parts along dimension 0
- new_depths: float32 [64, 256], P(('groups', 'edge')), parts along dimension 0
There are 2 independent parts, one for each index of `groups`. A program takes and returns all parts, laid end to end along the dimension named above; an argument that names none is the same for every part. Nothing has to cross between parts.
Inputs may be any that keep to these rules, and one draw needn't show every extreme that they name: Each row neighbours[f] names 12 different keyframes, none equal to f, and every named t satisfies |t // 2 - f // 2| <= 6.
All inputs are finite; a program needn't handle non-finite values.
Results may differ from a plain program's by a relative error of at most 0.0048.
Values may be sent and summed in bfloat16 or wider, within the bound.
No kernel may reach another device: no remote copies, remote signals or barrier semaphores. Data moves between devices by JAX's collectives and lax.ppermute only.
A program may use at most 64 MiB of HBM per device.

v0:
```python
import math

import jax
import jax.numpy as jnp
from jax import lax
from jax.sharding import PartitionSpec as P

REACH = 6
CORR_X = 3
CORR_Y = 3
WIDTH = 64
ROWS = 4


def passed_along(value, axis, steps):
    count = lax.axis_size(axis)
    first, last = (max(0, -steps), min(count, count - steps))
    return lax.ppermute(value, axis, [(source, source + steps) for source in range(first, last)])


def correlate(source, target):
    pixels = source.shape[0]
    channels = source.shape[-1]
    spread = CORR_Y * WIDTH + CORR_X
    padded = jnp.pad(target, ((0, 0), (spread, spread), (0, 0)))
    pixel_ids = lax.iota(jnp.int32, pixels)
    row_ids = pixel_ids // WIDTH
    col_ids = pixel_ids % WIDTH
    inv_root = 1.0 / math.sqrt(channels)
    columns = []
    for row_step in range(-CORR_Y, CORR_Y + 1):
        for col_step in range(-CORR_X, CORR_X + 1):
            place = spread + row_step * WIDTH + col_step
            shifted = padded[:, place : place + pixels, :]
            summed = jnp.einsum("epc,pc->ep", shifted, source, preferred_element_type=jnp.float32)
            inside = (
                (row_ids + row_step >= 0)
                & (row_ids + row_step < ROWS)
                & (col_ids + col_step >= 0)
                & (col_ids + col_step < WIDTH)
            )
            columns.append(
                (summed * inside.astype(jnp.float32)[None] * inv_root).astype(jnp.bfloat16)
            )
    return jnp.stack(columns, 0)


def update_block(source, ctx_rows, state_rows, target, w_corr, w_gates, w_cand, w_motion, w_heads):
    edge_count = state_rows.shape[0]
    channels = source.shape[-1]
    correlation = correlate(source, target)
    encoded = jax.nn.relu(
        jnp.einsum("oep,oc->epc", correlation, w_corr, preferred_element_type=jnp.float32)
    )
    motion = (
        (encoded + ctx_rows.astype(jnp.float32)[None]).astype(jnp.bfloat16).reshape(-1, channels)
    )
    hidden = state_rows.reshape(-1, channels)
    gate_pre = jnp.dot(
        jnp.concatenate([hidden, motion], -1), w_gates, preferred_element_type=jnp.float32
    )
    update = jax.nn.sigmoid(gate_pre[:, :channels])
    reset_gate = jax.nn.sigmoid(gate_pre[:, channels:])
    reset_state = (reset_gate * hidden.astype(jnp.float32)).astype(jnp.bfloat16)
    reset_state = reset_state.reshape(edge_count, ROWS, WIDTH, channels)
    framed = jnp.pad(reset_state, ((0, 0), (1, 1), (1, 1), (0, 0)))
    conv_sum = jnp.dot(motion, w_motion, preferred_element_type=jnp.float32)
    for row_step in range(3):
        for col_step in range(3):
            tap = framed[:, row_step : row_step + ROWS, col_step : col_step + WIDTH, :].reshape(
                -1, channels
            )
            conv_sum = conv_sum + jnp.dot(
                tap, w_cand[3 * row_step + col_step], preferred_element_type=jnp.float32
            )
    candidate = jnp.tanh(conv_sum)
    new_hidden = ((1.0 - update) * hidden.astype(jnp.float32) + update * candidate).astype(
        jnp.bfloat16
    )
    head_out = jnp.dot(new_hidden, jnp.transpose(w_heads), preferred_element_type=jnp.float32)
    revision = head_out[:, 0]
    confidence = jax.nn.sigmoid(head_out[:, 1])
    return (
        new_hidden.reshape(edge_count, -1, channels),
        (confidence * revision).reshape(edge_count, -1),
        confidence.reshape(edge_count, -1),
    )


def on_device(
    features,
    context,
    states,
    neighbours,
    depths,
    damping,
    w_corr,
    w_gates,
    w_cand,
    w_motion,
    w_heads,
):
    frames_here = features.shape[0]
    own_block = lax.axis_index("edge")
    below_side = features
    above_side = features
    covered = 1
    while covered < REACH + 1:
        sending = min(covered, REACH + 1 - covered)
        tail_part = below_side[below_side.shape[0] - sending * frames_here :]
        head_part = above_side[: sending * frames_here]
        below_side = jnp.concatenate([passed_along(tail_part, "edge", covered), below_side], 0)
        above_side = jnp.concatenate([above_side, passed_along(head_part, "edge", -covered)], 0)
        covered = covered + sending
    window = jnp.concatenate([below_side, above_side[frames_here:]], 0)
    local_index = neighbours - (own_block - REACH) * frames_here
    targets = jnp.take(window, local_index.reshape(-1), axis=0)
    targets = targets.reshape((frames_here, neighbours.shape[1]) + features.shape[1:])

    def per_frame(items):
        source, ctx_rows, state_rows, target = items
        return update_block(
            source, ctx_rows, state_rows, target, w_corr, w_gates, w_cand, w_motion, w_heads
        )

    new_states, pushed, confidence = lax.map(per_frame, (features, context, states, targets))
    pixels = depths.shape[1]
    values = jnp.concatenate([pushed, confidence], -1).reshape(-1, 2 * pixels)
    window_frames = window.shape[0]
    slots = lax.iota(jnp.int32, window_frames)
    selector = (local_index.reshape(-1)[:, None] == slots[None, :]).astype(jnp.float32)
    partial_sums = jnp.einsum(
        "er,ec->rc",
        selector,
        values,
        precision=lax.Precision.HIGHEST,
        preferred_element_type=jnp.float32,
    )
    sums = partial_sums[REACH * frames_here : (REACH + 1) * frames_here]
    for offset in range(-REACH, REACH + 1):
        if offset != 0:
            block_part = partial_sums[
                (offset + REACH) * frames_here : (offset + REACH + 1) * frames_here
            ]
            sums = sums + passed_along(block_part, "edge", offset)
    new_depths = depths + sums[:, :pixels] / (damping + sums[:, pixels:])
    return (new_states, new_depths)


def solution(mesh):
    return jax.shard_map(
        on_device,
        mesh=mesh,
        in_specs=(
            P(("groups", "edge"), None, None),
            P(("groups", "edge"), None, None),
            P(("groups", "edge"), None, None, None),
            P(("groups", "edge"), None),
            P(("groups", "edge"), None),
            P(("groups", "edge"), None),
            P(),
            P(),
            P(),
            P(),
            P(),
        ),
        out_specs=(P(("groups", "edge"), None, None, None), P(("groups", "edge"), None)),
        check_vma=False,
    )
```

profile of v0, /device:TPU:0, one launch (start us, length us, event | category | flops | bytes accessed | tf_op | source)
XLA Modules:
  0.0 501.4 jit_solution(18246480661819224454)
XLA Ops:
  4.3 4.2 collective-permute-done.3
  9.6 5.3 %collective-permute-start.1 = (bf16[4,256,128]{2,1,0:T(8,128)(2,1)S(1)}, bf16[4,256,128]{2,1,0:T(8,128)(2,1)S(1)}, u32[]{:S(2)}, u32[]{:S(2)}) collective-permute-start(bf16[4,256,128]{2,1,0:T(8,128)(2,1)S(1)} %get-tuple-element.311), channel_id=1, source_target_pairs={{0,2},{1,3},{2,4},{3,5},{4,6},{5,7},{6,8},{7,9},{8,10},{9,11},{10,... | collective-permute-start | bytes 786440 | tf_op jit(solution)/shard_map/ppermute | solution.py:18
  16.2 3.7 collective-permute-done.1
  19.9 5.6 %collective-permute-done.4 = bf16[4,256,128]{2,1,0:T(8,128)(2,1)S(1)} collective-permute-done((bf16[4,256,128]{2,1,0:T(8,128)(2,1)S(1)}, bf16[4,256,128]{2,1,0:T(8,128)(2,1)S(1)}, u32[]{:S(2)}, u32[]{:S(2)}) %collective-permute-start.4) | collective-permute-done | bytes 262176 | tf_op jit(solution)/shard_map/ppermute | solution.py:18
  26.6 7.7 %collective-permute-start.2 = (bf16[6,256,128]{2,1,0:T(8,128)(2,1)S(1)}, bf16[6,256,128]{2,1,0:T(8,128)(2,1)S(1)}, u32[]{:S(2)}, u32[]{:S(2)}) collective-permute-start(bf16[6,256,128]{2,1,0:T(8,128)(2,1)S(1)} %get-tuple-element.309), channel_id=1, source_target_pairs={{0,4},{1,5},{2,6},{3,7},{4,8},{5,9},{6,10},{7,11},{8,12},{9,13},{1... | collective-permute-start | bytes 1179656 | tf_op jit(solution)/shard_map/ppermute | solution.py:18
  36.3 6.6 %collective-permute-done.2 = bf16[6,256,128]{2,1,0:T(8,128)(2,1)S(1)} collective-permute-done((bf16[6,256,128]{2,1,0:T(8,128)(2,1)S(1)}, bf16[6,256,128]{2,1,0:T(8,128)(2,1)S(1)}, u32[]{:S(2)}, u32[]{:S(2)}) %collective-permute-start.2) | collective-permute-done | bytes 393248 | tf_op jit(solution)/shard_map/ppermute | solution.py:18
  52.2 414.0 %while.16 = (s32[]{:T(128)}, bf16[2,12,256,128]{3,2,1,0:T(8,128)(2,1)}, f32[2,12,256]{2,1,0:T(8,128)}, f32[2,12,256]{2,1,0:T(8,128)}, bf16[2,12,256,128]{3,2,1,0...) while((s32[]{:T(128)}, ...), condition=%wide.region_1.2_spmd, body=%wide.region_0.1_spmd.sunk | while | flops 1502366464 | bytes 156670800 | solution.py:126
  53.4 4.6 pad_slice_fusion.61
  63.9 2.5 fusion.721
  68.0 2.5 fusion.723
  108.8 2.5 fusion.743
  125.9 5.3 %pad_slice_fusion.62 = (bf16[12,256,128]{2,1,0:T(8,128)(2,1)S(1)}, bf16[12,256,128]{2,1,0:T(8,128)(2,1)S(1)}, bf16[12,256,128]{2,1,0:T(8,128)(2,1)}, bf16[12,256...) fusion(bf16[12,256,128]{2,1,0:T(8,128)(2,1)S(1)} %dynamic-slice, ...), kind=kLoop, calls=%fused_computation.2.clone.1 | loop fusion | bytes 15728640 | tf_op jit(solution)/shard_map/while/body/eval_jaxpr/slice | solution.py:34
  146.4 2.5 fusion.761
  187.1 2.5 fusion.783
  205.2 2.5 pad_slice_fusion.60
  222.9 2.5 fusion.799
  246.8 2.5 pad_slice_fusion.63
  259.9 4.6 pad_slice_fusion.61
  270.4 2.5 fusion.721
  274.5 2.5 fusion.723
  315.3 2.5 fusion.743
  332.0 5.3 %pad_slice_fusion.62 = (bf16[12,256,128]{2,1,0:T(8,128)(2,1)S(1)}, bf16[12,256,128]{2,1,0:T(8,128)(2,1)S(1)}, bf16[12,256,128]{2,1,0:T(8,128)(2,1)}, bf16[12,256...) fusion(bf16[12,256,128]{2,1,0:T(8,128)(2,1)S(1)} %dynamic-slice, ...), kind=kLoop, calls=%fused_computation.2.clone.1 | loop fusion | bytes 15728640 | tf_op jit(solution)/shard_map/while/body/eval_jaxpr/slice | solution.py:34
  352.5 2.5 fusion.761
  411.3 2.5 pad_slice_fusion.60
  429.0 2.5 fusion.799
  452.9 2.7 pad_slice_fusion.63
  470.6 3.0 collective-permute-start.12
  473.6 4.6 collective-permute-start.13
  478.1 4.2 collective-permute-start.14
  482.3 3.5 collective-permute-start.15
  485.8 2.5 collective-permute-start.16
  488.4 2.6 collective-permute-start.17
  (726 shorter events, 377.6 us)
Async XLA Ops:
  0.6 33.6 %copy-start.50 = (s32[2,12]{1,0:T(2,128)S(1)}, s32[2,12]{1,0:T(2,128)}, u32[]{:S(2)}) copy-start(s32[2,12]{1,0:T(2,128)} %param.16) | copy-start | bytes 292
  0.6 3.7 collective-permute-start
  3.0 5.6 %collective-permute-start.3 = (bf16[2,256,128]{2,1,0:T(8,128)(2,1)}, bf16[2,256,128]{2,1,0:T(8,128)(2,1)S(1)}, u32[]{:S(2)}, u32[]{:S(2)}) collective-permute-start(bf16[2,256,128]{2,1,0:T(8,128)(2,1)} %param.13), channel_id=1, source_target_pairs={{1,0},{2,1},{3,2},{4,3},{5,4},{6,5},{7,6},{8,7},{9,8},{10,9},{11,1... | collective-permute-start | bytes 393224 | tf_op jit(solution)/shard_map/ppermute | solution.py:18
  9.6 10.3 %collective-permute-start.1 = (bf16[4,256,128]{2,1,0:T(8,128)(2,1)S(1)}, bf16[4,256,128]{2,1,0:T(8,128)(2,1)S(1)}, u32[]{:S(2)}, u32[]{:S(2)}) collective-permute-start(bf16[4,256,128]{2,1,0:T(8,128)(2,1)S(1)} %get-tuple-element.311), channel_id=1, source_target_pairs={{0,2},{1,3},{2,4},{3,5},{4,6},{5,7},{6,8},{7,9},{8,10},{9,11},{10,... | collective-permute-start | bytes 786440 | tf_op jit(solution)/shard_map/ppermute | solution.py:18
  14.9 10.6 %collective-permute-start.4 = (bf16[4,256,128]{2,1,0:T(8,128)(2,1)S(1)}, bf16[4,256,128]{2,1,0:T(8,128)(2,1)S(1)}, u32[]{:S(2)}, u32[]{:S(2)}) collective-permute-start(bf16[4,256,128]{2,1,0:T(8,128)(2,1)S(1)} %get-tuple-element.310), channel_id=1, source_target_pairs={{2,0},{3,1},{4,2},{5,3},{6,4},{7,5},{8,6},{9,7},{10,8},{11,9},{12,... | collective-permute-start | bytes 786440 | tf_op jit(solution)/shard_map/ppermute | solution.py:18
  16.2 28.8 %copy-start.2 = (bf16[2,256,128]{2,1,0:T(8,128)(2,1)S(1)}, bf16[2,256,128]{2,1,0:T(8,128)(2,1)}, u32[]{:S(2)}) copy-start(bf16[2,256,128]{2,1,0:T(8,128)(2,1)} %param.13) | copy-start | bytes 393220
  26.6 16.3 %collective-permute-start.2 = (bf16[6,256,128]{2,1,0:T(8,128)(2,1)S(1)}, bf16[6,256,128]{2,1,0:T(8,128)(2,1)S(1)}, u32[]{:S(2)}, u32[]{:S(2)}) collective-permute-start(bf16[6,256,128]{2,1,0:T(8,128)(2,1)S(1)} %get-tuple-element.309), channel_id=1, source_target_pairs={{0,4},{1,5},{2,6},{3,7},{4,8},{5,9},{6,10},{7,11},{8,12},{9,13},{1... | collective-permute-start | bytes 1179656 | tf_op jit(solution)/shard_map/ppermute | solution.py:18
  35.0 12.7 %collective-permute-start.5 = (bf16[6,256,128]{2,1,0:T(8,128)(2,1)S(1)}, bf16[6,256,128]{2,1,0:T(8,128)(2,1)S(1)}, u32[]{:S(2)}, u32[]{:S(2)}) collective-permute-start(bf16[6,256,128]{2,1,0:T(8,128)(2,1)S(1)} %get-tuple-element.308), channel_id=1, source_target_pairs={{4,0},{5,1},{6,2},{7,3},{8,4},{9,5},{10,6},{11,7},{12,8},{13,9},{1... | collective-permute-start | bytes 1179656 | tf_op jit(solution)/shard_map/ppermute | solution.py:18
  50.9 1.4 copy-start.1
  239.4 1.9 copy-start.5
  241.2 4.4 copy-start
  243.6 2.1 copy-start.4
  246.8 2.6 copy-start.44
  253.3 1.4 copy-start.3
  445.5 1.9 copy-start.5
  446.2 1.3 copy-start.7
  447.3 4.4 copy-start
  449.7 2.1 copy-start.4
  452.9 2.8 copy-start.44
  459.6 1.4 copy-start.3
  468.0 14.4 %collective-permute-start.10 = (f32[2,512]{1,0:T(2,128)S(1)}, f32[2,512]{1,0:T(2,128)S(1)}, u32[]{:S(2)}, u32[]{:S(2)}) collective-permute-start(f32[2,512]{1,0:T(2,128)S(1)} %get-tuple-element.320), channel_id=1, source_target_pairs={{2,0},{3,1},{4,2},{5,3},{6,4},{7,5},{8,6},{9,7},{10,8},{11,9},{12,... | collective-permute-start | bytes 12296 | tf_op jit(solution)/shard_map/ppermute | solution.py:18
  469.3 16.6 %collective-permute-start.11 = (f32[2,512]{1,0:T(2,128)S(1)}, f32[2,512]{1,0:T(2,128)S(1)}, u32[]{:S(2)}, u32[]{:S(2)}) collective-permute-start(f32[2,512]{1,0:T(2,128)S(1)} %get-tuple-element.319), channel_id=1, source_target_pairs={{1,0},{2,1},{3,2},{4,3},{5,4},{6,5},{7,6},{8,7},{9,8},{10,9},{11,1... | collective-permute-start | bytes 12296 | tf_op jit(solution)/shard_map/ppermute | solution.py:18
  470.6 17.8 %collective-permute-start.12 = (f32[2,512]{1,0:T(2,128)S(1)}, f32[2,512]{1,0:T(2,128)S(1)}, u32[]{:S(2)}, u32[]{:S(2)}) collective-permute-start(f32[2,512]{1,0:T(2,128)S(1)} %get-tuple-element.318), channel_id=1, source_target_pairs={{0,1},{1,2},{2,3},{3,4},{4,5},{5,6},{6,7},{7,8},{8,9},{9,10},{10,1... | collective-permute-start | bytes 12296 | tf_op jit(solution)/shard_map/ppermute | solution.py:18
  473.6 17.4 %collective-permute-start.13 = (f32[2,512]{1,0:T(2,128)S(1)}, f32[2,512]{1,0:T(2,128)S(1)}, u32[]{:S(2)}, u32[]{:S(2)}) collective-permute-start(f32[2,512]{1,0:T(2,128)S(1)} %get-tuple-element.317), channel_id=1, source_target_pairs={{0,2},{1,3},{2,4},{3,5},{4,6},{5,7},{6,8},{7,9},{8,10},{9,11},{10,... | collective-permute-start | bytes 12296 | tf_op jit(solution)/shard_map/ppermute | solution.py:18
  478.1 14.2 %collective-permute-start.14 = (f32[2,512]{1,0:T(2,128)S(1)}, f32[2,512]{1,0:T(2,128)S(1)}, u32[]{:S(2)}, u32[]{:S(2)}) collective-permute-start(f32[2,512]{1,0:T(2,128)S(1)} %get-tuple-element.316), channel_id=1, source_target_pairs={{0,3},{1,4},{2,5},{3,6},{4,7},{5,8},{6,9},{7,10},{8,11},{9,12},{10... | collective-permute-start | bytes 12296 | tf_op jit(solution)/shard_map/ppermute | solution.py:18
  482.3 11.3 %collective-permute-start.15 = (f32[2,512]{1,0:T(2,128)S(1)}, f32[2,512]{1,0:T(2,128)S(1)}, u32[]{:S(2)}, u32[]{:S(2)}) collective-permute-start(f32[2,512]{1,0:T(2,128)S(1)} %get-tuple-element.315), channel_id=1, source_target_pairs={{0,4},{1,5},{2,6},{3,7},{4,8},{5,9},{6,10},{7,11},{8,12},{9,13},{1... | collective-permute-start | bytes 12296 | tf_op jit(solution)/shard_map/ppermute | solution.py:18
  485.8 9.1 %collective-permute-start.16 = (f32[2,512]{1,0:T(2,128)S(1)}, f32[2,512]{1,0:T(2,128)S(1)}, u32[]{:S(2)}, u32[]{:S(2)}) collective-permute-start(f32[2,512]{1,0:T(2,128)S(1)} %get-tuple-element.314), channel_id=1, source_target_pairs={{0,5},{1,6},{2,7},{3,8},{4,9},{5,10},{6,11},{7,12},{8,13},{9,14},{... | collective-permute-start | bytes 12296 | tf_op jit(solution)/shard_map/ppermute | solution.py:18
  488.4 7.9 %collective-permute-start.17 = (f32[2,512]{1,0:T(2,128)S(1)}, f32[2,512]{1,0:T(2,128)S(1)}, u32[]{:S(2)}, u32[]{:S(2)}) collective-permute-start(f32[2,512]{1,0:T(2,128)S(1)} %get-tuple-element.313), channel_id=1, source_target_pairs={{0,6},{1,7},{2,8},{3,9},{4,10},{5,11},{6,12},{7,13},{8,14},{9,15},... | collective-permute-start | bytes 12296 | tf_op jit(solution)/shard_map/ppermute | solution.py:18
  491.0 6.4 %collective-permute-start.6 = (f32[2,512]{1,0:T(2,128)S(1)}, f32[2,512]{1,0:T(2,128)S(1)}, u32[]{:S(2)}, u32[]{:S(2)}) collective-permute-start(f32[2,512]{1,0:T(2,128)S(1)} %get-tuple-element.312), channel_id=1, source_target_pairs={{6,0},{7,1},{8,2},{9,3},{10,4},{11,5},{12,6},{13,7},{14,8},{15,9},... | collective-permute-start | bytes 12296 | tf_op jit(solution)/shard_map/ppermute | solution.py:18
  492.3 5.1 %collective-permute-start.7 = (f32[2,512]{1,0:T(2,128)S(1)}, f32[2,512]{1,0:T(2,128)S(1)}, u32[]{:S(2)}, u32[]{:S(2)}) collective-permute-start(f32[2,512]{1,0:T(2,128)S(1)} %get-tuple-element.323), channel_id=1, source_target_pairs={{5,0},{6,1},{7,2},{8,3},{9,4},{10,5},{11,6},{12,7},{13,8},{14,9},{... | collective-permute-start | bytes 12296 | tf_op jit(solution)/shard_map/ppermute | solution.py:18
  493.6 5.5 %collective-permute-start.8 = (f32[2,512]{1,0:T(2,128)S(1)}, f32[2,512]{1,0:T(2,128)S(1)}, u32[]{:S(2)}, u32[]{:S(2)}) collective-permute-start(f32[2,512]{1,0:T(2,128)S(1)} %get-tuple-element.322), channel_id=1, source_target_pairs={{4,0},{5,1},{6,2},{7,3},{8,4},{9,5},{10,6},{11,7},{12,8},{13,9},{1... | collective-permute-start | bytes 12296 | tf_op jit(solution)/shard_map/ppermute | solution.py:18
  494.9 4.9 collective-permute-start.9
  (85 other events, 108.2 us)
where the time goes:
time: 511 us; the launch traced here: 501 us
  matrix products  219 us (43%)
  local copies, waits for them, and re-layouts  188 us (37%)
  starting transfers between devices  47.3 us (9%)
  waiting for transfers between devices  24.4 us (5%)
  loops' own time  11.8 us (2%)
  other arithmetic  9.8 us (2%)
    dot_general x98, matrix products, correlate(): jnp.einsum('epc,pc->ep', shifted, source, preferred_element_type=jnp.floa...  207 us
    dot_general x98, local copies, waits for them, and re-layouts, correlate(): jnp.einsum('epc,pc->ep', shifted, source, preferred_element_type=jnp.floa...  85.2 us
    another operation x100, local copies, waits for them, and re-layouts, correlate(): return jnp.stack(columns, 0)  59.2 us
    ppermute x18, starting transfers between devices, passed_along(): lax.ppermute(value, axis, [(source, source + steps) for source in range(f...  47.3 us
    slice x6, local copies, waits for them, and re-layouts, correlate(): shifted = padded[:, place:place + pixels, :]  25 us
    ppermute x18, waiting for transfers between devices, passed_along(): lax.ppermute(value, axis, [(source, source + steps) for source in range(f...  24.4 us
    another operation x1, loops' own time, on_device(): lax.map(per_frame, (features, context, states, targets))  11.8 us
  transfers between devices with their start and end apart: 18, of which 8 were waited for; matrix products, arithmetic and copies ran while one was open for 1% of the time, Pallas kernels for 0%

commit v1 on v0

v1 whole, which is shorter than its diff:
```python
import functools
import math

import jax
import jax.numpy as jnp
import numpy as np
from jax import lax
from jax.experimental import pallas as pl
from jax.experimental.pallas import tpu as pltpu
from jax.sharding import PartitionSpec as P

REACH = 6
CORR_X = 3
CORR_Y = 3
WIDTH = 64
ROWS = 4
PIX = ROWS * WIDTH
EDGES_PER_STEP = 4


def passed_along(value, axis, steps):
    count = lax.axis_size(axis)
    first, last = (max(0, -steps), min(count, count - steps))
    return lax.ppermute(value, axis, [(source, source + steps) for source in range(first, last)])


def corr_picks():
    side = 2 * CORR_X + 1
    picks = np.zeros((ROWS, PIX, (2 * CORR_Y + 1) * side), np.float32)
    for y in range(ROWS):
        for y2 in range(ROWS):
            if abs(y2 - y) <= CORR_Y:
                for dx in range(-CORR_X, CORR_X + 1):
                    picks[y, (y2 * WIDTH + WIDTH - 1 - dx) % PIX, (y2 - y + CORR_Y) * side + dx + CORR_X] = 1
    return picks.reshape(ROWS * PIX, -1)


def edge_kernel(
    edges, index_ref, feat_ref, ctx_ref, state_ref, window_ref, w_corr_ref, w_gates_ref,
    w_conv_ref, w_heads_ref, new_ref, sums_ref
):
    frame = pl.program_id(0)
    part = pl.program_id(1)
    chans = feat_ref.shape[-1]
    block = edges * WIDTH

    @pl.when((frame == 0) & (part == 0))
    def _():
        sums_ref[...] = jnp.zeros_like(sums_ref)

    slots = [index_ref[frame, part * edges + g] for g in range(edges)]
    source = feat_ref[0]
    inv_root = 1.0 / math.sqrt(chans)
    xs = lax.broadcasted_iota(jnp.int32, (WIDTH, PIX), 0)
    dxs = lax.broadcasted_iota(jnp.int32, (WIDTH, PIX), 1)
    dxs = WIDTH // 2 - (dxs + 1 + WIDTH // 2) % WIDTH
    valid = ((xs + dxs >= 0) & (xs + dxs < WIDTH)).astype(jnp.float32)
    skewed = [[] for _ in range(ROWS)]
    for g in range(edges):
        scores = lax.dot_general(
            source, window_ref[slots[g]], (((1,), (1,)), ((), ())),
            preferred_element_type=jnp.float32,
        )
        for y in range(ROWS):
            rolled = pltpu.roll(
                scores[y * WIDTH : (y + 1) * WIDTH], 0, 1, stride=1, stride_axis=0
            )
            skewed[y].append((rolled * valid * inv_root).astype(jnp.bfloat16))
    motions = []
    for y in range(ROWS):
        encoded = jnp.dot(
            jnp.concatenate(skewed[y], 0), w_corr_ref[y], preferred_element_type=jnp.float32
        )
        ctx = ctx_ref[0, y * WIDTH : (y + 1) * WIDTH].astype(jnp.float32)
        ctx = jnp.concatenate([ctx] * edges, 0)
        motions.append((jnp.maximum(encoded, 0.0) + ctx).astype(jnp.bfloat16))
    motion = jnp.concatenate(motions, 0)
    hidden = jnp.concatenate(
        [
            state_ref[0, g, y * WIDTH : (y + 1) * WIDTH]
            for y in range(ROWS)
            for g in range(edges)
        ],
        0,
    )
    gate_pre = jnp.dot(
        jnp.concatenate([hidden, motion], 1), w_gates_ref[...], preferred_element_type=jnp.float32
    )
    hidden_wide = hidden.astype(jnp.float32)
    gate_tanh = jnp.tanh(0.5 * gate_pre)
    reset_state = (0.5 * hidden_wide * (1.0 + gate_tanh[:, chans:])).astype(jnp.bfloat16)
    blank = jnp.zeros((block, chans), jnp.bfloat16)
    above = jnp.concatenate([blank, reset_state[: (ROWS - 1) * block]], 0)
    below = jnp.concatenate([reset_state[block:], blank], 0)
    taps = jnp.concatenate([above, reset_state, below, motion], 1)
    conv = jnp.dot(taps, w_conv_ref[...], preferred_element_type=jnp.float32)
    total = ROWS * block
    col = lax.broadcasted_iota(jnp.int32, (total, chans), 0) % WIDTH
    conv_sum = (
        conv[:, chans : 2 * chans]
        + jnp.where(col > 0, pltpu.roll(conv[:, :chans], 1, 0), 0.0)
        + jnp.where(col < WIDTH - 1, pltpu.roll(conv[:, 2 * chans :], total - 1, 0), 0.0)
    )
    candidate = jnp.tanh(conv_sum)
    update = 0.5 + 0.5 * gate_tanh[:, :chans]
    new_hidden = (hidden_wide + update * (candidate - hidden_wide)).astype(jnp.bfloat16)
    heads = lax.dot_general(
        w_heads_ref[...], new_hidden, (((1,), (1,)), ((), ())),
        preferred_element_type=jnp.float32,
    )
    revision = heads[0:1]
    confidence = 0.5 + 0.5 * jnp.tanh(0.5 * heads[1:2])
    pushed = jnp.concatenate([confidence * revision, confidence], 0)
    for g in range(edges):
        for y in range(ROWS):
            new_ref[0, g, y * WIDTH : (y + 1) * WIDTH] = new_hidden[
                y * block + g * WIDTH : y * block + (g + 1) * WIDTH
            ]
        mine = jnp.concatenate(
            [pushed[:, y * block + g * WIDTH : y * block + (g + 1) * WIDTH] for y in range(ROWS)],
            1,
        )
        sums_ref[slots[g]] += mine


def on_device(
    features, context, states, neighbours, depths, damping,
    w_corr, w_gates, w_cand, w_motion, w_heads,
):
    frames_here, pixels, chans = features.shape
    neigh = states.shape[1]
    own_block = lax.axis_index("edge")
    mirrored = features.reshape(frames_here, ROWS, WIDTH, chans)[:, :, ::-1].reshape(features.shape)
    below_side = mirrored
    above_side = mirrored
    covered = 1
    while covered < REACH + 1:
        sending = min(covered, REACH + 1 - covered)
        tail_part = below_side[below_side.shape[0] - sending * frames_here :]
        head_part = above_side[: sending * frames_here]
        below_side = jnp.concatenate([passed_along(tail_part, "edge", covered), below_side], 0)
        above_side = jnp.concatenate([above_side, passed_along(head_part, "edge", -covered)], 0)
        covered = covered + sending
    window = jnp.concatenate([below_side, above_side[frames_here:]], 0)
    slots = window.shape[0]
    local_index = neighbours - (own_block - REACH) * frames_here

    picks = jnp.asarray(corr_picks(), jnp.bfloat16)
    w_corr_wide = jnp.dot(picks, w_corr).reshape(ROWS, PIX, chans)
    taps = w_cand.reshape(3, 3, chans, chans)
    by_col = [
        jnp.concatenate(
            [taps[0, c], taps[1, c], taps[2, c], w_motion if c == 1 else jnp.zeros_like(w_motion)],
            0,
        )
        for c in range(3)
    ]
    w_conv = jnp.concatenate(by_col, 1)
    edges = math.gcd(EDGES_PER_STEP, neigh)
    whole = pl.BlockSpec(memory_space=pltpu.VMEM)
    new_states, sums = pl.pallas_call(
        functools.partial(edge_kernel, edges),
        out_shape=(
            jax.ShapeDtypeStruct(states.shape, states.dtype),
            jax.ShapeDtypeStruct((slots, 2, pixels), jnp.float32),
        ),
        grid_spec=pltpu.PrefetchScalarGridSpec(
            num_scalar_prefetch=1,
            grid=(frames_here, neigh // edges),
            in_specs=[
                pl.BlockSpec((1, pixels, chans), lambda f, k, *_: (f, 0, 0)),
                pl.BlockSpec((1, pixels, chans), lambda f, k, *_: (f, 0, 0)),
                pl.BlockSpec((1, edges, pixels, chans), lambda f, k, *_: (f, k, 0, 0)),
                whole, whole, whole, whole, whole,
            ],
            out_specs=[
                pl.BlockSpec((1, edges, pixels, chans), lambda f, k, *_: (f, k, 0, 0)),
                whole,
            ],
        ),
        compiler_params=pltpu.CompilerParams(vmem_limit_bytes=48 * 1024 * 1024),
        name="edge_update",
    )(local_index, features, context, states, window, w_corr_wide, w_gates, w_conv, w_heads)
    partial_sums = sums.reshape(slots, 2 * pixels)
    sums = partial_sums[REACH * frames_here : (REACH + 1) * frames_here]
    for offset in range(-REACH, REACH + 1):
        if offset != 0:
            block_part = partial_sums[
                (offset + REACH) * frames_here : (offset + REACH + 1) * frames_here
            ]
            sums = sums + passed_along(block_part, "edge", offset)
    new_depths = depths + sums[:, :pixels] / (damping + sums[:, pixels:])
    return (new_states, new_depths)


def solution(mesh):
    split = P(("groups", "edge"))
    return jax.shard_map(
        on_device,
        mesh=mesh,
        in_specs=(split,) * 6 + (P(),) * 5,
        out_specs=(split, split),
        check_vma=False,
    )
```

time: 511 us -> 92.3 us (0.18)
  the two profiles are of different devices: /device:TPU:0 before, /device:TPU:18 now
where the time goes in v1:
time: 92.3 us; the launch traced here: 91.6 us
  starting transfers between devices  50.3 us (54%)
  waiting for transfers between devices  25.7 us (28%)
  Pallas kernels  11.1 us (12%)
  local copies, waits for them, and re-layouts  2.22 us (2%)
  between operations  1.22 us (1%)
    ppermute x18, starting transfers between devices, passed_along(): lax.ppermute(value, axis, [(source, source + steps) for source in range(f...  50.3 us
    ppermute x18, waiting for transfers between devices, passed_along(): lax.ppermute(value, axis, [(source, source + steps) for source in range(f...  25.7 us
    pallas_call x1, Pallas kernels, on_device(): pl.pallas_call(functools.partial(edge_kernel, edges), out_shape=(jax.Shap...  11.1 us
  transfers between devices with their start and end apart: 18, of which 7 were waited for; matrix products, arithmetic and copies ran while one was open for 2% of the time, Pallas kernels for 0%

profile of v1, /device:TPU:18, one launch (start us, length us, event | category | flops | bytes accessed | tf_op | source)
XLA Modules:
  0.0 91.6 jit_solution(13669454950943075968)
XLA Ops:
  0.7 1.0 %rev.3 = bf16[2,4,64,128]{3,2,1,0:T(8,128)(2,1)S(1)} reverse(bf16[2,4,64,128]{3,2,1,0:T(8,128)(2,1)} %bitcast.64), dimensions={2} | reverse | bytes 262144 | tf_op jit(solution)/shard_map/rev | solution.py:133
  1.6 1.9 %collective-permute-start = (bf16[2,256,128]{2,1,0:T(8,128)(2,1)S(1)}, bf16[2,256,128]{2,1,0:T(8,128)(2,1)S(1)}, u32[]{:S(2)}, u32[]{:S(2)}) collective-permute-start(bf16[2,256,128]{2,1,0:T(8,128)(2,1)S(1)} %bitcast.65), channel_id=1, source_target_pairs={{0,1},{1,2},{2,3},{3,4},{4,5},{5,6},{6,7},{7,8},{8,9},{9,10},{10,1... | collective-permute-start | bytes 393224 | tf_op jit(solution)/shard_map/ppermute | solution.py:24
  3.6 3.6 %collective-permute-start.3 = (bf16[2,256,128]{2,1,0:T(8,128)(2,1)S(1)}, bf16[2,256,128]{2,1,0:T(8,128)(2,1)S(1)}, u32[]{:S(2)}, u32[]{:S(2)}) collective-permute-start(bf16[2,256,128]{2,1,0:T(8,128)(2,1)S(1)} %bitcast.66), channel_id=1, source_target_pairs={{1,0},{2,1},{3,2},{4,3},{5,4},{6,5},{7,6},{8,7},{9,8},{10,9},{11,1... | collective-permute-start | bytes 393224 | tf_op jit(solution)/shard_map/ppermute | solution.py:24
  7.2 0.7 collective-permute-done
  7.9 1.8 %collective-permute-done.3 = bf16[2,256,128]{2,1,0:T(8,128)(2,1)S(1)} collective-permute-done((bf16[2,256,128]{2,1,0:T(8,128)(2,1)S(1)}, bf16[2,256,128]{2,1,0:T(8,128)(2,1)S(1)}, u32[]{:S(2)}, u32[]{:S(2)}) %collective-permute-start.3) | collective-permute-done | bytes 131104 | tf_op jit(solution)/shard_map/ppermute | solution.py:24
  9.8 4.5 %collective-permute-start.1 = (bf16[4,256,128]{2,1,0:T(8,128)(2,1)S(1)}, bf16[4,256,128]{2,1,0:T(8,128)(2,1)S(1)}, u32[]{:S(2)}, u32[]{:S(2)}) collective-permute-start(bf16[4,256,128]{2,1,0:T(8,128)(2,1)S(1)} %get-tuple-element.18), channel_id=1, source_target_pairs={{0,2},{1,3},{2,4},{3,5},{4,6},{5,7},{6,8},{7,9},{8,10},{9,11},{10,... | collective-permute-start | bytes 786440 | tf_op jit(solution)/shard_map/ppermute | solution.py:24
  14.3 1.9 %collective-permute-start.4 = (bf16[4,256,128]{2,1,0:T(8,128)(2,1)S(1)}, bf16[4,256,128]{2,1,0:T(8,128)(2,1)S(1)}, u32[]{:S(2)}, u32[]{:S(2)}) collective-permute-start(bf16[4,256,128]{2,1,0:T(8,128)(2,1)S(1)} %get-tuple-element.17), channel_id=1, source_target_pairs={{2,0},{3,1},{4,2},{5,3},{6,4},{7,5},{8,6},{9,7},{10,8},{11,9},{12,... | collective-permute-start | bytes 786440 | tf_op jit(solution)/shard_map/ppermute | solution.py:24
  16.2 0.9 slice_bitcast_fusion.8
  17.1 3.7 %collective-permute-done.1 = bf16[4,256,128]{2,1,0:T(8,128)(2,1)S(1)} collective-permute-done((bf16[4,256,128]{2,1,0:T(8,128)(2,1)S(1)}, bf16[4,256,128]{2,1,0:T(8,128)(2,1)S(1)}, u32[]{:S(2)}, u32[]{:S(2)}) %collective-permute-start.1) | collective-permute-done | bytes 262176 | tf_op jit(solution)/shard_map/ppermute | solution.py:24
  20.8 5.4 %collective-permute-done.4 = bf16[4,256,128]{2,1,0:T(8,128)(2,1)S(1)} collective-permute-done((bf16[4,256,128]{2,1,0:T(8,128)(2,1)S(1)}, bf16[4,256,128]{2,1,0:T(8,128)(2,1)S(1)}, u32[]{:S(2)}, u32[]{:S(2)}) %collective-permute-start.4) | collective-permute-done | bytes 262176 | tf_op jit(solution)/shard_map/ppermute | solution.py:24
  26.2 0.1 pad_maximum_fusion
  26.3 3.6 %collective-permute-start.2 = (bf16[6,256,128]{2,1,0:T(8,128)(2,1)S(1)}, bf16[6,256,128]{2,1,0:T(8,128)(2,1)S(1)}, u32[]{:S(2)}, u32[]{:S(2)}) collective-permute-start(bf16[6,256,128]{2,1,0:T(8,128)(2,1)S(1)} %get-tuple-element.16), channel_id=1, source_target_pairs={{0,4},{1,5},{2,6},{3,7},{4,8},{5,9},{6,10},{7,11},{8,12},{9,13},{1... | collective-permute-start | bytes 1179656 | tf_op jit(solution)/shard_map/ppermute | solution.py:24
  29.9 0.1 maximum_maximum_fusion.w_conv_ref
  30.0 0.2 fusion.2
  30.3 2.4 %collective-permute-start.5 = (bf16[6,256,128]{2,1,0:T(8,128)(2,1)S(1)}, bf16[6,256,128]{2,1,0:T(8,128)(2,1)S(1)}, u32[]{:S(2)}, u32[]{:S(2)}) collective-permute-start(bf16[6,256,128]{2,1,0:T(8,128)(2,1)S(1)} %get-tuple-element.15), channel_id=1, source_target_pairs={{4,0},{5,1},{6,2},{7,3},{8,4},{9,5},{10,6},{11,7},{12,8},{13,9},{1... | collective-permute-start | bytes 1179656 | tf_op jit(solution)/shard_map/ppermute | solution.py:24
  32.7 6.8 %collective-permute-done.2 = bf16[6,256,128]{2,1,0:T(8,128)(2,1)S(1)} collective-permute-done((bf16[6,256,128]{2,1,0:T(8,128)(2,1)S(1)}, bf16[6,256,128]{2,1,0:T(8,128)(2,1)S(1)}, u32[]{:S(2)}, u32[]{:S(2)}) %collective-permute-start.2) | collective-permute-done | bytes 393248 | tf_op jit(solution)/shard_map/ppermute | solution.py:24
  39.7 3.4 %collective-permute-done.5 = bf16[6,256,128]{2,1,0:T(8,128)(2,1)S(1)} collective-permute-done((bf16[6,256,128]{2,1,0:T(8,128)(2,1)S(1)}, bf16[6,256,128]{2,1,0:T(8,128)(2,1)S(1)}, u32[]{:S(2)}, u32[]{:S(2)}) %collective-permute-start.5) | collective-permute-done | bytes 393248 | tf_op jit(solution)/shard_map/ppermute | solution.py:24
  43.2 11.1 %edge_update.1 = (bf16[2,12,256,128]{3,2,1,0:T(8,128)(2,1)}, f32[26,2,256]{2,1,0:T(2,128)S(1)}) custom-call(s32[2,12]{1,0:T(2,128)S(1)} %broadcast_subtract_fusion.index_ref, bf16[2,256,128]{2,1,0:T(8,128)(2,1)S(1)} %copy-done.2, bf16[2,256,128]{2,1,0:T(8,128)(2,1)S(1)} %copy-done.3, bf16[2,12,256,128]{3,2,1,0:T(8,128)(2,1)S(1)} %copy-done.1, ...), custom_call_target="tpu_custom_call" | custom-call | tf_op jit(solution)/shard_map/edge_update/pallas_call | solution.py:161
  54.4 4.4 %collective-permute-start.10 = (f32[2,512]{1,0:T(2,128)S(1)}, f32[2,512]{1,0:T(2,128)S(1)}, u32[]{:S(2)}, u32[]{:S(2)}) collective-permute-start(f32[2,512]{1,0:T(2,128)S(1)} %bitcast.83), channel_id=1, source_target_pairs={{2,0},{3,1},{4,2},{5,3},{6,4},{7,5},{8,6},{9,7},{10,8},{11,9},{12,... | collective-permute-start | bytes 12296 | tf_op jit(solution)/shard_map/ppermute | solution.py:24
  58.8 1.9 %collective-permute-start.11 = (f32[2,512]{1,0:T(2,128)S(1)}, f32[2,512]{1,0:T(2,128)S(1)}, u32[]{:S(2)}, u32[]{:S(2)}) collective-permute-start(f32[2,512]{1,0:T(2,128)S(1)} %bitcast.82), channel_id=1, source_target_pairs={{1,0},{2,1},{3,2},{4,3},{5,4},{6,5},{7,6},{8,7},{9,8},{10,9},{11,1... | collective-permute-start | bytes 12296 | tf_op jit(solution)/shard_map/ppermute | solution.py:24
  60.7 2.4 %collective-permute-start.12 = (f32[2,512]{1,0:T(2,128)S(1)}, f32[2,512]{1,0:T(2,128)S(1)}, u32[]{:S(2)}, u32[]{:S(2)}) collective-permute-start(f32[2,512]{1,0:T(2,128)S(1)} %bitcast.81), channel_id=1, source_target_pairs={{0,1},{1,2},{2,3},{3,4},{4,5},{5,6},{6,7},{7,8},{8,9},{9,10},{10,1... | collective-permute-start | bytes 12296 | tf_op jit(solution)/shard_map/ppermute | solution.py:24
  63.1 2.5 %collective-permute-start.13 = (f32[2,512]{1,0:T(2,128)S(1)}, f32[2,512]{1,0:T(2,128)S(1)}, u32[]{:S(2)}, u32[]{:S(2)}) collective-permute-start(f32[2,512]{1,0:T(2,128)S(1)} %bitcast.80), channel_id=1, source_target_pairs={{0,2},{1,3},{2,4},{3,5},{4,6},{5,7},{6,8},{7,9},{8,10},{9,11},{10,... | collective-permute-start | bytes 12296 | tf_op jit(solution)/shard_map/ppermute | solution.py:24
  65.7 1.9 %collective-permute-start.14 = (f32[2,512]{1,0:T(2,128)S(1)}, f32[2,512]{1,0:T(2,128)S(1)}, u32[]{:S(2)}, u32[]{:S(2)}) collective-permute-start(f32[2,512]{1,0:T(2,128)S(1)} %bitcast.79), channel_id=1, source_target_pairs={{0,3},{1,4},{2,5},{3,6},{4,7},{5,8},{6,9},{7,10},{8,11},{9,12},{10... | collective-permute-start | bytes 12296 | tf_op jit(solution)/shard_map/ppermute | solution.py:24
  67.7 1.9 %collective-permute-start.15 = (f32[2,512]{1,0:T(2,128)S(1)}, f32[2,512]{1,0:T(2,128)S(1)}, u32[]{:S(2)}, u32[]{:S(2)}) collective-permute-start(f32[2,512]{1,0:T(2,128)S(1)} %bitcast.77), channel_id=1, source_target_pairs={{0,4},{1,5},{2,6},{3,7},{4,8},{5,9},{6,10},{7,11},{8,12},{9,13},{1... | collective-permute-start | bytes 12296 | tf_op jit(solution)/shard_map/ppermute | solution.py:24
  69.6 1.9 %collective-permute-start.16 = (f32[2,512]{1,0:T(2,128)S(1)}, f32[2,512]{1,0:T(2,128)S(1)}, u32[]{:S(2)}, u32[]{:S(2)}) collective-permute-start(f32[2,512]{1,0:T(2,128)S(1)} %bitcast.73), channel_id=1, source_target_pairs={{0,5},{1,6},{2,7},{3,8},{4,9},{5,10},{6,11},{7,12},{8,13},{9,14},{... | collective-permute-start | bytes 12296 | tf_op jit(solution)/shard_map/ppermute | solution.py:24
  71.6 1.3 %collective-permute-start.17 = (f32[2,512]{1,0:T(2,128)S(1)}, f32[2,512]{1,0:T(2,128)S(1)}, u32[]{:S(2)}, u32[]{:S(2)}) collective-permute-start(f32[2,512]{1,0:T(2,128)S(1)} %bitcast.78), channel_id=1, source_target_pairs={{0,6},{1,7},{2,8},{3,9},{4,10},{5,11},{6,12},{7,13},{8,14},{9,15},... | collective-permute-start | bytes 12296 | tf_op jit(solution)/shard_map/ppermute | solution.py:24
  72.9 5.4 %collective-permute-start.6 = (f32[2,512]{1,0:T(2,128)S(1)}, f32[2,512]{1,0:T(2,128)S(1)}, u32[]{:S(2)}, u32[]{:S(2)}) collective-permute-start(f32[2,512]{1,0:T(2,128)S(1)} %bitcast.76), channel_id=1, source_target_pairs={{6,0},{7,1},{8,2},{9,3},{10,4},{11,5},{12,6},{13,7},{14,8},{15,9},... | collective-permute-start | bytes 12296 | tf_op jit(solution)/shard_map/ppermute | solution.py:24
  78.4 1.9 %collective-permute-start.7 = (f32[2,512]{1,0:T(2,128)S(1)}, f32[2,512]{1,0:T(2,128)S(1)}, u32[]{:S(2)}, u32[]{:S(2)}) collective-permute-start(f32[2,512]{1,0:T(2,128)S(1)} %bitcast.75), channel_id=1, source_target_pairs={{5,0},{6,1},{7,2},{8,3},{9,4},{10,5},{11,6},{12,7},{13,8},{14,9},{... | collective-permute-start | bytes 12296 | tf_op jit(solution)/shard_map/ppermute | solution.py:24
  80.3 4.8 %collective-permute-start.8 = (f32[2,512]{1,0:T(2,128)S(1)}, f32[2,512]{1,0:T(2,128)S(1)}, u32[]{:S(2)}, u32[]{:S(2)}) collective-permute-start(f32[2,512]{1,0:T(2,128)S(1)} %bitcast.74), channel_id=1, source_target_pairs={{4,0},{5,1},{6,2},{7,3},{8,4},{9,5},{10,6},{11,7},{12,8},{13,9},{1... | collective-permute-start | bytes 12296 | tf_op jit(solution)/shard_map/ppermute | solution.py:24
  85.1 1.9 %collective-permute-start.9 = (f32[2,512]{1,0:T(2,128)S(1)}, f32[2,512]{1,0:T(2,128)S(1)}, u32[]{:S(2)}, u32[]{:S(2)}) collective-permute-start(f32[2,512]{1,0:T(2,128)S(1)} %bitcast.72), channel_id=1, source_target_pairs={{3,0},{4,1},{5,2},{6,3},{7,4},{8,5},{9,6},{10,7},{11,8},{12,9},{13... | collective-permute-start | bytes 12296 | tf_op jit(solution)/shard_map/ppermute | solution.py:24
  87.1 3.8 %collective-permute-done.9 = f32[2,512]{1,0:T(2,128)S(1)} collective-permute-done((f32[2,512]{1,0:T(2,128)S(1)}, f32[2,512]{1,0:T(2,128)S(1)}, u32[]{:S(2)}, u32[]{:S(2)}) %collective-permute-start.9) | collective-permute-done | bytes 4128 | tf_op jit(solution)/shard_map/ppermute | solution.py:24
  91.0 0.6 fusion.1
  (58 shorter events, 0.4 us)
Async XLA Ops:
  0.6 29.4 %copy-start = (bf16[49,128]{1,0:T(8,128)(2,1)S(1)}, bf16[49,128]{1,0:T(8,128)(2,1)}, u32[]{:S(2)}) copy-start(bf16[49,128]{1,0:T(8,128)(2,1)} %param.18) | copy-start | bytes 37636
  0.6 29.2 %copy-start.10 = (s32[2,12]{1,0:T(2,128)S(1)}, s32[2,12]{1,0:T(2,128)}, u32[]{:S(2)}) copy-start(s32[2,12]{1,0:T(2,128)} %param.15) | copy-start | bytes 292
  1.6 28.3 %copy-start.7 = (bf16[128,128]{1,0:T(8,128)(2,1)S(1)}, bf16[128,128]{1,0:T(8,128)(2,1)}, u32[]{:S(2)}) copy-start(bf16[128,128]{1,0:T(8,128)(2,1)} %param.21) | copy-start | bytes 98308
  1.6 6.3 %collective-permute-start = (bf16[2,256,128]{2,1,0:T(8,128)(2,1)S(1)}, bf16[2,256,128]{2,1,0:T(8,128)(2,1)S(1)}, u32[]{:S(2)}, u32[]{:S(2)}) collective-permute-start(bf16[2,256,128]{2,1,0:T(8,128)(2,1)S(1)} %bitcast.65), channel_id=1, source_target_pairs={{0,1},{1,2},{2,3},{3,4},{4,5},{5,6},{6,7},{7,8},{8,9},{9,10},{10,1... | collective-permute-start | bytes 393224 | tf_op jit(solution)/shard_map/ppermute | solution.py:24
  3.6 6.1 %collective-permute-start.3 = (bf16[2,256,128]{2,1,0:T(8,128)(2,1)S(1)}, bf16[2,256,128]{2,1,0:T(8,128)(2,1)S(1)}, u32[]{:S(2)}, u32[]{:S(2)}) collective-permute-start(bf16[2,256,128]{2,1,0:T(8,128)(2,1)S(1)} %bitcast.66), channel_id=1, source_target_pairs={{1,0},{2,1},{3,2},{4,3},{5,4},{6,5},{7,6},{8,7},{9,8},{10,9},{11,1... | collective-permute-start | bytes 393224 | tf_op jit(solution)/shard_map/ppermute | solution.py:24
  9.8 20.3 %copy-start.6 = (bf16[1024,49]{1,0:T(8,128)(2,1)S(1)}, bf16[1024,49]{1,0:T(8,128)(2,1)}, u32[]{:S(2)}) copy-start(bf16[1024,49]{1,0:T(8,128)(2,1)} %constant.13.clone) | copy-start | bytes 301060
  9.8 11.1 %collective-permute-start.1 = (bf16[4,256,128]{2,1,0:T(8,128)(2,1)S(1)}, bf16[4,256,128]{2,1,0:T(8,128)(2,1)S(1)}, u32[]{:S(2)}, u32[]{:S(2)}) collective-permute-start(bf16[4,256,128]{2,1,0:T(8,128)(2,1)S(1)} %get-tuple-element.18), channel_id=1, source_target_pairs={{0,2},{1,3},{2,4},{3,5},{4,6},{5,7},{6,8},{7,9},{8,10},{9,11},{10,... | collective-permute-start | bytes 786440 | tf_op jit(solution)/shard_map/ppermute | solution.py:24
  14.3 11.9 %collective-permute-start.4 = (bf16[4,256,128]{2,1,0:T(8,128)(2,1)S(1)}, bf16[4,256,128]{2,1,0:T(8,128)(2,1)S(1)}, u32[]{:S(2)}, u32[]{:S(2)}) collective-permute-start(bf16[4,256,128]{2,1,0:T(8,128)(2,1)S(1)} %get-tuple-element.17), channel_id=1, source_target_pairs={{2,0},{3,1},{4,2},{5,3},{6,4},{7,5},{8,6},{9,7},{10,8},{11,9},{12,... | collective-permute-start | bytes 786440 | tf_op jit(solution)/shard_map/ppermute | solution.py:24
  26.3 13.2 %collective-permute-start.2 = (bf16[6,256,128]{2,1,0:T(8,128)(2,1)S(1)}, bf16[6,256,128]{2,1,0:T(8,128)(2,1)S(1)}, u32[]{:S(2)}, u32[]{:S(2)}) collective-permute-start(bf16[6,256,128]{2,1,0:T(8,128)(2,1)S(1)} %get-tuple-element.16), channel_id=1, source_target_pairs={{0,4},{1,5},{2,6},{3,7},{4,8},{5,9},{6,10},{7,11},{8,12},{9,13},{1... | collective-permute-start | bytes 1179656 | tf_op jit(solution)/shard_map/ppermute | solution.py:24
  30.2 12.9 %copy-start.1 = (bf16[2,12,256,128]{3,2,1,0:T(8,128)(2,1)S(1)}, bf16[2,12,256,128]{3,2,1,0:T(8,128)(2,1)}, u32[]{:S(2)}) copy-start(bf16[2,12,256,128]{3,2,1,0:T(8,128)(2,1)} %state_ref.1) | copy-start | bytes 4718596
  30.2 12.9 %copy-start.2 = (bf16[2,256,128]{2,1,0:T(8,128)(2,1)S(1)}, bf16[2,256,128]{2,1,0:T(8,128)(2,1)}, u32[]{:S(2)}) copy-start(bf16[2,256,128]{2,1,0:T(8,128)(2,1)} %feat_ref.1) | copy-start | bytes 393220
  30.3 12.9 %copy-start.3 = (bf16[2,256,128]{2,1,0:T(8,128)(2,1)S(1)}, bf16[2,256,128]{2,1,0:T(8,128)(2,1)}, u32[]{:S(2)}) copy-start(bf16[2,256,128]{2,1,0:T(8,128)(2,1)} %ctx_ref.1) | copy-start | bytes 393220
  30.3 12.9 %copy-start.4 = (bf16[256,256]{1,0:T(8,128)(2,1)S(1)}, bf16[256,256]{1,0:T(8,128)(2,1)}, u32[]{:S(2)}) copy-start(bf16[256,256]{1,0:T(8,128)(2,1)} %w_gates_ref.1) | copy-start | bytes 393220
  30.3 12.9 %copy-start.5 = (bf16[2,128]{1,0:T(2,128)(2,1)S(1)}, bf16[2,128]{1,0:T(2,128)(2,1)}, u32[]{:S(2)}) copy-start(bf16[2,128]{1,0:T(2,128)(2,1)} %w_heads_ref.1) | copy-start | bytes 1540
  30.3 12.8 %collective-permute-start.5 = (bf16[6,256,128]{2,1,0:T(8,128)(2,1)S(1)}, bf16[6,256,128]{2,1,0:T(8,128)(2,1)S(1)}, u32[]{:S(2)}, u32[]{:S(2)}) collective-permute-start(bf16[6,256,128]{2,1,0:T(8,128)(2,1)S(1)} %get-tuple-element.15), channel_id=1, source_target_pairs={{4,0},{5,1},{6,2},{7,3},{8,4},{9,5},{10,6},{11,7},{12,8},{13,9},{1... | collective-permute-start | bytes 1179656 | tf_op jit(solution)/shard_map/ppermute | solution.py:24
  43.2 47.8 %copy-start.8 = (f32[2,256]{1,0:T(2,128)S(1)}, f32[2,256]{1,0:T(2,128)}, u32[]{:S(2)}) copy-start(f32[2,256]{1,0:T(2,128)} %param.16) | copy-start | bytes 6148
  43.2 47.8 %copy-start.9 = (f32[2,256]{1,0:T(2,128)S(1)}, f32[2,256]{1,0:T(2,128)}, u32[]{:S(2)}) copy-start(f32[2,256]{1,0:T(2,128)} %param.17) | copy-start | bytes 6148
  54.4 13.3 %collective-permute-start.10 = (f32[2,512]{1,0:T(2,128)S(1)}, f32[2,512]{1,0:T(2,128)S(1)}, u32[]{:S(2)}, u32[]{:S(2)}) collective-permute-start(f32[2,512]{1,0:T(2,128)S(1)} %bitcast.83), channel_id=1, source_target_pairs={{2,0},{3,1},{4,2},{5,3},{6,4},{7,5},{8,6},{9,7},{10,8},{11,9},{12,... | collective-permute-start | bytes 12296 | tf_op jit(solution)/shard_map/ppermute | solution.py:24
  58.8 10.8 %collective-permute-start.11 = (f32[2,512]{1,0:T(2,128)S(1)}, f32[2,512]{1,0:T(2,128)S(1)}, u32[]{:S(2)}, u32[]{:S(2)}) collective-permute-start(f32[2,512]{1,0:T(2,128)S(1)} %bitcast.82), channel_id=1, source_target_pairs={{1,0},{2,1},{3,2},{4,3},{5,4},{6,5},{7,6},{8,7},{9,8},{10,9},{11,1... | collective-permute-start | bytes 12296 | tf_op jit(solution)/shard_map/ppermute | solution.py:24
  60.7 10.9 %collective-permute-start.12 = (f32[2,512]{1,0:T(2,128)S(1)}, f32[2,512]{1,0:T(2,128)S(1)}, u32[]{:S(2)}, u32[]{:S(2)}) collective-permute-start(f32[2,512]{1,0:T(2,128)S(1)} %bitcast.81), channel_id=1, source_target_pairs={{0,1},{1,2},{2,3},{3,4},{4,5},{5,6},{6,7},{7,8},{8,9},{9,10},{10,1... | collective-permute-start | bytes 12296 | tf_op jit(solution)/shard_map/ppermute | solution.py:24
  63.1 9.8 %collective-permute-start.13 = (f32[2,512]{1,0:T(2,128)S(1)}, f32[2,512]{1,0:T(2,128)S(1)}, u32[]{:S(2)}, u32[]{:S(2)}) collective-permute-start(f32[2,512]{1,0:T(2,128)S(1)} %bitcast.80), channel_id=1, source_target_pairs={{0,2},{1,3},{2,4},{3,5},{4,6},{5,7},{6,8},{7,9},{8,10},{9,11},{10,... | collective-permute-start | bytes 12296 | tf_op jit(solution)/shard_map/ppermute | solution.py:24
  65.7 12.7 %collective-permute-start.14 = (f32[2,512]{1,0:T(2,128)S(1)}, f32[2,512]{1,0:T(2,128)S(1)}, u32[]{:S(2)}, u32[]{:S(2)}) collective-permute-start(f32[2,512]{1,0:T(2,128)S(1)} %bitcast.79), channel_id=1, source_target_pairs={{0,3},{1,4},{2,5},{3,6},{4,7},{5,8},{6,9},{7,10},{8,11},{9,12},{10... | collective-permute-start | bytes 12296 | tf_op jit(solution)/shard_map/ppermute | solution.py:24
  67.7 12.6 %collective-permute-start.15 = (f32[2,512]{1,0:T(2,128)S(1)}, f32[2,512]{1,0:T(2,128)S(1)}, u32[]{:S(2)}, u32[]{:S(2)}) collective-permute-start(f32[2,512]{1,0:T(2,128)S(1)} %bitcast.77), channel_id=1, source_target_pairs={{0,4},{1,5},{2,6},{3,7},{4,8},{5,9},{6,10},{7,11},{8,12},{9,13},{1... | collective-permute-start | bytes 12296 | tf_op jit(solution)/shard_map/ppermute | solution.py:24
  69.6 15.5 %collective-permute-start.16 = (f32[2,512]{1,0:T(2,128)S(1)}, f32[2,512]{1,0:T(2,128)S(1)}, u32[]{:S(2)}, u32[]{:S(2)}) collective-permute-start(f32[2,512]{1,0:T(2,128)S(1)} %bitcast.73), channel_id=1, source_target_pairs={{0,5},{1,6},{2,7},{3,8},{4,9},{5,10},{6,11},{7,12},{8,13},{9,14},{... | collective-permute-start | bytes 12296 | tf_op jit(solution)/shard_map/ppermute | solution.py:24
  71.6 15.5 %collective-permute-start.17 = (f32[2,512]{1,0:T(2,128)S(1)}, f32[2,512]{1,0:T(2,128)S(1)}, u32[]{:S(2)}, u32[]{:S(2)}) collective-permute-start(f32[2,512]{1,0:T(2,128)S(1)} %bitcast.78), channel_id=1, source_target_pairs={{0,6},{1,7},{2,8},{3,9},{4,10},{5,11},{6,12},{7,13},{8,14},{9,15},... | collective-permute-start | bytes 12296 | tf_op jit(solution)/shard_map/ppermute | solution.py:24
  72.9 14.2 %collective-permute-start.6 = (f32[2,512]{1,0:T(2,128)S(1)}, f32[2,512]{1,0:T(2,128)S(1)}, u32[]{:S(2)}, u32[]{:S(2)}) collective-permute-start(f32[2,512]{1,0:T(2,128)S(1)} %bitcast.76), channel_id=1, source_target_pairs={{6,0},{7,1},{8,2},{9,3},{10,4},{11,5},{12,6},{13,7},{14,8},{15,9},... | collective-permute-start | bytes 12296 | tf_op jit(solution)/shard_map/ppermute | solution.py:24
  78.4 8.7 %collective-permute-start.7 = (f32[2,512]{1,0:T(2,128)S(1)}, f32[2,512]{1,0:T(2,128)S(1)}, u32[]{:S(2)}, u32[]{:S(2)}) collective-permute-start(f32[2,512]{1,0:T(2,128)S(1)} %bitcast.75), channel_id=1, source_target_pairs={{5,0},{6,1},{7,2},{8,3},{9,4},{10,5},{11,6},{12,7},{13,8},{14,9},{... | collective-permute-start | bytes 12296 | tf_op jit(solution)/shard_map/ppermute | solution.py:24
  80.3 6.8 %collective-permute-start.8 = (f32[2,512]{1,0:T(2,128)S(1)}, f32[2,512]{1,0:T(2,128)S(1)}, u32[]{:S(2)}, u32[]{:S(2)}) collective-permute-start(f32[2,512]{1,0:T(2,128)S(1)} %bitcast.74), channel_id=1, source_target_pairs={{4,0},{5,1},{6,2},{7,3},{8,4},{9,5},{10,6},{11,7},{12,8},{13,9},{1... | collective-permute-start | bytes 12296 | tf_op jit(solution)/shard_map/ppermute | solution.py:24
  85.1 5.8 %collective-permute-start.9 = (f32[2,512]{1,0:T(2,128)S(1)}, f32[2,512]{1,0:T(2,128)S(1)}, u32[]{:S(2)}, u32[]{:S(2)}) collective-permute-start(f32[2,512]{1,0:T(2,128)S(1)} %bitcast.72), channel_id=1, source_target_pairs={{3,0},{4,1},{5,2},{6,3},{7,4},{8,5},{9,6},{10,7},{11,8},{12,9},{13... | collective-permute-start | bytes 12296 | tf_op jit(solution)/shard_map/ppermute | solution.py:24

commit v2 on v1

--- a/solution.py
+++ b/solution.py
@@ -18,10 +18,37 @@
 EDGES_PER_STEP = 4
 
 
-def passed_along(value, axis, steps):
-    count = lax.axis_size(axis)
-    first, last = (max(0, -steps), min(count, count - steps))
-    return lax.ppermute(value, axis, [(source, source + steps) for source in range(first, last)])
+def sent(value, pairs):
+    count = lax.axis_size("edge")
+    return lax.ppermute(
+        value, "edge", [(a, b) for a, b in pairs if 0 <= a < count and 0 <= b < count]
+    )
+
+
+def swapped(value, steps, odd):
+    low = [i for i in range(lax.axis_size("edge")) if (i // steps) % 2 == odd]
+    low = [i for i in low if i + steps < lax.axis_size("edge")]
+    return sent(value, [(i, i + steps) for i in low] + [(i + steps, i) for i in low])
+
+
+def gather_window(own):
+    count = lax.axis_size("edge")
+    beside = swapped(own, 2, 0)
+    two = jnp.concatenate([own, beside], 0)
+    far = sent(own, [(i, i + REACH) if i % 4 >= 2 else (i, i - REACH) for i in range(count)])
+    even = swapped(two, 4, 0)
+    odd = swapped(two, 4, 1)
+    mine = [two, even, odd, far]
+    return mine + [swapped(piece, 1, 0) for piece in mine]
+
+
+def window_block(block):
+    own = lax.axis_index("edge")
+    group, own_group = block // 4, own // 4
+    column = ((block // 2) % 2 != (own // 2) % 2).astype(jnp.int32)
+    place = jnp.where(group == own_group, 0, jnp.where(group == own_group ^ 1, 2, 4)) + column
+    place = jnp.where(jnp.abs(group - own_group) == 2, 6, place)
+    return place + 7 * (block % 2 != own % 2).astype(jnp.int32)
 
 
 def corr_picks():
@@ -36,7 +63,7 @@
 
 
 def edge_kernel(
-    edges, index_ref, feat_ref, ctx_ref, state_ref, window_ref, w_corr_ref, w_gates_ref,
+    edges, index_ref, target_ref, feat_ref, ctx_ref, state_ref, window_ref, w_corr_ref, w_gates_ref,
     w_conv_ref, w_heads_ref, new_ref, sums_ref
 ):
     frame = pl.program_id(0)
@@ -120,7 +147,7 @@
             [pushed[:, y * block + g * WIDTH : y * block + (g + 1) * WIDTH] for y in range(ROWS)],
             1,
         )
-        sums_ref[slots[g]] += mine
+        sums_ref[target_ref[frame, part * edges + g]] += mine
 
 
 def on_device(
@@ -129,21 +156,12 @@
 ):
     frames_here, pixels, chans = features.shape
     neigh = states.shape[1]
-    own_block = lax.axis_index("edge")
     mirrored = features.reshape(frames_here, ROWS, WIDTH, chans)[:, :, ::-1].reshape(features.shape)
-    below_side = mirrored
-    above_side = mirrored
-    covered = 1
-    while covered < REACH + 1:
-        sending = min(covered, REACH + 1 - covered)
-        tail_part = below_side[below_side.shape[0] - sending * frames_here :]
-        head_part = above_side[: sending * frames_here]
-        below_side = jnp.concatenate([passed_along(tail_part, "edge", covered), below_side], 0)
-        above_side = jnp.concatenate([above_side, passed_along(head_part, "edge", -covered)], 0)
-        covered = covered + sending
-    window = jnp.concatenate([below_side, above_side[frames_here:]], 0)
-    slots = window.shape[0]
-    local_index = neighbours - (own_block - REACH) * frames_here
+    pieces = gather_window(mirrored)
+    window = jnp.concatenate(pieces, 0)
+    blocks = neighbours // frames_here
+    local_index = window_block(blocks) * frames_here + neighbours % frames_here
+    frames_all = lax.axis_size("edge") * frames_here
 
     picks = jnp.asarray(corr_picks(), jnp.bfloat16)
     w_corr_wide = jnp.dot(picks, w_corr).reshape(ROWS, PIX, chans)
@@ -162,10 +180,10 @@
         functools.partial(edge_kernel, edges),
         out_shape=(
             jax.ShapeDtypeStruct(states.shape, states.dtype),
-            jax.ShapeDtypeStruct((slots, 2, pixels), jnp.float32),
+            jax.ShapeDtypeStruct((frames_all, 2, pixels), jnp.float32),
         ),
         grid_spec=pltpu.PrefetchScalarGridSpec(
-            num_scalar_prefetch=1,
+            num_scalar_prefetch=2,
             grid=(frames_here, neigh // edges),
             in_specs=[
                 pl.BlockSpec((1, pixels, chans), lambda f, k, *_: (f, 0, 0)),
@@ -180,16 +198,11 @@
         ),
         compiler_params=pltpu.CompilerParams(vmem_limit_bytes=48 * 1024 * 1024),
         name="edge_update",
-    )(local_index, features, context, states, window, w_corr_wide, w_gates, w_conv, w_heads)
-    partial_sums = sums.reshape(slots, 2 * pixels)
-    sums = partial_sums[REACH * frames_here : (REACH + 1) * frames_here]
-    for offset in range(-REACH, REACH + 1):
-        if offset != 0:
-            block_part = partial_sums[
-                (offset + REACH) * frames_here : (offset + REACH + 1) * frames_here
-            ]
-            sums = sums + passed_along(block_part, "edge", offset)
-    new_depths = depths + sums[:, :pixels] / (damping + sums[:, pixels:])
+    )(local_index, neighbours, features, context, states, window, w_corr_wide, w_gates, w_conv, w_heads)
+    sums = sums.reshape(-1, frames_here, 2, pixels)
+    arrived = lax.all_to_all(sums, "edge", 0, 0, tiled=True)
+    sums = jnp.sum(arrived, 0)
+    new_depths = depths + sums[:, 0] / (damping + sums[:, 1])
     return (new_states, new_depths)
 
 

time: 92.3 us -> 46.3 us (0.50)
  the two profiles are of different devices: /device:TPU:18 before, /device:TPU:0 now
where the time goes in v2:
time: 46.3 us; the launch traced here: 46 us
  blocking collectives  14.1 us (30%)
  Pallas kernels  11.2 us (24%)
  starting transfers between devices  7.46 us (16%)
  waiting for transfers between devices  7.45 us (16%)
  local copies, waits for them, and re-layouts  2.2 us (5%)
  other arithmetic  1.42 us (3%)
  matrix products  1.15 us (2%)
  between operations  0.98 us (2%)
    all_to_all x1, blocking collectives, on_device(): arrived = lax.all_to_all(sums, 'edge', 0, 0, tiled=True)  14.1 us
    pallas_call x1, Pallas kernels, on_device(): pl.pallas_call(functools.partial(edge_kernel, edges), out_shape=(jax.Shap...  11.2 us
    ppermute x8, starting transfers between devices, sent(): lax.ppermute(value, 'edge', [(a, b) for a, b in pairs if 0 <= a < count a...  7.46 us
    ppermute x8, waiting for transfers between devices, sent(): lax.ppermute(value, 'edge', [(a, b) for a, b in pairs if 0 <= a < count a...  7.45 us
    dot_general x1, matrix products, on_device(): w_corr_wide = jnp.dot(picks, w_corr).reshape(ROWS, PIX, chans)  1.15 us
    rev x1, local copies, waits for them, and re-layouts, on_device(): features.reshape(frames_here, ROWS, WIDTH, chans)[:, :, ::-1]  0.96 us
  transfers between devices with their start and end apart: 8, of which 3 were waited for; matrix products, arithmetic and copies ran while one was open for 7% of the time, Pallas kernels for 0%

profile of v2, /device:TPU:0, one launch (start us, length us, event | category | flops | bytes accessed | tf_op | source)
XLA Modules:
  0.0 46.0 jit_solution(2060812650398512937)
XLA Ops:
  0.6 0.0 copy-start
  0.7 1.0 %rev.3 = bf16[2,4,64,128]{3,2,1,0:T(8,128)(2,1)S(1)} reverse(bf16[2,4,64,128]{3,2,1,0:T(8,128)(2,1)} %bitcast.36), dimensions={2} | reverse | bytes 262144 | tf_op jit(solution)/shard_map/rev | solution.py:159
  1.6 3.0 %collective-permute-start = (bf16[2,256,128]{2,1,0:T(8,128)(2,1)S(1)}, bf16[2,256,128]{2,1,0:T(8,128)(2,1)S(1)}, u32[]{:S(2)}, u32[]{:S(2)}) collective-permute-start(bf16[2,256,128]{2,1,0:T(8,128)(2,1)S(1)} %bitcast.38), channel_id=1, source_target_pairs={{0,2},{1,3},{4,6},{5,7},{8,10},{9,11},{12,14},{13,15},{2,0},{3,1},... | collective-permute-start | bytes 393224 | tf_op jit(solution)/shard_map/ppermute | solution.py:23
  4.6 0.7 %collective-permute-start.3 = (bf16[2,256,128]{2,1,0:T(8,128)(2,1)S(1)}, bf16[2,256,128]{2,1,0:T(8,128)(2,1)S(1)}, u32[]{:S(2)}, u32[]{:S(2)}) collective-permute-start(bf16[2,256,128]{2,1,0:T(8,128)(2,1)S(1)} %bitcast.39), channel_id=1, source_target_pairs={{2,8},{3,9},{6,12},{7,13},{8,2},{9,3},{12,6},{13,7},{18,24},{19,25... | collective-permute-start | bytes 393224 | tf_op jit(solution)/shard_map/ppermute | solution.py:23
  5.3 0.9 %slice_bitcast_fusion.8 = (bf16[128,128]{1,0:T(8,128)(2,1)S(1)}, bf16[128,128]{1,0:T(8,128)(2,1)S(1)}, bf16[128,128]{1,0:T(8,128)(2,1)S(1)}, bf16[128,128]{1,0:T...) fusion(bf16[3,3,128,128]{3,2,1,0:T(8,128)(2,1)} %bitcast.42), kind=kLoop, calls=%fused_computation.10 | loop fusion | bytes 589824 | tf_op jit(solution)/shard_map/squeeze | solution.py:171
  6.3 1.1 %fusion.8 = bf16[1024,128]{1,0:T(8,128)(2,1)S(1)} fusion(bf16[1024,49]{1,0:T(8,128)(2,1)} %constant.98.clone, bf16[49,128]{1,0:T(8,128)(2,1)S(1)} %copy-done), kind=kOutput, calls=%fused_computation.51 | convolution fusion | flops 12845056 | bytes 375040 | tf_op jit(solution)/shard_map/dot_general | solution.py:167
  7.4 0.7 %fusion.4.index_ref = s32[2,12]{1,0:T(2,128)S(1)} fusion(s32[2,12]{1,0:T(2,128)} %target_ref.1, s32[]{:T(128)S(6)} %select_n.66, s32[]{:T(128)S(6)} %select_n.63, s32[]{:T(128)S(6)} %xor.3, s32[]{:T(128)S(6)} %select_n.57), kind=kLoop, calls=%fused_computation.47 | loop fusion | flops 1800 | bytes 208 | tf_op jit(solution)/shard_map/add | solution.py:163
  8.1 0.0 collective-permute-done
  8.2 1.9 %collective-permute-start.1 = (bf16[4,256,128]{2,1,0:T(8,128)(2,1)S(1)}, bf16[4,256,128]{2,1,0:T(8,128)(2,1)S(1)}, u32[]{:S(2)}, u32[]{:S(2)}) collective-permute-start(bf16[4,256,128]{2,1,0:T(8,128)(2,1)S(1)} %pad_maximum_fusion), channel_id=1, source_target_pairs={{0,4},{1,5},{2,6},{3,7},{8,12},{9,13},{10,14},{11,15},{4,0},{5,1},... | collective-permute-start | bytes 786440 | tf_op jit(solution)/shard_map/ppermute | solution.py:23
  10.1 0.1 maximum_maximum_fusion.w_conv_ref
  10.1 0.0 copy-start.1
  10.1 0.0 copy-start.2
  10.1 0.0 copy-start.3
  10.1 0.0 copy-start.4
  10.2 0.0 copy-start.5
  10.2 0.0 copy-start.6
  10.2 0.8 %collective-permute-start.2 = (bf16[4,256,128]{2,1,0:T(8,128)(2,1)S(1)}, bf16[4,256,128]{2,1,0:T(8,128)(2,1)S(1)}, u32[]{:S(2)}, u32[]{:S(2)}) collective-permute-start(bf16[4,256,128]{2,1,0:T(8,128)(2,1)S(1)} %pad_maximum_fusion), channel_id=1, source_target_pairs={{4,8},{5,9},{6,10},{7,11},{8,4},{9,5},{10,6},{11,7},{20,24},{21,25... | collective-permute-start | bytes 786440 | tf_op jit(solution)/shard_map/ppermute | solution.py:23
  11.0 0.1 collective-permute-start.4
  11.1 0.0 collective-permute-done.3
  11.1 0.5 %collective-permute-start.7 = (bf16[2,256,128]{2,1,0:T(8,128)(2,1)S(1)}, bf16[2,256,128]{2,1,0:T(8,128)(2,1)S(1)}, u32[]{:S(2)}, u32[]{:S(2)}) collective-permute-start(bf16[2,256,128]{2,1,0:T(8,128)(2,1)S(1)} %collective-permute-done.3), channel_id=1, source_target_pairs={{0,1},{2,3},{4,5},{6,7},{8,9},{10,11},{12,13},{14,15},{1,0},{3,2},... | collective-permute-start | bytes 393224 | tf_op jit(solution)/shard_map/ppermute | solution.py:23
  11.6 6.3 %collective-permute-done.1 = bf16[4,256,128]{2,1,0:T(8,128)(2,1)S(1)} collective-permute-done((bf16[4,256,128]{2,1,0:T(8,128)(2,1)S(1)}, bf16[4,256,128]{2,1,0:T(8,128)(2,1)S(1)}, u32[]{:S(2)}, u32[]{:S(2)}) %collective-permute-start.1) | collective-permute-done | bytes 262176 | tf_op jit(solution)/shard_map/ppermute | solution.py:23
  17.9 0.0 collective-permute-start.5
  18.0 0.0 collective-permute-done.2
  18.0 0.6 %collective-permute-start.6 = (bf16[4,256,128]{2,1,0:T(8,128)(2,1)S(1)}, bf16[4,256,128]{2,1,0:T(8,128)(2,1)S(1)}, u32[]{:S(2)}, u32[]{:S(2)}) collective-permute-start(bf16[4,256,128]{2,1,0:T(8,128)(2,1)S(1)} %collective-permute-done.2), channel_id=1, source_target_pairs={{0,1},{2,3},{4,5},{6,7},{8,9},{10,11},{12,13},{14,15},{1,0},{3,2},... | collective-permute-start | bytes 786440 | tf_op jit(solution)/shard_map/ppermute | solution.py:23
  18.6 0.0 collective-permute-done.4
  18.7 0.8 %collective-permute-done.5 = bf16[4,256,128]{2,1,0:T(8,128)(2,1)S(1)} collective-permute-done((bf16[4,256,128]{2,1,0:T(8,128)(2,1)S(1)}, bf16[4,256,128]{2,1,0:T(8,128)(2,1)S(1)}, u32[]{:S(2)}, u32[]{:S(2)}) %collective-permute-start.5) | collective-permute-done | bytes 262176 | tf_op jit(solution)/shard_map/ppermute | solution.py:23
  19.5 0.3 collective-permute-done.6
  20.0 0.0 copy-start.8
  20.0 0.0 copy-start.9
  20.0 11.2 %edge_update.1 = (bf16[2,12,256,128]{3,2,1,0:T(8,128)(2,1)}, f32[32,2,256]{2,1,0:T(2,128)S(1)}) custom-call(s32[2,12]{1,0:T(2,128)S(1)} %fusion.4.index_ref, s32[2,12]{1,0:T(2,128)S(1)} %copy-done.5, bf16[2,256,128]{2,1,0:T(8,128)(2,1)S(1)} %copy-done.2, bf16[2,256,128]{2,1,0:T(8,128)(2,1)S(1)} %copy-done.3, bf16[2,12,256,128]{3,2,1,0:T(8,128)(2,1)S(1)} %copy-done.1, ...), custom_call_target="tpu_custom_call" | custom-call | tf_op jit(solution)/shard_map/edge_update/pallas_call | solution.py:179
  31.2 14.1 %all_to_all.5 = f32[16,2,2,256]{3,2,1,0:T(2,128)S(1)} all-to-all(f32[16,2,2,256]{3,2,1,0:T(2,128)S(1)} %bitcast.37), channel_id=1, replica_groups=mesh['groups'=2,'edge'=16] {'edge'}, dimensions={0} | all-to-all | bytes 131072 | tf_op jit(solution)/shard_map/all_to_all | solution.py:203
  45.4 0.6 %fusion.1 = f32[2,256]{1,0:T(2,128)} fusion(f32[2,256]{1,0:T(2,128)S(1)} %copy-done.8, f32[2,1,256]{2,1,0:T(1,128)S(1)} %get-tuple-element.16, f32[2,256]{1,0:T(2,128)S(1)} %copy-done.9, f32[2,1,256]{2,1,0:T(1,128)S(1)} %get-tuple-element.15), kind=kLoop, calls=%fused_computation.24 | loop fusion | flops 1536 | bytes 10240 | tf_op jit(solution)/shard_map/add | solution.py:205
  (25 shorter events, 0.4 us)
Async XLA Ops:
  0.6 5.6 %copy-start = (bf16[49,128]{1,0:T(8,128)(2,1)S(1)}, bf16[49,128]{1,0:T(8,128)(2,1)}, u32[]{:S(2)}) copy-start(bf16[49,128]{1,0:T(8,128)(2,1)} %param.18) | copy-start | bytes 37636
  0.6 9.4 %copy-start.7 = (bf16[128,128]{1,0:T(8,128)(2,1)S(1)}, bf16[128,128]{1,0:T(8,128)(2,1)}, u32[]{:S(2)}) copy-start(bf16[128,128]{1,0:T(8,128)(2,1)} %param.21) | copy-start | bytes 98308
  1.6 6.5 %collective-permute-start = (bf16[2,256,128]{2,1,0:T(8,128)(2,1)S(1)}, bf16[2,256,128]{2,1,0:T(8,128)(2,1)S(1)}, u32[]{:S(2)}, u32[]{:S(2)}) collective-permute-start(bf16[2,256,128]{2,1,0:T(8,128)(2,1)S(1)} %bitcast.38), channel_id=1, source_target_pairs={{0,2},{1,3},{4,6},{5,7},{8,10},{9,11},{12,14},{13,15},{2,0},{3,1},... | collective-permute-start | bytes 393224 | tf_op jit(solution)/shard_map/ppermute | solution.py:23
  4.6 6.5 %collective-permute-start.3 = (bf16[2,256,128]{2,1,0:T(8,128)(2,1)S(1)}, bf16[2,256,128]{2,1,0:T(8,128)(2,1)S(1)}, u32[]{:S(2)}, u32[]{:S(2)}) collective-permute-start(bf16[2,256,128]{2,1,0:T(8,128)(2,1)S(1)} %bitcast.39), channel_id=1, source_target_pairs={{2,8},{3,9},{6,12},{7,13},{8,2},{9,3},{12,6},{13,7},{18,24},{19,25... | collective-permute-start | bytes 393224 | tf_op jit(solution)/shard_map/ppermute | solution.py:23
  8.2 9.7 %collective-permute-start.1 = (bf16[4,256,128]{2,1,0:T(8,128)(2,1)S(1)}, bf16[4,256,128]{2,1,0:T(8,128)(2,1)S(1)}, u32[]{:S(2)}, u32[]{:S(2)}) collective-permute-start(bf16[4,256,128]{2,1,0:T(8,128)(2,1)S(1)} %pad_maximum_fusion), channel_id=1, source_target_pairs={{0,4},{1,5},{2,6},{3,7},{8,12},{9,13},{10,14},{11,15},{4,0},{5,1},... | collective-permute-start | bytes 786440 | tf_op jit(solution)/shard_map/ppermute | solution.py:23
  10.1 9.8 %copy-start.1 = (bf16[2,12,256,128]{3,2,1,0:T(8,128)(2,1)S(1)}, bf16[2,12,256,128]{3,2,1,0:T(8,128)(2,1)}, u32[]{:S(2)}) copy-start(bf16[2,12,256,128]{3,2,1,0:T(8,128)(2,1)} %state_ref.1) | copy-start | bytes 4718596
  10.1 9.8 %copy-start.2 = (bf16[2,256,128]{2,1,0:T(8,128)(2,1)S(1)}, bf16[2,256,128]{2,1,0:T(8,128)(2,1)}, u32[]{:S(2)}) copy-start(bf16[2,256,128]{2,1,0:T(8,128)(2,1)} %feat_ref.1) | copy-start | bytes 393220
  10.1 9.8 %copy-start.3 = (bf16[2,256,128]{2,1,0:T(8,128)(2,1)S(1)}, bf16[2,256,128]{2,1,0:T(8,128)(2,1)}, u32[]{:S(2)}) copy-start(bf16[2,256,128]{2,1,0:T(8,128)(2,1)} %ctx_ref.1) | copy-start | bytes 393220
  10.1 9.8 %copy-start.4 = (bf16[256,256]{1,0:T(8,128)(2,1)S(1)}, bf16[256,256]{1,0:T(8,128)(2,1)}, u32[]{:S(2)}) copy-start(bf16[256,256]{1,0:T(8,128)(2,1)} %w_gates_ref.1) | copy-start | bytes 393220
  10.2 9.8 %copy-start.5 = (s32[2,12]{1,0:T(2,128)S(1)}, s32[2,12]{1,0:T(2,128)}, u32[]{:S(2)}) copy-start(s32[2,12]{1,0:T(2,128)} %target_ref.1) | copy-start | bytes 292
  10.2 9.8 %copy-start.6 = (bf16[2,128]{1,0:T(2,128)(2,1)S(1)}, bf16[2,128]{1,0:T(2,128)(2,1)}, u32[]{:S(2)}) copy-start(bf16[2,128]{1,0:T(2,128)(2,1)} %w_heads_ref.1) | copy-start | bytes 1540
  10.2 7.8 %collective-permute-start.2 = (bf16[4,256,128]{2,1,0:T(8,128)(2,1)S(1)}, bf16[4,256,128]{2,1,0:T(8,128)(2,1)S(1)}, u32[]{:S(2)}, u32[]{:S(2)}) collective-permute-start(bf16[4,256,128]{2,1,0:T(8,128)(2,1)S(1)} %pad_maximum_fusion), channel_id=1, source_target_pairs={{4,8},{5,9},{6,10},{7,11},{8,4},{9,5},{10,6},{11,7},{20,24},{21,25... | collective-permute-start | bytes 786440 | tf_op jit(solution)/shard_map/ppermute | solution.py:23
  11.0 7.6 %collective-permute-start.4 = (bf16[4,256,128]{2,1,0:T(8,128)(2,1)S(1)}, bf16[4,256,128]{2,1,0:T(8,128)(2,1)S(1)}, u32[]{:S(2)}, u32[]{:S(2)}) collective-permute-start(bf16[4,256,128]{2,1,0:T(8,128)(2,1)S(1)} %pad_maximum_fusion), channel_id=1, source_target_pairs={{0,1},{2,3},{4,5},{6,7},{8,9},{10,11},{12,13},{14,15},{1,0},{3,2},... | collective-permute-start | bytes 786440 | tf_op jit(solution)/shard_map/ppermute | solution.py:23
  11.1 8.8 %collective-permute-start.7 = (bf16[2,256,128]{2,1,0:T(8,128)(2,1)S(1)}, bf16[2,256,128]{2,1,0:T(8,128)(2,1)S(1)}, u32[]{:S(2)}, u32[]{:S(2)}) collective-permute-start(bf16[2,256,128]{2,1,0:T(8,128)(2,1)S(1)} %collective-permute-done.3), channel_id=1, source_target_pairs={{0,1},{2,3},{4,5},{6,7},{8,9},{10,11},{12,13},{14,15},{1,0},{3,2},... | collective-permute-start | bytes 393224 | tf_op jit(solution)/shard_map/ppermute | solution.py:23
  17.9 1.5 %collective-permute-start.5 = (bf16[4,256,128]{2,1,0:T(8,128)(2,1)S(1)}, bf16[4,256,128]{2,1,0:T(8,128)(2,1)S(1)}, u32[]{:S(2)}, u32[]{:S(2)}) collective-permute-start(bf16[4,256,128]{2,1,0:T(8,128)(2,1)S(1)} %collective-permute-done.1), channel_id=1, source_target_pairs={{0,1},{2,3},{4,5},{6,7},{8,9},{10,11},{12,13},{14,15},{1,0},{3,2},... | collective-permute-start | bytes 786440 | tf_op jit(solution)/shard_map/ppermute | solution.py:23
  18.0 1.9 %collective-permute-start.6 = (bf16[4,256,128]{2,1,0:T(8,128)(2,1)S(1)}, bf16[4,256,128]{2,1,0:T(8,128)(2,1)S(1)}, u32[]{:S(2)}, u32[]{:S(2)}) collective-permute-start(bf16[4,256,128]{2,1,0:T(8,128)(2,1)S(1)} %collective-permute-done.2), channel_id=1, source_target_pairs={{0,1},{2,3},{4,5},{6,7},{8,9},{10,11},{12,13},{14,15},{1,0},{3,2},... | collective-permute-start | bytes 786440 | tf_op jit(solution)/shard_map/ppermute | solution.py:23
  20.0 25.4 %copy-start.8 = (f32[2,256]{1,0:T(2,128)S(1)}, f32[2,256]{1,0:T(2,128)}, u32[]{:S(2)}) copy-start(f32[2,256]{1,0:T(2,128)} %param.16) | copy-start | bytes 6148
  20.0 25.4 %copy-start.9 = (f32[2,256]{1,0:T(2,128)S(1)}, f32[2,256]{1,0:T(2,128)}, u32[]{:S(2)}) copy-start(f32[2,256]{1,0:T(2,128)} %param.17) | copy-start | bytes 6148

commit v3 on v2

v3 whole, which is shorter than its diff:
```python
import functools
import math

import jax
import jax.numpy as jnp
import numpy as np
from jax import lax
from jax.experimental import pallas as pl
from jax.experimental.pallas import tpu as pltpu
from jax.sharding import PartitionSpec as P

REACH = 6
CORR_X = 3
CORR_Y = 3
WIDTH = 64
ROWS = 4
PIX = ROWS * WIDTH


def sent(value, pairs):
    count = lax.axis_size("edge")
    return lax.ppermute(
        value, "edge", [(a, b) for a, b in pairs if 0 <= a < count and 0 <= b < count]
    )


def swapped(value, steps, odd):
    low = [i for i in range(lax.axis_size("edge")) if (i // steps) % 2 == odd]
    low = [i for i in low if i + steps < lax.axis_size("edge")]
    return sent(value, [(i, i + steps) for i in low] + [(i + steps, i) for i in low])


def gather_window(own):
    count = lax.axis_size("edge")
    beside = swapped(own, 2, 0)
    two = jnp.concatenate([own, beside], 0)
    far = sent(own, [(i, i + REACH) if i % 4 >= 2 else (i, i - REACH) for i in range(count)])
    even = swapped(two, 4, 0)
    odd = swapped(two, 4, 1)
    mine = [two, even, odd, far]
    return mine + [swapped(piece, 1, 0) for piece in mine]


def window_block(block):
    own = lax.axis_index("edge")
    group, own_group = block // 4, own // 4
    column = ((block // 2) % 2 != (own // 2) % 2).astype(jnp.int32)
    place = jnp.where(group == own_group, 0, jnp.where(group == own_group ^ 1, 2, 4)) + column
    place = jnp.where(jnp.abs(group - own_group) == 2, 6, place)
    return place + 7 * (block % 2 != own % 2).astype(jnp.int32)


def corr_weights(w_corr):
    side = 2 * CORR_X + 1
    picks = np.zeros((ROWS, 2, PIX, (2 * CORR_Y + 1) * side), np.float32)
    for y in range(ROWS):
        for y2 in range(ROWS):
            for dx in range(-CORR_X, CORR_X + 1):
                if abs(y2 - y) <= CORR_Y:
                    for half in range(2):
                        lane = y2 * WIDTH + WIDTH - 1 - dx + half * (WIDTH // 2)
                        offset = (y2 - y + CORR_Y) * side + dx + CORR_X
                        picks[y, half, lane % PIX, offset] = 1
    picks = jnp.asarray(picks.reshape(-1, picks.shape[-1]), jnp.bfloat16)
    wide = jnp.dot(picks, w_corr).reshape(ROWS, 2, PIX, -1)
    return jnp.concatenate([wide[:, 0], wide[:, 1]], -1)


def conv_inputs(pair):
    return [r for r in range(2 * pair - 1, 2 * pair + 3) if 0 <= r < ROWS]


def conv_weights(w_cand, w_motion):
    blank = jnp.zeros_like(w_motion)
    pairs = []
    for pair in range(ROWS // 2):
        rows = []
        for dx in range(3):
            for r in conv_inputs(pair):
                rows.append(
                    jnp.concatenate(
                        [
                            w_cand[3 * (r - y + 1) + dx] if abs(r - y) <= 1 else blank
                            for y in (2 * pair, 2 * pair + 1)
                        ],
                        1,
                    )
                )
        rows.append(jnp.concatenate([w_motion, blank], 1))
        rows.append(jnp.concatenate([blank, w_motion], 1))
        pairs.append(jnp.concatenate(rows, 0))
    return jnp.stack(pairs)


def edge_kernel(
    batch, index_ref, target_ref, feat_ref, ctx_ref, state_ref, window_ref, w_corr_ref,
    w_gates_ref, w_conv_ref, w_heads_ref, new_ref, sums_ref, held_ref, sem
):
    chans = feat_ref.shape[-1]
    edges = state_ref.shape[0]
    neigh = edges // feat_ref.shape[0]
    narrow = jnp.bfloat16
    sums_ref[...] = jnp.zeros_like(sums_ref)
    inv_root = 1.0 / math.sqrt(chans)
    xs = lax.broadcasted_iota(jnp.int32, (WIDTH, PIX), 0)
    lanes = lax.broadcasted_iota(jnp.int32, (WIDTH, PIX), 1)
    scales = []
    for half in range(2):
        dxs = WIDTH // 2 - (lanes + 1 + WIDTH // 2 * (1 - half)) % WIDTH
        used = (jnp.abs(dxs) <= CORR_X) & (xs + dxs >= 0) & (xs + dxs < WIDTH)
        scales.append(jnp.where(used, inv_root, 0.0).astype(jnp.float32))
    cols = lax.broadcasted_iota(jnp.int32, (WIDTH, chans), 0)
    has_left = jnp.concatenate([cols > 0] * batch, 0)
    has_right = jnp.concatenate([cols < WIDTH - 1] * batch, 0)
    length = batch * WIDTH
    half_batch = batch // 2
    copies = []
    for start in range(0, edges, batch):
        these = list(range(start, start + batch))
        scores = [
            lax.dot_general(
                feat_ref[e // neigh], window_ref[index_ref[e // neigh, e % neigh]],
                (((1,), (1,)), ((), ())), preferred_element_type=jnp.float32,
            )
            for e in these
        ]
        motion, hidden, update_tanh, reset = [], [], [], []
        for y in range(ROWS):
            row = slice(y * WIDTH, (y + 1) * WIDTH)
            both = []
            for i in range(half_batch):
                one = pltpu.roll(scores[i][row], 0, 1, stride=1, stride_axis=0)
                two = pltpu.roll(
                    scores[i + half_batch][row], WIDTH // 2, 1, stride=1, stride_axis=0
                )
                both.append((one * scales[0] + two * scales[1]).astype(narrow))
            encoded = jnp.dot(
                jnp.concatenate(both, 0), w_corr_ref[y], preferred_element_type=jnp.float32
            )
            encoded = jnp.concatenate([encoded[:, :chans], encoded[:, chans:]], 0)
            ctx = jnp.concatenate([ctx_ref[e // neigh, row] for e in these], 0)
            motion.append((jnp.maximum(encoded, 0.0) + ctx.astype(jnp.float32)).astype(narrow))
            hidden.append(jnp.concatenate([state_ref[e, row] for e in these], 0))
        for y in range(ROWS):
            gates = jnp.tanh(
                jnp.dot(
                    jnp.concatenate([hidden[y], motion[y]], 1), w_gates_ref[...],
                    preferred_element_type=jnp.float32,
                )
            )
            half_hidden = 0.5 * hidden[y].astype(jnp.float32)
            update_tanh.append(gates[:, :chans])
            reset.append(half_hidden + half_hidden * gates[:, chans:])
        left = [jnp.where(has_left, pltpu.roll(r, 1, 0), 0.0).astype(narrow) for r in reset]
        right = [
            jnp.where(has_right, pltpu.roll(r, length - 1, 0), 0.0).astype(narrow) for r in reset
        ]
        centre = [r.astype(narrow) for r in reset]
        conv = []
        for pair in range(ROWS // 2):
            taps = [side[r] for side in (left, centre, right) for r in conv_inputs(pair)]
            taps = jnp.concatenate(taps + motion[2 * pair : 2 * pair + 2], 1)
            out = jnp.dot(taps, w_conv_ref[pair], preferred_element_type=jnp.float32)
            conv += [out[:, :chans], out[:, chans:]]
        new_hidden = []
        for y in range(ROWS):
            wide = hidden[y].astype(jnp.float32)
            update = 0.5 + 0.5 * update_tanh[y]
            new_hidden.append((wide + update * (jnp.tanh(conv[y]) - wide)).astype(narrow))
        for i, e in enumerate(these):
            mine = jnp.concatenate([n[i * WIDTH : (i + 1) * WIDTH] for n in new_hidden], 0)
            held_ref[e] = mine
            heads = lax.dot_general(
                w_heads_ref[...], mine, (((1,), (1,)), ((), ())),
                preferred_element_type=jnp.float32,
            )
            confidence = 0.5 + 0.5 * jnp.tanh(0.5 * heads[1:2])
            sums_ref[target_ref[e // neigh, e % neigh]] += jnp.concatenate(
                [confidence * heads[0:1], confidence], 0
            )
        copies.append(
            pltpu.make_async_copy(
                held_ref.at[pl.ds(start, batch)], new_ref.at[pl.ds(start, batch)],
                sem.at[start // batch],
            )
        )
        copies[-1].start()
    for copy in copies:
        copy.wait()


def on_device(
    features, context, states, neighbours, depths, damping,
    w_corr, w_gates, w_cand, w_motion, w_heads,
):
    frames_here, pixels, chans = features.shape
    edges = frames_here * states.shape[1]
    mirrored = features.reshape(frames_here, ROWS, WIDTH, chans)[:, :, ::-1].reshape(features.shape)
    window = jnp.concatenate(gather_window(mirrored), 0)
    blocks = neighbours // frames_here
    local_index = window_block(blocks) * frames_here + neighbours % frames_here
    frames_all = lax.axis_size("edge") * frames_here
    batch = 12
    vmem = pl.BlockSpec(memory_space=pltpu.VMEM)
    smem = pl.BlockSpec(memory_space=pltpu.SMEM)
    new_states, sums = pl.pallas_call(
        functools.partial(edge_kernel, batch),
        out_shape=(
            jax.ShapeDtypeStruct((edges, pixels, chans), states.dtype),
            jax.ShapeDtypeStruct((frames_all, 2, pixels), jnp.float32),
        ),
        in_specs=[smem, smem] + [vmem] * 8,
        out_specs=[pl.BlockSpec(memory_space=pl.ANY), vmem],
        scratch_shapes=[
            pltpu.VMEM((edges, pixels, chans), states.dtype),
            pltpu.SemaphoreType.DMA((edges // batch,)),
        ],
        compiler_params=pltpu.CompilerParams(vmem_limit_bytes=32 * 1024 * 1024),
        name="edge_update",
    )(
        local_index, neighbours, features, context, states.reshape(edges, pixels, chans),
        window, corr_weights(w_corr), w_gates * jnp.bfloat16(0.5),
        conv_weights(w_cand, w_motion), w_heads,
    )
    new_states = new_states.reshape(states.shape)
    sums = sums.reshape(-1, frames_here, 2, pixels)
    sums = jnp.sum(lax.all_to_all(sums, "edge", 0, 0, tiled=True), 0)
    new_depths = depths + sums[:, 0] / (damping + sums[:, 1])
    return (new_states, new_depths)


def solution(mesh):
    split = P(("groups", "edge"))
    return jax.shard_map(
        on_device,
        mesh=mesh,
        in_specs=(split,) * 6 + (P(),) * 5,
        out_specs=(split, split),
        check_vma=False,
    )
```

time: 46.3 us -> 42.7 us (0.922)
  Pallas kernels: 11.2 us -> 7.6 us
  waiting for transfers between devices: 7.45 us -> 7.92 us
    pallas_call x1, Pallas kernels: 11.2 us -> 7.6 us  [on_device(): pl.pallas_call(functools.partial(edge_kernel, batch), out_shape=(jax.Shap...]
    squeeze x1 -> x2, local copies, waits for them, and re-layouts: 0.91 us -> 0.06 us  [the longest x1 0.04 us: corr_weights(): return jnp.concatenate([wide[:, 0], wide[:, 1]], -1)]
    add x1, other arithmetic: 0.71 us -> 0.03 us  [on_device(): local_index = window_block(blocks) * frames_here + neighbours % frames_here]
    ppermute x8, waiting for transfers between devices: 7.45 us -> 7.92 us  [sent(): lax.ppermute(value, 'edge', [(a, b) for a, b in pairs if 0 <= a < count a...]
    unnamed x28 -> x36, local copies, waits for them, and re-layouts: 0.29 us -> 0.76 us
  transfers between devices with their start and end apart: 8 -> 8, of which waited for: 3 -> 4; matrix products, arithmetic and copies ran while one was open for 7% -> 5% of each run, Pallas kernels for 0% -> 0%
where the time goes in v3:
time: 42.7 us; the launch traced here: 42.4 us
  blocking collectives  14.1 us (33%)
  waiting for transfers between devices  7.92 us (19%)
  Pallas kernels  7.6 us (18%)
  starting transfers between devices  7.5 us (18%)
  local copies, waits for them, and re-layouts  1.88 us (4%)
  matrix products  1.31 us (3%)
  between operations  1.12 us (3%)
  other arithmetic  0.98 us (2%)
    all_to_all x1, blocking collectives, on_device(): sums = jnp.sum(lax.all_to_all(sums, 'edge', 0, 0, tiled=True), 0)  14.1 us
    ppermute x8, waiting for transfers between devices, sent(): lax.ppermute(value, 'edge', [(a, b) for a, b in pairs if 0 <= a < count a...  7.92 us
    pallas_call x1, Pallas kernels, on_device(): pl.pallas_call(functools.partial(edge_kernel, batch), out_shape=(jax.Shap...  7.6 us
    ppermute x8, starting transfers between devices, sent(): lax.ppermute(value, 'edge', [(a, b) for a, b in pairs if 0 <= a < count a...  7.5 us
    dot_general x1, matrix products, corr_weights(): wide = jnp.dot(picks, w_corr).reshape(ROWS, 2, PIX, -1)  1.31 us
    rev x1, local copies, waits for them, and re-layouts, on_device(): features.reshape(frames_here, ROWS, WIDTH, chans)[:, :, ::-1]  1 us
  transfers between devices with their start and end apart: 8, of which 4 were waited for; matrix products, arithmetic and copies ran while one was open for 5% of the time, Pallas kernels for 0%

profile of v3, /device:TPU:0, one launch (start us, length us, event | category | flops | bytes accessed | tf_op | source)
XLA Modules:
  0.0 42.4 jit_solution(11313905641844986485)
XLA Ops:
  0.6 0.0 copy-start
  0.7 1.0 %rev.3 = bf16[2,4,64,128]{3,2,1,0:T(8,128)(2,1)S(1)} reverse(bf16[2,4,64,128]{3,2,1,0:T(8,128)(2,1)} %bitcast.47), dimensions={2} | reverse | bytes 262144 | tf_op jit(solution)/shard_map/rev | solution.py:198
  1.7 3.0 %collective-permute-start = (bf16[2,256,128]{2,1,0:T(8,128)(2,1)S(1)}, bf16[2,256,128]{2,1,0:T(8,128)(2,1)S(1)}, u32[]{:S(2)}, u32[]{:S(2)}) collective-permute-start(bf16[2,256,128]{2,1,0:T(8,128)(2,1)S(1)} %bitcast.50), channel_id=1, source_target_pairs={{0,2},{1,3},{4,6},{5,7},{8,10},{9,11},{12,14},{13,15},{2,0},{3,1},... | collective-permute-start | bytes 393224 | tf_op jit(solution)/shard_map/ppermute | solution.py:22
  4.7 0.7 %collective-permute-start.3 = (bf16[2,256,128]{2,1,0:T(8,128)(2,1)S(1)}, bf16[2,256,128]{2,1,0:T(8,128)(2,1)S(1)}, u32[]{:S(2)}, u32[]{:S(2)}) collective-permute-start(bf16[2,256,128]{2,1,0:T(8,128)(2,1)S(1)} %bitcast.51), channel_id=1, source_target_pairs={{2,8},{3,9},{6,12},{7,13},{8,2},{9,3},{12,6},{13,7},{18,24},{19,25... | collective-permute-start | bytes 393224 | tf_op jit(solution)/shard_map/ppermute | solution.py:22
  5.4 1.3 %fusion.8 = bf16[2048,128]{1,0:T(8,128)(2,1)S(1)} fusion(bf16[2048,49]{1,0:T(8,128)(2,1)} %constant.100.clone, bf16[49,128]{1,0:T(8,128)(2,1)S(1)} %copy-done), kind=kOutput, calls=%fused_computation.83 | convolution fusion | flops 25690112 | bytes 737536 | tf_op jit(solution)/shard_map/dot_general | solution.py:65
  6.7 0.0 copy-start.6
  7.0 0.0 copy-start.4
  7.1 0.4 copy-done.6
  7.5 0.1 pad_maximum_fusion.w_conv_ref
  7.7 0.0 copy-done.4
  7.7 0.4 %collective-permute-done = bf16[2,256,128]{2,1,0:T(8,128)(2,1)S(1)} collective-permute-done((bf16[2,256,128]{2,1,0:T(8,128)(2,1)S(1)}, bf16[2,256,128]{2,1,0:T(8,128)(2,1)S(1)}, u32[]{:S(2)}, u32[]{:S(2)}) %collective-permute-start) | collective-permute-done | bytes 131104 | tf_op jit(solution)/shard_map/ppermute | solution.py:22
  8.2 1.9 %collective-permute-start.1 = (bf16[4,256,128]{2,1,0:T(8,128)(2,1)S(1)}, bf16[4,256,128]{2,1,0:T(8,128)(2,1)S(1)}, u32[]{:S(2)}, u32[]{:S(2)}) collective-permute-start(bf16[4,256,128]{2,1,0:T(8,128)(2,1)S(1)} %pad_maximum_fusion.2), channel_id=1, source_target_pairs={{0,4},{1,5},{2,6},{3,7},{8,12},{9,13},{10,14},{11,15},{4,0},{5,1},... | collective-permute-start | bytes 786440 | tf_op jit(solution)/shard_map/ppermute | solution.py:22
  10.1 0.1 pad_maximum_fusion.1.w_corr_ref
  10.2 0.0 copy-start.1
  10.2 0.0 copy-start.2
  10.2 0.0 copy-start.3
  10.2 0.0 copy-start.5
  10.2 0.8 %collective-permute-start.2 = (bf16[4,256,128]{2,1,0:T(8,128)(2,1)S(1)}, bf16[4,256,128]{2,1,0:T(8,128)(2,1)S(1)}, u32[]{:S(2)}, u32[]{:S(2)}) collective-permute-start(bf16[4,256,128]{2,1,0:T(8,128)(2,1)S(1)} %pad_maximum_fusion.2), channel_id=1, source_target_pairs={{4,8},{5,9},{6,10},{7,11},{8,4},{9,5},{10,6},{11,7},{20,24},{21,25... | collective-permute-start | bytes 786440 | tf_op jit(solution)/shard_map/ppermute | solution.py:22
  11.0 0.1 collective-permute-start.4
  11.1 0.0 collective-permute-done.3
  11.1 0.5 %collective-permute-start.7 = (bf16[2,256,128]{2,1,0:T(8,128)(2,1)S(1)}, bf16[2,256,128]{2,1,0:T(8,128)(2,1)S(1)}, u32[]{:S(2)}, u32[]{:S(2)}) collective-permute-start(bf16[2,256,128]{2,1,0:T(8,128)(2,1)S(1)} %collective-permute-done.3), channel_id=1, source_target_pairs={{0,1},{2,3},{4,5},{6,7},{8,9},{10,11},{12,13},{14,15},{1,0},{3,2},... | collective-permute-start | bytes 393224 | tf_op jit(solution)/shard_map/ppermute | solution.py:22
  11.6 6.3 %collective-permute-done.1 = bf16[4,256,128]{2,1,0:T(8,128)(2,1)S(1)} collective-permute-done((bf16[4,256,128]{2,1,0:T(8,128)(2,1)S(1)}, bf16[4,256,128]{2,1,0:T(8,128)(2,1)S(1)}, u32[]{:S(2)}, u32[]{:S(2)}) %collective-permute-start.1) | collective-permute-done | bytes 262176 | tf_op jit(solution)/shard_map/ppermute | solution.py:22
  18.0 0.0 collective-permute-start.5
  18.0 0.6 %collective-permute-start.6 = (bf16[4,256,128]{2,1,0:T(8,128)(2,1)S(1)}, bf16[4,256,128]{2,1,0:T(8,128)(2,1)S(1)}, u32[]{:S(2)}, u32[]{:S(2)}) collective-permute-start(bf16[4,256,128]{2,1,0:T(8,128)(2,1)S(1)} %collective-permute-done.2), channel_id=1, source_target_pairs={{0,1},{2,3},{4,5},{6,7},{8,9},{10,11},{12,13},{14,15},{1,0},{3,2},... | collective-permute-start | bytes 786440 | tf_op jit(solution)/shard_map/ppermute | solution.py:22
  18.7 0.8 %collective-permute-done.5 = bf16[4,256,128]{2,1,0:T(8,128)(2,1)S(1)} collective-permute-done((bf16[4,256,128]{2,1,0:T(8,128)(2,1)S(1)}, bf16[4,256,128]{2,1,0:T(8,128)(2,1)S(1)}, u32[]{:S(2)}, u32[]{:S(2)}) %collective-permute-start.5) | collective-permute-done | bytes 262176 | tf_op jit(solution)/shard_map/ppermute | solution.py:22
  19.6 0.3 collective-permute-done.6
  19.9 0.0 collective-permute-done.7
  20.0 0.0 copy-start.9
  20.0 0.0 copy-start.10
  20.0 7.6 %edge_update.1 = (bf16[24,256,128]{2,1,0:T(8,128)(2,1)}, f32[32,2,256]{2,1,0:T(2,128)S(1)}) custom-call(s32[2,12]{1,0:T(2,128)S(1)} %fusion.4.index_ref, s32[2,12]{1,0:T(2,128)S(1)} %copy-done.4, bf16[2,256,128]{2,1,0:T(8,128)(2,1)S(1)} %copy-done.2, bf16[2,256,128]{2,1,0:T(8,128)(2,1)S(1)} %copy-done.3, bf16[24,256,128]{2,1,0:T(8,128)(2,1)S(1)} %bitcast.46, ...), custom_call_target="tpu_custom_call" | custom-call | tf_op jit(solution)/shard_map/edge_update/pallas_call | solution.py:206
  27.6 14.1 %all_to_all.5 = f32[16,2,2,256]{3,2,1,0:T(2,128)S(1)} all-to-all(f32[16,2,2,256]{3,2,1,0:T(2,128)S(1)} %bitcast.48), channel_id=1, replica_groups=mesh['groups'=2,'edge'=16] {'edge'}, dimensions={0} | all-to-all | bytes 131072 | tf_op jit(solution)/shard_map/all_to_all | solution.py:227
  41.8 0.6 %fusion.1 = f32[2,256]{1,0:T(2,128)} fusion(f32[2,256]{1,0:T(2,128)S(1)} %copy-done.9, f32[2,1,256]{2,1,0:T(1,128)S(1)} %get-tuple-element.32, f32[2,256]{1,0:T(2,128)S(1)} %copy-done.10, f32[2,1,256]{2,1,0:T(1,128)S(1)} %get-tuple-element.31), kind=kLoop, calls=%fused_computation.56 | loop fusion | flops 1536 | bytes 10240 | tf_op jit(solution)/shard_map/add | solution.py:228
  (43 shorter events, 0.6 us)
Async XLA Ops:
  0.6 4.8 %copy-start = (bf16[49,128]{1,0:T(8,128)(2,1)S(1)}, bf16[49,128]{1,0:T(8,128)(2,1)}, u32[]{:S(2)}) copy-start(bf16[49,128]{1,0:T(8,128)(2,1)} %param.18) | copy-start | bytes 37636
  0.6 6.1 %copy-start.8 = (bf16[256,256]{1,0:T(8,128)(2,1)S(1)}, bf16[256,256]{1,0:T(8,128)(2,1)}, u32[]{:S(2)}) copy-start(bf16[256,256]{1,0:T(8,128)(2,1)} %param.19) | copy-start | bytes 393220
  0.7 6.1 %copy-start.7 = (bf16[9,128,128]{2,1,0:T(8,128)(2,1)S(1)}, bf16[9,128,128]{2,1,0:T(8,128)(2,1)}, u32[]{:S(2)}) copy-start(bf16[9,128,128]{2,1,0:T(8,128)(2,1)} %param.20) | copy-start | bytes 884740
  1.7 6.5 %collective-permute-start = (bf16[2,256,128]{2,1,0:T(8,128)(2,1)S(1)}, bf16[2,256,128]{2,1,0:T(8,128)(2,1)S(1)}, u32[]{:S(2)}, u32[]{:S(2)}) collective-permute-start(bf16[2,256,128]{2,1,0:T(8,128)(2,1)S(1)} %bitcast.50), channel_id=1, source_target_pairs={{0,2},{1,3},{4,6},{5,7},{8,10},{9,11},{12,14},{13,15},{2,0},{3,1},... | collective-permute-start | bytes 393224 | tf_op jit(solution)/shard_map/ppermute | solution.py:22
  4.7 6.4 %collective-permute-start.3 = (bf16[2,256,128]{2,1,0:T(8,128)(2,1)S(1)}, bf16[2,256,128]{2,1,0:T(8,128)(2,1)S(1)}, u32[]{:S(2)}, u32[]{:S(2)}) collective-permute-start(bf16[2,256,128]{2,1,0:T(8,128)(2,1)S(1)} %bitcast.51), channel_id=1, source_target_pairs={{2,8},{3,9},{6,12},{7,13},{8,2},{9,3},{12,6},{13,7},{18,24},{19,25... | collective-permute-start | bytes 393224 | tf_op jit(solution)/shard_map/ppermute | solution.py:22
  6.7 0.8 %copy-start.6 = (bf16[128,128]{1,0:T(8,128)(2,1)S(1)}, bf16[128,128]{1,0:T(8,128)(2,1)}, u32[]{:S(2)}) copy-start(bf16[128,128]{1,0:T(8,128)(2,1)} %param.21) | copy-start | bytes 98308
  7.0 0.7 %copy-start.4 = (s32[2,12]{1,0:T(2,128)S(1)}, s32[2,12]{1,0:T(2,128)}, u32[]{:S(2)}) copy-start(s32[2,12]{1,0:T(2,128)} %target_ref.1) | copy-start | bytes 292
  8.2 9.8 %collective-permute-start.1 = (bf16[4,256,128]{2,1,0:T(8,128)(2,1)S(1)}, bf16[4,256,128]{2,1,0:T(8,128)(2,1)S(1)}, u32[]{:S(2)}, u32[]{:S(2)}) collective-permute-start(bf16[4,256,128]{2,1,0:T(8,128)(2,1)S(1)} %pad_maximum_fusion.2), channel_id=1, source_target_pairs={{0,4},{1,5},{2,6},{3,7},{8,12},{9,13},{10,14},{11,15},{4,0},{5,1},... | collective-permute-start | bytes 786440 | tf_op jit(solution)/shard_map/ppermute | solution.py:22
  10.2 9.8 %copy-start.1 = (bf16[2,12,256,128]{3,2,1,0:T(8,128)(2,1)S(1)}, bf16[2,12,256,128]{3,2,1,0:T(8,128)(2,1)}, u32[]{:S(2)}) copy-start(bf16[2,12,256,128]{3,2,1,0:T(8,128)(2,1)} %param.14) | copy-start | bytes 4718596
  10.2 9.8 %copy-start.2 = (bf16[2,256,128]{2,1,0:T(8,128)(2,1)S(1)}, bf16[2,256,128]{2,1,0:T(8,128)(2,1)}, u32[]{:S(2)}) copy-start(bf16[2,256,128]{2,1,0:T(8,128)(2,1)} %feat_ref.1) | copy-start | bytes 393220
  10.2 9.8 %copy-start.3 = (bf16[2,256,128]{2,1,0:T(8,128)(2,1)S(1)}, bf16[2,256,128]{2,1,0:T(8,128)(2,1)}, u32[]{:S(2)}) copy-start(bf16[2,256,128]{2,1,0:T(8,128)(2,1)} %ctx_ref.1) | copy-start | bytes 393220
  10.2 9.8 %copy-start.5 = (bf16[2,128]{1,0:T(2,128)(2,1)S(1)}, bf16[2,128]{1,0:T(2,128)(2,1)}, u32[]{:S(2)}) copy-start(bf16[2,128]{1,0:T(2,128)(2,1)} %w_heads_ref.1) | copy-start | bytes 1540
  10.2 7.8 %collective-permute-start.2 = (bf16[4,256,128]{2,1,0:T(8,128)(2,1)S(1)}, bf16[4,256,128]{2,1,0:T(8,128)(2,1)S(1)}, u32[]{:S(2)}, u32[]{:S(2)}) collective-permute-start(bf16[4,256,128]{2,1,0:T(8,128)(2,1)S(1)} %pad_maximum_fusion.2), channel_id=1, source_target_pairs={{4,8},{5,9},{6,10},{7,11},{8,4},{9,5},{10,6},{11,7},{20,24},{21,25... | collective-permute-start | bytes 786440 | tf_op jit(solution)/shard_map/ppermute | solution.py:22
  11.0 7.6 %collective-permute-start.4 = (bf16[4,256,128]{2,1,0:T(8,128)(2,1)S(1)}, bf16[4,256,128]{2,1,0:T(8,128)(2,1)S(1)}, u32[]{:S(2)}, u32[]{:S(2)}) collective-permute-start(bf16[4,256,128]{2,1,0:T(8,128)(2,1)S(1)} %pad_maximum_fusion.2), channel_id=1, source_target_pairs={{0,1},{2,3},{4,5},{6,7},{8,9},{10,11},{12,13},{14,15},{1,0},{3,2},... | collective-permute-start | bytes 786440 | tf_op jit(solution)/shard_map/ppermute | solution.py:22
  11.1 8.8 %collective-permute-start.7 = (bf16[2,256,128]{2,1,0:T(8,128)(2,1)S(1)}, bf16[2,256,128]{2,1,0:T(8,128)(2,1)S(1)}, u32[]{:S(2)}, u32[]{:S(2)}) collective-permute-start(bf16[2,256,128]{2,1,0:T(8,128)(2,1)S(1)} %collective-permute-done.3), channel_id=1, source_target_pairs={{0,1},{2,3},{4,5},{6,7},{8,9},{10,11},{12,13},{14,15},{1,0},{3,2},... | collective-permute-start | bytes 393224 | tf_op jit(solution)/shard_map/ppermute | solution.py:22
  18.0 1.5 %collective-permute-start.5 = (bf16[4,256,128]{2,1,0:T(8,128)(2,1)S(1)}, bf16[4,256,128]{2,1,0:T(8,128)(2,1)S(1)}, u32[]{:S(2)}, u32[]{:S(2)}) collective-permute-start(bf16[4,256,128]{2,1,0:T(8,128)(2,1)S(1)} %collective-permute-done.1), channel_id=1, source_target_pairs={{0,1},{2,3},{4,5},{6,7},{8,9},{10,11},{12,13},{14,15},{1,0},{3,2},... | collective-permute-start | bytes 786440 | tf_op jit(solution)/shard_map/ppermute | solution.py:22
  18.0 1.9 %collective-permute-start.6 = (bf16[4,256,128]{2,1,0:T(8,128)(2,1)S(1)}, bf16[4,256,128]{2,1,0:T(8,128)(2,1)S(1)}, u32[]{:S(2)}, u32[]{:S(2)}) collective-permute-start(bf16[4,256,128]{2,1,0:T(8,128)(2,1)S(1)} %collective-permute-done.2), channel_id=1, source_target_pairs={{0,1},{2,3},{4,5},{6,7},{8,9},{10,11},{12,13},{14,15},{1,0},{3,2},... | collective-permute-start | bytes 786440 | tf_op jit(solution)/shard_map/ppermute | solution.py:22
  20.0 21.8 %copy-start.9 = (f32[2,256]{1,0:T(2,128)S(1)}, f32[2,256]{1,0:T(2,128)}, u32[]{:S(2)}) copy-start(f32[2,256]{1,0:T(2,128)} %param.16) | copy-start | bytes 6148
  20.0 21.8 %copy-start.10 = (f32[2,256]{1,0:T(2,128)S(1)}, f32[2,256]{1,0:T(2,128)}, u32[]{:S(2)}) copy-start(f32[2,256]{1,0:T(2,128)} %param.17) | copy-start | bytes 6148

commit v4 on v3

--- a/solution.py
+++ b/solution.py
@@ -14,6 +14,7 @@
 CORR_Y = 3
 WIDTH = 64
 ROWS = 4
+SHARE = 2
 PIX = ROWS * WIDTH
 
 
@@ -34,7 +35,9 @@
     count = lax.axis_size("edge")
     beside = swapped(own, 2, 0)
     two = jnp.concatenate([own, beside], 0)
-    far = sent(own, [(i, i + REACH) if i % 4 >= 2 else (i, i - REACH) for i in range(count)])
+    step = [REACH, 8]
+    far = sent(own, [(i, i + step[i % 2] * (1 if i % 4 >= 2 else -1)) for i in range(count)])
+    far = sent(far, [(i, i ^ 2 if i % 2 else i) for i in range(count)])
     even = swapped(two, 4, 0)
     odd = swapped(two, 4, 1)
     mine = [two, even, odd, far]
@@ -52,18 +55,18 @@
 
 def corr_weights(w_corr):
     side = 2 * CORR_X + 1
-    picks = np.zeros((ROWS, 2, PIX, (2 * CORR_Y + 1) * side), np.float32)
+    picks = np.zeros((ROWS, SHARE, PIX, (2 * CORR_Y + 1) * side), np.float32)
     for y in range(ROWS):
         for y2 in range(ROWS):
             for dx in range(-CORR_X, CORR_X + 1):
                 if abs(y2 - y) <= CORR_Y:
-                    for half in range(2):
-                        lane = y2 * WIDTH + WIDTH - 1 - dx + half * (WIDTH // 2)
+                    for k in range(SHARE):
+                        lane = y2 * WIDTH + WIDTH - 1 - dx + k * (WIDTH // SHARE)
                         offset = (y2 - y + CORR_Y) * side + dx + CORR_X
-                        picks[y, half, lane % PIX, offset] = 1
+                        picks[y, k, lane % PIX, offset] = 1
     picks = jnp.asarray(picks.reshape(-1, picks.shape[-1]), jnp.bfloat16)
-    wide = jnp.dot(picks, w_corr).reshape(ROWS, 2, PIX, -1)
-    return jnp.concatenate([wide[:, 0], wide[:, 1]], -1)
+    wide = jnp.dot(picks, w_corr).reshape(ROWS, SHARE, PIX, -1)
+    return jnp.concatenate([wide[:, k] for k in range(SHARE)], -1)
 
 
 def conv_inputs(pair):
@@ -105,39 +108,41 @@
     xs = lax.broadcasted_iota(jnp.int32, (WIDTH, PIX), 0)
     lanes = lax.broadcasted_iota(jnp.int32, (WIDTH, PIX), 1)
     scales = []
-    for half in range(2):
-        dxs = WIDTH // 2 - (lanes + 1 + WIDTH // 2 * (1 - half)) % WIDTH
-        used = (jnp.abs(dxs) <= CORR_X) & (xs + dxs >= 0) & (xs + dxs < WIDTH)
-        scales.append(jnp.where(used, inv_root, 0.0).astype(jnp.float32))
+    for k in range(SHARE):
+        target = WIDTH - 1 - (lanes + PIX - k * (WIDTH // SHARE)) % WIDTH
+        scales.append(jnp.where(jnp.abs(target - xs) <= CORR_X, inv_root, 0.0).astype(jnp.float32))
     cols = lax.broadcasted_iota(jnp.int32, (WIDTH, chans), 0)
     has_left = jnp.concatenate([cols > 0] * batch, 0)
     has_right = jnp.concatenate([cols < WIDTH - 1] * batch, 0)
     length = batch * WIDTH
-    half_batch = batch // 2
+    quarter = batch // SHARE
     copies = []
     for start in range(0, edges, batch):
         these = list(range(start, start + batch))
-        scores = [
-            lax.dot_general(
-                feat_ref[e // neigh], window_ref[index_ref[e // neigh, e % neigh]],
-                (((1,), (1,)), ((), ())), preferred_element_type=jnp.float32,
-            )
-            for e in these
-        ]
+        scores = []
+        for i, e in enumerate(these):
+            target = window_ref.at[index_ref[e // neigh, e % neigh]]
+            turn = i // quarter * (WIDTH // SHARE)
+            target = [target[PIX - turn :], target[: PIX - turn]] if turn else [target[...]]
+            scores.append(
+                lax.dot_general(
+                    feat_ref[e // neigh], jnp.concatenate(target, 0),
+                    (((1,), (1,)), ((), ())), preferred_element_type=jnp.float32,
+                )
+            )
         motion, hidden, update_tanh, reset = [], [], [], []
         for y in range(ROWS):
             row = slice(y * WIDTH, (y + 1) * WIDTH)
-            both = []
-            for i in range(half_batch):
-                one = pltpu.roll(scores[i][row], 0, 1, stride=1, stride_axis=0)
-                two = pltpu.roll(
-                    scores[i + half_batch][row], WIDTH // 2, 1, stride=1, stride_axis=0
-                )
-                both.append((one * scales[0] + two * scales[1]).astype(narrow))
+            shared = []
+            for i in range(quarter):
+                bands = sum(scores[i + k * quarter][row] * scales[k] for k in range(SHARE))
+                shared.append(pltpu.roll(bands, 0, 1, stride=1, stride_axis=0).astype(narrow))
             encoded = jnp.dot(
-                jnp.concatenate(both, 0), w_corr_ref[y], preferred_element_type=jnp.float32
-            )
-            encoded = jnp.concatenate([encoded[:, :chans], encoded[:, chans:]], 0)
+                jnp.concatenate(shared, 0), w_corr_ref[y], preferred_element_type=jnp.float32
+            )
+            encoded = jnp.concatenate(
+                [encoded[:, k * chans : (k + 1) * chans] for k in range(SHARE)], 0
+            )
             ctx = jnp.concatenate([ctx_ref[e // neigh, row] for e in these], 0)
             motion.append((jnp.maximum(encoded, 0.0) + ctx.astype(jnp.float32)).astype(narrow))
             hidden.append(jnp.concatenate([state_ref[e, row] for e in these], 0))
@@ -156,20 +161,28 @@
             jnp.where(has_right, pltpu.roll(r, length - 1, 0), 0.0).astype(narrow) for r in reset
         ]
         centre = [r.astype(narrow) for r in reset]
-        conv = []
+        done = []
         for pair in range(ROWS // 2):
             taps = [side[r] for side in (left, centre, right) for r in conv_inputs(pair)]
             taps = jnp.concatenate(taps + motion[2 * pair : 2 * pair + 2], 1)
-            out = jnp.dot(taps, w_conv_ref[pair], preferred_element_type=jnp.float32)
-            conv += [out[:, :chans], out[:, chans:]]
-        new_hidden = []
-        for y in range(ROWS):
-            wide = hidden[y].astype(jnp.float32)
-            update = 0.5 + 0.5 * update_tanh[y]
-            new_hidden.append((wide + update * (jnp.tanh(conv[y]) - wide)).astype(narrow))
+            conv = jnp.dot(taps, w_conv_ref[pair], preferred_element_type=jnp.float32)
+            for part in range(2):
+                y = 2 * pair + part
+                wide = hidden[y].astype(jnp.float32)
+                update = 0.5 + 0.5 * update_tanh[y]
+                candidate = jnp.tanh(conv[:, part * chans : (part + 1) * chans])
+                done.append((wide + update * (candidate - wide)).astype(narrow))
+                for i, e in enumerate(these):
+                    held_ref[e, y * WIDTH : (y + 1) * WIDTH] = done[y][i * WIDTH : (i + 1) * WIDTH]
+            place = (pl.ds(start, batch), pl.ds(2 * pair * WIDTH, 2 * WIDTH))
+            copies.append(
+                pltpu.make_async_copy(
+                    held_ref.at[place], new_ref.at[place], sem.at[start // batch, pair]
+                )
+            )
+            copies[-1].start()
         for i, e in enumerate(these):
-            mine = jnp.concatenate([n[i * WIDTH : (i + 1) * WIDTH] for n in new_hidden], 0)
-            held_ref[e] = mine
+            mine = jnp.concatenate([n[i * WIDTH : (i + 1) * WIDTH] for n in done], 0)
             heads = lax.dot_general(
                 w_heads_ref[...], mine, (((1,), (1,)), ((), ())),
                 preferred_element_type=jnp.float32,
@@ -178,13 +191,6 @@
             sums_ref[target_ref[e // neigh, e % neigh]] += jnp.concatenate(
                 [confidence * heads[0:1], confidence], 0
             )
-        copies.append(
-            pltpu.make_async_copy(
-                held_ref.at[pl.ds(start, batch)], new_ref.at[pl.ds(start, batch)],
-                sem.at[start // batch],
-            )
-        )
-        copies[-1].start()
     for copy in copies:
         copy.wait()
 
@@ -213,7 +219,7 @@
         out_specs=[pl.BlockSpec(memory_space=pl.ANY), vmem],
         scratch_shapes=[
             pltpu.VMEM((edges, pixels, chans), states.dtype),
-            pltpu.SemaphoreType.DMA((edges // batch,)),
+            pltpu.SemaphoreType.DMA((edges // batch, ROWS // 2)),
         ],
         compiler_params=pltpu.CompilerParams(vmem_limit_bytes=32 * 1024 * 1024),
         name="edge_update",

time: 42.7 us -> 41.5 us (0.972)
  starting transfers between devices: 7.5 us -> 15.6 us
  waiting for transfers between devices: 7.92 us -> 1.58 us
  blocking collectives: 14.1 us -> 11.5 us
  Pallas kernels: 7.6 us -> 7.13 us
    ppermute x8 -> x9, starting transfers between devices: 7.5 us -> 15.6 us  [sent(): lax.ppermute(value, 'edge', [(a, b) for a, b in pairs if 0 <= a < count a...]
    ppermute x8 -> x9, waiting for transfers between devices: 7.92 us -> 1.58 us  [sent(): lax.ppermute(value, 'edge', [(a, b) for a, b in pairs if 0 <= a < count a...]
    all_to_all x1, blocking collectives: 14.1 us -> 11.5 us  [on_device(): sums = jnp.sum(lax.all_to_all(sums, 'edge', 0, 0, tiled=True), 0)]
    pallas_call x1, Pallas kernels: 7.6 us -> 7.13 us  [on_device(): pl.pallas_call(functools.partial(edge_kernel, batch), out_shape=(jax.Shap...]
  transfers between devices with their start and end apart: 8 -> 9, of which waited for: 4 -> 3; matrix products, arithmetic and copies ran while one was open for 5% -> 5% of each run, Pallas kernels for 0% -> 0%
where the time goes in v4:
time: 41.5 us; the launch traced here: 41.1 us
  starting transfers between devices  15.6 us (38%)
  blocking collectives  11.5 us (28%)
  Pallas kernels  7.13 us (17%)
  local copies, waits for them, and re-layouts  1.88 us (5%)
  waiting for transfers between devices  1.58 us (4%)
  matrix products  1.31 us (3%)
  between operations  1.13 us (3%)
  other arithmetic  0.98 us (2%)
    ppermute x9, starting transfers between devices, sent(): lax.ppermute(value, 'edge', [(a, b) for a, b in pairs if 0 <= a < count a...  15.6 us
    all_to_all x1, blocking collectives, on_device(): sums = jnp.sum(lax.all_to_all(sums, 'edge', 0, 0, tiled=True), 0)  11.5 us
    pallas_call x1, Pallas kernels, on_device(): pl.pallas_call(functools.partial(edge_kernel, batch), out_shape=(jax.Shap...  7.13 us
    ppermute x9, waiting for transfers between devices, sent(): lax.ppermute(value, 'edge', [(a, b) for a, b in pairs if 0 <= a < count a...  1.58 us
    dot_general x1, matrix products, corr_weights(): wide = jnp.dot(picks, w_corr).reshape(ROWS, SHARE, PIX, -1)  1.31 us
    rev x1, local copies, waits for them, and re-layouts, on_device(): features.reshape(frames_here, ROWS, WIDTH, chans)[:, :, ::-1]  1 us
  transfers between devices with their start and end apart: 9, of which 3 were waited for; matrix products, arithmetic and copies ran while one was open for 5% of the time, Pallas kernels for 0%

profile of v4, /device:TPU:0, one launch (start us, length us, event | category | flops | bytes accessed | tf_op | source)
XLA Modules:
  0.0 41.1 jit_solution(6882197650275885139)
XLA Ops:
  0.6 0.0 copy-start
  0.7 1.0 %rev.3 = bf16[2,4,64,128]{3,2,1,0:T(8,128)(2,1)S(1)} reverse(bf16[2,4,64,128]{3,2,1,0:T(8,128)(2,1)} %bitcast.47), dimensions={2} | reverse | bytes 262144 | tf_op jit(solution)/shard_map/rev | solution.py:204
  1.7 3.0 %collective-permute-start = (bf16[2,256,128]{2,1,0:T(8,128)(2,1)S(1)}, bf16[2,256,128]{2,1,0:T(8,128)(2,1)S(1)}, u32[]{:S(2)}, u32[]{:S(2)}) collective-permute-start(bf16[2,256,128]{2,1,0:T(8,128)(2,1)S(1)} %bitcast.50), channel_id=1, source_target_pairs={{0,2},{1,3},{4,6},{5,7},{8,10},{9,11},{12,14},{13,15},{2,0},{3,1},... | collective-permute-start | bytes 393224 | tf_op jit(solution)/shard_map/ppermute | solution.py:23
  4.7 0.7 %collective-permute-start.3 = (bf16[2,256,128]{2,1,0:T(8,128)(2,1)S(1)}, bf16[2,256,128]{2,1,0:T(8,128)(2,1)S(1)}, u32[]{:S(2)}, u32[]{:S(2)}) collective-permute-start(bf16[2,256,128]{2,1,0:T(8,128)(2,1)S(1)} %bitcast.51), channel_id=1, source_target_pairs={{2,8},{3,11},{6,12},{7,15},{8,2},{9,1},{12,6},{13,5},{18,24},{19,2... | collective-permute-start | bytes 393224 | tf_op jit(solution)/shard_map/ppermute | solution.py:23
  5.4 1.3 %fusion.8 = bf16[2048,128]{1,0:T(8,128)(2,1)S(1)} fusion(bf16[2048,49]{1,0:T(8,128)(2,1)} %constant.100.clone, bf16[49,128]{1,0:T(8,128)(2,1)S(1)} %copy-done), kind=kOutput, calls=%fused_computation.83 | convolution fusion | flops 25690112 | bytes 737536 | tf_op jit(solution)/shard_map/dot_general | solution.py:68
  6.7 0.0 copy-start.6
  7.0 0.0 copy-start.4
  7.1 0.4 copy-done.6
  7.5 0.1 pad_maximum_fusion.w_conv_ref
  7.7 0.0 copy-done.4
  7.7 0.4 %collective-permute-done = bf16[2,256,128]{2,1,0:T(8,128)(2,1)S(1)} collective-permute-done((bf16[2,256,128]{2,1,0:T(8,128)(2,1)S(1)}, bf16[2,256,128]{2,1,0:T(8,128)(2,1)S(1)}, u32[]{:S(2)}, u32[]{:S(2)}) %collective-permute-start) | collective-permute-done | bytes 131104 | tf_op jit(solution)/shard_map/ppermute | solution.py:23
  8.2 1.9 %collective-permute-start.1 = (bf16[4,256,128]{2,1,0:T(8,128)(2,1)S(1)}, bf16[4,256,128]{2,1,0:T(8,128)(2,1)S(1)}, u32[]{:S(2)}, u32[]{:S(2)}) collective-permute-start(bf16[4,256,128]{2,1,0:T(8,128)(2,1)S(1)} %pad_maximum_fusion.2), channel_id=1, source_target_pairs={{0,4},{1,5},{2,6},{3,7},{8,12},{9,13},{10,14},{11,15},{4,0},{5,1},... | collective-permute-start | bytes 786440 | tf_op jit(solution)/shard_map/ppermute | solution.py:23
  10.1 0.1 pad_maximum_fusion.1.w_corr_ref
  10.2 0.0 copy-start.1
  10.2 0.0 copy-start.2
  10.2 0.0 copy-start.3
  10.2 0.0 copy-start.5
  10.2 0.8 %collective-permute-start.2 = (bf16[4,256,128]{2,1,0:T(8,128)(2,1)S(1)}, bf16[4,256,128]{2,1,0:T(8,128)(2,1)S(1)}, u32[]{:S(2)}, u32[]{:S(2)}) collective-permute-start(bf16[4,256,128]{2,1,0:T(8,128)(2,1)S(1)} %pad_maximum_fusion.2), channel_id=1, source_target_pairs={{4,8},{5,9},{6,10},{7,11},{8,4},{9,5},{10,6},{11,7},{20,24},{21,25... | collective-permute-start | bytes 786440 | tf_op jit(solution)/shard_map/ppermute | solution.py:23
  11.0 0.7 %collective-permute-start.4 = (bf16[2,256,128]{2,1,0:T(8,128)(2,1)S(1)}, bf16[2,256,128]{2,1,0:T(8,128)(2,1)S(1)}, u32[]{:S(2)}, u32[]{:S(2)}) collective-permute-start(bf16[2,256,128]{2,1,0:T(8,128)(2,1)S(1)} %collective-permute-done.3), channel_id=1, source_target_pairs={{0,0},{1,3},{2,2},{3,1},{4,4},{5,7},{6,6},{7,5},{8,8},{9,11},{10,1... | collective-permute-start | bytes 393224 | tf_op jit(solution)/shard_map/ppermute | solution.py:23
  11.7 4.3 %collective-permute-start.5 = (bf16[4,256,128]{2,1,0:T(8,128)(2,1)S(1)}, bf16[4,256,128]{2,1,0:T(8,128)(2,1)S(1)}, u32[]{:S(2)}, u32[]{:S(2)}) collective-permute-start(bf16[4,256,128]{2,1,0:T(8,128)(2,1)S(1)} %pad_maximum_fusion.2), channel_id=1, source_target_pairs={{0,1},{2,3},{4,5},{6,7},{8,9},{10,11},{12,13},{14,15},{1,0},{3,2},... | collective-permute-start | bytes 786440 | tf_op jit(solution)/shard_map/ppermute | solution.py:23
  16.1 0.0 collective-permute-done.4
  16.1 3.7 %collective-permute-start.8 = (bf16[2,256,128]{2,1,0:T(8,128)(2,1)S(1)}, bf16[2,256,128]{2,1,0:T(8,128)(2,1)S(1)}, u32[]{:S(2)}, u32[]{:S(2)}) collective-permute-start(bf16[2,256,128]{2,1,0:T(8,128)(2,1)S(1)} %collective-permute-done.4), channel_id=1, source_target_pairs={{0,1},{2,3},{4,5},{6,7},{8,9},{10,11},{12,13},{14,15},{1,0},{3,2},... | collective-permute-start | bytes 393224 | tf_op jit(solution)/shard_map/ppermute | solution.py:23
  19.8 0.0 collective-permute-start.6
  19.8 0.0 collective-permute-done.2
  19.8 0.6 %collective-permute-start.7 = (bf16[4,256,128]{2,1,0:T(8,128)(2,1)S(1)}, bf16[4,256,128]{2,1,0:T(8,128)(2,1)S(1)}, u32[]{:S(2)}, u32[]{:S(2)}) collective-permute-start(bf16[4,256,128]{2,1,0:T(8,128)(2,1)S(1)} %collective-permute-done.2), channel_id=1, source_target_pairs={{0,1},{2,3},{4,5},{6,7},{8,9},{10,11},{12,13},{14,15},{1,0},{3,2},... | collective-permute-start | bytes 786440 | tf_op jit(solution)/shard_map/ppermute | solution.py:23
  20.5 0.8 %collective-permute-done.6 = bf16[4,256,128]{2,1,0:T(8,128)(2,1)S(1)} collective-permute-done((bf16[4,256,128]{2,1,0:T(8,128)(2,1)S(1)}, bf16[4,256,128]{2,1,0:T(8,128)(2,1)S(1)}, u32[]{:S(2)}, u32[]{:S(2)}) %collective-permute-start.6) | collective-permute-done | bytes 262176 | tf_op jit(solution)/shard_map/ppermute | solution.py:23
  21.3 0.3 collective-permute-done.7
  21.8 0.0 copy-start.9
  21.8 0.0 copy-start.10
  21.8 7.1 %edge_update.1 = (bf16[24,256,128]{2,1,0:T(8,128)(2,1)}, f32[32,2,256]{2,1,0:T(2,128)S(1)}) custom-call(s32[2,12]{1,0:T(2,128)S(1)} %fusion.4.index_ref, s32[2,12]{1,0:T(2,128)S(1)} %copy-done.4, bf16[2,256,128]{2,1,0:T(8,128)(2,1)S(1)} %copy-done.2, bf16[2,256,128]{2,1,0:T(8,128)(2,1)S(1)} %copy-done.3, bf16[24,256,128]{2,1,0:T(8,128)(2,1)S(1)} %bitcast.46, ...), custom_call_target="tpu_custom_call" | custom-call | tf_op jit(solution)/shard_map/edge_update/pallas_call | solution.py:212
  28.9 11.5 %all_to_all.5 = f32[16,2,2,256]{3,2,1,0:T(2,128)S(1)} all-to-all(f32[16,2,2,256]{3,2,1,0:T(2,128)S(1)} %bitcast.48), channel_id=1, replica_groups=mesh['groups'=2,'edge'=16] {'edge'}, dimensions={0} | all-to-all | bytes 131072 | tf_op jit(solution)/shard_map/all_to_all | solution.py:233
  40.5 0.6 %fusion.1 = f32[2,256]{1,0:T(2,128)} fusion(f32[2,256]{1,0:T(2,128)S(1)} %copy-done.9, f32[2,1,256]{2,1,0:T(1,128)S(1)} %get-tuple-element.32, f32[2,256]{1,0:T(2,128)S(1)} %copy-done.10, f32[2,1,256]{2,1,0:T(1,128)S(1)} %get-tuple-element.31), kind=kLoop, calls=%fused_computation.56 | loop fusion | flops 1536 | bytes 10240 | tf_op jit(solution)/shard_map/add | solution.py:234
  (45 shorter events, 0.6 us)
Async XLA Ops:
  0.6 4.8 %copy-start = (bf16[49,128]{1,0:T(8,128)(2,1)S(1)}, bf16[49,128]{1,0:T(8,128)(2,1)}, u32[]{:S(2)}) copy-start(bf16[49,128]{1,0:T(8,128)(2,1)} %param.18) | copy-start | bytes 37636
  0.6 6.1 %copy-start.8 = (bf16[256,256]{1,0:T(8,128)(2,1)S(1)}, bf16[256,256]{1,0:T(8,128)(2,1)}, u32[]{:S(2)}) copy-start(bf16[256,256]{1,0:T(8,128)(2,1)} %param.19) | copy-start | bytes 393220
  0.7 6.1 %copy-start.7 = (bf16[9,128,128]{2,1,0:T(8,128)(2,1)S(1)}, bf16[9,128,128]{2,1,0:T(8,128)(2,1)}, u32[]{:S(2)}) copy-start(bf16[9,128,128]{2,1,0:T(8,128)(2,1)} %param.20) | copy-start | bytes 884740
  1.7 6.5 %collective-permute-start = (bf16[2,256,128]{2,1,0:T(8,128)(2,1)S(1)}, bf16[2,256,128]{2,1,0:T(8,128)(2,1)S(1)}, u32[]{:S(2)}, u32[]{:S(2)}) collective-permute-start(bf16[2,256,128]{2,1,0:T(8,128)(2,1)S(1)} %bitcast.50), channel_id=1, source_target_pairs={{0,2},{1,3},{4,6},{5,7},{8,10},{9,11},{12,14},{13,15},{2,0},{3,1},... | collective-permute-start | bytes 393224 | tf_op jit(solution)/shard_map/ppermute | solution.py:23
  4.7 6.3 %collective-permute-start.3 = (bf16[2,256,128]{2,1,0:T(8,128)(2,1)S(1)}, bf16[2,256,128]{2,1,0:T(8,128)(2,1)S(1)}, u32[]{:S(2)}, u32[]{:S(2)}) collective-permute-start(bf16[2,256,128]{2,1,0:T(8,128)(2,1)S(1)} %bitcast.51), channel_id=1, source_target_pairs={{2,8},{3,11},{6,12},{7,15},{8,2},{9,1},{12,6},{13,5},{18,24},{19,2... | collective-permute-start | bytes 393224 | tf_op jit(solution)/shard_map/ppermute | solution.py:23
  6.7 0.8 %copy-start.6 = (bf16[128,128]{1,0:T(8,128)(2,1)S(1)}, bf16[128,128]{1,0:T(8,128)(2,1)}, u32[]{:S(2)}) copy-start(bf16[128,128]{1,0:T(8,128)(2,1)} %param.21) | copy-start | bytes 98308
  7.0 0.7 %copy-start.4 = (s32[2,12]{1,0:T(2,128)S(1)}, s32[2,12]{1,0:T(2,128)}, u32[]{:S(2)}) copy-start(s32[2,12]{1,0:T(2,128)} %target_ref.1) | copy-start | bytes 292
  8.2 11.6 %collective-permute-start.1 = (bf16[4,256,128]{2,1,0:T(8,128)(2,1)S(1)}, bf16[4,256,128]{2,1,0:T(8,128)(2,1)S(1)}, u32[]{:S(2)}, u32[]{:S(2)}) collective-permute-start(bf16[4,256,128]{2,1,0:T(8,128)(2,1)S(1)} %pad_maximum_fusion.2), channel_id=1, source_target_pairs={{0,4},{1,5},{2,6},{3,7},{8,12},{9,13},{10,14},{11,15},{4,0},{5,1},... | collective-permute-start | bytes 786440 | tf_op jit(solution)/shard_map/ppermute | solution.py:23
  10.2 11.6 %copy-start.1 = (bf16[2,12,256,128]{3,2,1,0:T(8,128)(2,1)S(1)}, bf16[2,12,256,128]{3,2,1,0:T(8,128)(2,1)}, u32[]{:S(2)}) copy-start(bf16[2,12,256,128]{3,2,1,0:T(8,128)(2,1)} %param.14) | copy-start | bytes 4718596
  10.2 11.6 %copy-start.2 = (bf16[2,256,128]{2,1,0:T(8,128)(2,1)S(1)}, bf16[2,256,128]{2,1,0:T(8,128)(2,1)}, u32[]{:S(2)}) copy-start(bf16[2,256,128]{2,1,0:T(8,128)(2,1)} %feat_ref.1) | copy-start | bytes 393220
  10.2 11.6 %copy-start.3 = (bf16[2,256,128]{2,1,0:T(8,128)(2,1)S(1)}, bf16[2,256,128]{2,1,0:T(8,128)(2,1)}, u32[]{:S(2)}) copy-start(bf16[2,256,128]{2,1,0:T(8,128)(2,1)} %ctx_ref.1) | copy-start | bytes 393220
  10.2 11.6 %copy-start.5 = (bf16[2,128]{1,0:T(2,128)(2,1)S(1)}, bf16[2,128]{1,0:T(2,128)(2,1)}, u32[]{:S(2)}) copy-start(bf16[2,128]{1,0:T(2,128)(2,1)} %w_heads_ref.1) | copy-start | bytes 1540
  10.2 9.6 %collective-permute-start.2 = (bf16[4,256,128]{2,1,0:T(8,128)(2,1)S(1)}, bf16[4,256,128]{2,1,0:T(8,128)(2,1)S(1)}, u32[]{:S(2)}, u32[]{:S(2)}) collective-permute-start(bf16[4,256,128]{2,1,0:T(8,128)(2,1)S(1)} %pad_maximum_fusion.2), channel_id=1, source_target_pairs={{4,8},{5,9},{6,10},{7,11},{8,4},{9,5},{10,6},{11,7},{20,24},{21,25... | collective-permute-start | bytes 786440 | tf_op jit(solution)/shard_map/ppermute | solution.py:23
  11.0 5.0 %collective-permute-start.4 = (bf16[2,256,128]{2,1,0:T(8,128)(2,1)S(1)}, bf16[2,256,128]{2,1,0:T(8,128)(2,1)S(1)}, u32[]{:S(2)}, u32[]{:S(2)}) collective-permute-start(bf16[2,256,128]{2,1,0:T(8,128)(2,1)S(1)} %collective-permute-done.3), channel_id=1, source_target_pairs={{0,0},{1,3},{2,2},{3,1},{4,4},{5,7},{6,6},{7,5},{8,8},{9,11},{10,1... | collective-permute-start | bytes 393224 | tf_op jit(solution)/shard_map/ppermute | solution.py:23
  11.7 8.7 %collective-permute-start.5 = (bf16[4,256,128]{2,1,0:T(8,128)(2,1)S(1)}, bf16[4,256,128]{2,1,0:T(8,128)(2,1)S(1)}, u32[]{:S(2)}, u32[]{:S(2)}) collective-permute-start(bf16[4,256,128]{2,1,0:T(8,128)(2,1)S(1)} %pad_maximum_fusion.2), channel_id=1, source_target_pairs={{0,1},{2,3},{4,5},{6,7},{8,9},{10,11},{12,13},{14,15},{1,0},{3,2},... | collective-permute-start | bytes 786440 | tf_op jit(solution)/shard_map/ppermute | solution.py:23
  16.1 5.6 %collective-permute-start.8 = (bf16[2,256,128]{2,1,0:T(8,128)(2,1)S(1)}, bf16[2,256,128]{2,1,0:T(8,128)(2,1)S(1)}, u32[]{:S(2)}, u32[]{:S(2)}) collective-permute-start(bf16[2,256,128]{2,1,0:T(8,128)(2,1)S(1)} %collective-permute-done.4), channel_id=1, source_target_pairs={{0,1},{2,3},{4,5},{6,7},{8,9},{10,11},{12,13},{14,15},{1,0},{3,2},... | collective-permute-start | bytes 393224 | tf_op jit(solution)/shard_map/ppermute | solution.py:23
  19.8 1.5 %collective-permute-start.6 = (bf16[4,256,128]{2,1,0:T(8,128)(2,1)S(1)}, bf16[4,256,128]{2,1,0:T(8,128)(2,1)S(1)}, u32[]{:S(2)}, u32[]{:S(2)}) collective-permute-start(bf16[4,256,128]{2,1,0:T(8,128)(2,1)S(1)} %collective-permute-done.1), channel_id=1, source_target_pairs={{0,1},{2,3},{4,5},{6,7},{8,9},{10,11},{12,13},{14,15},{1,0},{3,2},... | collective-permute-start | bytes 786440 | tf_op jit(solution)/shard_map/ppermute | solution.py:23
  19.8 1.9 %collective-permute-start.7 = (bf16[4,256,128]{2,1,0:T(8,128)(2,1)S(1)}, bf16[4,256,128]{2,1,0:T(8,128)(2,1)S(1)}, u32[]{:S(2)}, u32[]{:S(2)}) collective-permute-start(bf16[4,256,128]{2,1,0:T(8,128)(2,1)S(1)} %collective-permute-done.2), channel_id=1, source_target_pairs={{0,1},{2,3},{4,5},{6,7},{8,9},{10,11},{12,13},{14,15},{1,0},{3,2},... | collective-permute-start | bytes 786440 | tf_op jit(solution)/shard_map/ppermute | solution.py:23
  21.8 18.7 %copy-start.9 = (f32[2,256]{1,0:T(2,128)S(1)}, f32[2,256]{1,0:T(2,128)}, u32[]{:S(2)}) copy-start(f32[2,256]{1,0:T(2,128)} %param.16) | copy-start | bytes 6148
  21.8 18.7 %copy-start.10 = (f32[2,256]{1,0:T(2,128)S(1)}, f32[2,256]{1,0:T(2,128)}, u32[]{:S(2)}) copy-start(f32[2,256]{1,0:T(2,128)} %param.17) | copy-start | bytes 6148

commit v5 on v4

--- a/solution.py
+++ b/solution.py
@@ -14,7 +14,7 @@
 CORR_Y = 3
 WIDTH = 64
 ROWS = 4
-SHARE = 2
+SHARE = 4
 PIX = ROWS * WIDTH
 
 
@@ -53,20 +53,16 @@
     return place + 7 * (block % 2 != own % 2).astype(jnp.int32)
 
 
-def corr_weights(w_corr):
+def corr_picks():
     side = 2 * CORR_X + 1
-    picks = np.zeros((ROWS, SHARE, PIX, (2 * CORR_Y + 1) * side), np.float32)
+    picks = np.zeros((ROWS, PIX, (2 * CORR_Y + 1) * side), np.float32)
     for y in range(ROWS):
         for y2 in range(ROWS):
             for dx in range(-CORR_X, CORR_X + 1):
                 if abs(y2 - y) <= CORR_Y:
-                    for k in range(SHARE):
-                        lane = y2 * WIDTH + WIDTH - 1 - dx + k * (WIDTH // SHARE)
-                        offset = (y2 - y + CORR_Y) * side + dx + CORR_X
-                        picks[y, k, lane % PIX, offset] = 1
-    picks = jnp.asarray(picks.reshape(-1, picks.shape[-1]), jnp.bfloat16)
-    wide = jnp.dot(picks, w_corr).reshape(ROWS, SHARE, PIX, -1)
-    return jnp.concatenate([wide[:, k] for k in range(SHARE)], -1)
+                    lane = (y2 * WIDTH + WIDTH - 1 - dx) % PIX
+                    picks[y, lane, (y2 - y + CORR_Y) * side + dx + CORR_X] = 1
+    return jnp.asarray(picks, jnp.bfloat16)
 
 
 def conv_inputs(pair):
@@ -96,7 +92,7 @@
 
 
 def edge_kernel(
-    batch, index_ref, target_ref, feat_ref, ctx_ref, state_ref, window_ref, w_corr_ref,
+    batch, index_ref, target_ref, feat_ref, ctx_ref, state_ref, window_ref, picks_ref, w_corr_ref,
     w_gates_ref, w_conv_ref, w_heads_ref, new_ref, sums_ref, held_ref, sem
 ):
     chans = feat_ref.shape[-1]
@@ -111,6 +107,23 @@
     for k in range(SHARE):
         target = WIDTH - 1 - (lanes + PIX - k * (WIDTH // SHARE)) % WIDTH
         scales.append(jnp.where(jnp.abs(target - xs) <= CORR_X, inv_root, 0.0).astype(jnp.float32))
+    w_corr = []
+    for y in range(ROWS):
+        base = jnp.dot(picks_ref[y], w_corr_ref[...], preferred_element_type=jnp.float32)
+        base = base.astype(narrow)
+        turns = [(PIX - k * (WIDTH // SHARE)) % PIX for k in range(SHARE)]
+        w_corr.append(jnp.concatenate([jnp.concatenate([base[t:], base[:t]], 0) if t else base for t in turns], 1))
+    w_gates = w_gates_ref[...] * jnp.bfloat16(0.5)
+    heads_wide = w_heads_ref[...].astype(jnp.float32)
+    blank = jnp.zeros_like(heads_wide[:1])
+    w_heads = jnp.concatenate(
+        [
+            jnp.concatenate([heads_wide[r : r + 1] if p == j else blank for p in range(2)], 1)
+            for r in range(2)
+            for j in range(2)
+        ],
+        0,
+    ).astype(narrow)
     cols = lax.broadcasted_iota(jnp.int32, (WIDTH, chans), 0)
     has_left = jnp.concatenate([cols > 0] * batch, 0)
     has_right = jnp.concatenate([cols < WIDTH - 1] * batch, 0)
@@ -138,7 +151,7 @@
                 bands = sum(scores[i + k * quarter][row] * scales[k] for k in range(SHARE))
                 shared.append(pltpu.roll(bands, 0, 1, stride=1, stride_axis=0).astype(narrow))
             encoded = jnp.dot(
-                jnp.concatenate(shared, 0), w_corr_ref[y], preferred_element_type=jnp.float32
+                jnp.concatenate(shared, 0), w_corr[y], preferred_element_type=jnp.float32
             )
             encoded = jnp.concatenate(
                 [encoded[:, k * chans : (k + 1) * chans] for k in range(SHARE)], 0
@@ -149,7 +162,7 @@
         for y in range(ROWS):
             gates = jnp.tanh(
                 jnp.dot(
-                    jnp.concatenate([hidden[y], motion[y]], 1), w_gates_ref[...],
+                    jnp.concatenate([hidden[y], motion[y]], 1), w_gates,
                     preferred_element_type=jnp.float32,
                 )
             )
@@ -181,16 +194,22 @@
                 )
             )
             copies[-1].start()
-        for i, e in enumerate(these):
-            mine = jnp.concatenate([n[i * WIDTH : (i + 1) * WIDTH] for n in done], 0)
+        for i in range(0, batch, 2):
+            mine = [
+                jnp.concatenate([n[j * WIDTH : (j + 1) * WIDTH] for n in done], 0)
+                for j in (i, i + 1)
+            ]
             heads = lax.dot_general(
-                w_heads_ref[...], mine, (((1,), (1,)), ((), ())),
+                w_heads, jnp.concatenate(mine, 1), (((1,), (1,)), ((), ())),
                 preferred_element_type=jnp.float32,
             )
-            confidence = 0.5 + 0.5 * jnp.tanh(0.5 * heads[1:2])
-            sums_ref[target_ref[e // neigh, e % neigh]] += jnp.concatenate(
-                [confidence * heads[0:1], confidence], 0
-            )
+            confidence = 0.5 + 0.5 * jnp.tanh(0.5 * heads[2:4])
+            pushed = confidence * heads[0:2]
+            for j in range(2):
+                e = start + i + j
+                sums_ref[target_ref[e // neigh, e % neigh]] += jnp.concatenate(
+                    [pushed[j : j + 1], confidence[j : j + 1]], 0
+                )
     for copy in copies:
         copy.wait()
 
@@ -215,7 +234,7 @@
             jax.ShapeDtypeStruct((edges, pixels, chans), states.dtype),
             jax.ShapeDtypeStruct((frames_all, 2, pixels), jnp.float32),
         ),
-        in_specs=[smem, smem] + [vmem] * 8,
+        in_specs=[smem, smem] + [vmem] * 9,
         out_specs=[pl.BlockSpec(memory_space=pl.ANY), vmem],
         scratch_shapes=[
             pltpu.VMEM((edges, pixels, chans), states.dtype),
@@ -225,7 +244,7 @@
         name="edge_update",
     )(
         local_index, neighbours, features, context, states.reshape(edges, pixels, chans),
-        window, corr_weights(w_corr), w_gates * jnp.bfloat16(0.5),
+        window, corr_picks(), w_corr, w_gates,
         conv_weights(w_cand, w_motion), w_heads,
     )
     new_states = new_states.reshape(states.shape)

time: 41.5 us -> 41.1 us (level)
  matrix products: 1.31 us -> 0 us
  waiting for transfers between devices: 1.58 us -> 2.56 us
  starting transfers between devices: 15.6 us -> 15 us
    dot_general x1 -> x0, matrix products: 1.31 us -> none  [corr_weights(): wide = jnp.dot(picks, w_corr).reshape(ROWS, SHARE, PIX, -1)]
    ppermute x9, waiting for transfers between devices: 1.58 us -> 2.56 us  [sent(): lax.ppermute(value, 'edge', [(a, b) for a, b in pairs if 0 <= a < count a...]
    squeeze x1, local copies, waits for them, and re-layouts: 0.02 us -> 0.91 us  [conv_weights(): w_cand[3 * (r - y + 1) + dx]]
    ppermute x9, starting transfers between devices: 15.6 us -> 15 us  [sent(): lax.ppermute(value, 'edge', [(a, b) for a, b in pairs if 0 <= a < count a...]
  transfers between devices with their start and end apart: 9 -> 9, of which waited for: 3 -> 3; matrix products, arithmetic and copies ran while one was open for 5% -> 4% of each run, Pallas kernels for 0% -> 0%
where the time goes in v5:
time: 41.1 us; the launch traced here: 40.8 us
  starting transfers between devices  15 us (36%)
  blocking collectives  11.9 us (29%)
  Pallas kernels  7.05 us (17%)
  waiting for transfers between devices  2.56 us (6%)
  local copies, waits for them, and re-layouts  2.29 us (6%)
  between operations  1.09 us (3%)
  other arithmetic  0.9 us (2%)
    ppermute x9, starting transfers between devices, sent(): lax.ppermute(value, 'edge', [(a, b) for a, b in pairs if 0 <= a < count a...  15 us
    all_to_all x1, blocking collectives, on_device(): sums = jnp.sum(lax.all_to_all(sums, 'edge', 0, 0, tiled=True), 0)  11.9 us
    pallas_call x1, Pallas kernels, on_device(): pl.pallas_call(functools.partial(edge_kernel, batch), out_shape=(jax.Shap...  7.05 us
    ppermute x9, waiting for transfers between devices, sent(): lax.ppermute(value, 'edge', [(a, b) for a, b in pairs if 0 <= a < count a...  2.56 us
    rev x1, local copies, waits for them, and re-layouts, on_device(): features.reshape(frames_here, ROWS, WIDTH, chans)[:, :, ::-1]  0.95 us
    squeeze x1, local copies, waits for them, and re-layouts, conv_weights(): w_cand[3 * (r - y + 1) + dx]  0.91 us
  transfers between devices with their start and end apart: 9, of which 3 were waited for; matrix products, arithmetic and copies ran while one was open for 4% of the time, Pallas kernels for 0%

profile of v5, /device:TPU:0, one launch (start us, length us, event | category | flops | bytes accessed | tf_op | source)
XLA Modules:
  0.0 40.8 jit_solution(12961309214976324823)
XLA Ops:
  0.6 1.0 %rev.3 = bf16[2,4,64,128]{3,2,1,0:T(8,128)(2,1)S(1)} reverse(bf16[2,4,64,128]{3,2,1,0:T(8,128)(2,1)} %bitcast.36), dimensions={2} | reverse | bytes 262144 | tf_op jit(solution)/shard_map/rev | solution.py:223
  1.6 3.0 %collective-permute-start = (bf16[2,256,128]{2,1,0:T(8,128)(2,1)S(1)}, bf16[2,256,128]{2,1,0:T(8,128)(2,1)S(1)}, u32[]{:S(2)}, u32[]{:S(2)}) collective-permute-start(bf16[2,256,128]{2,1,0:T(8,128)(2,1)S(1)} %bitcast.38), channel_id=1, source_target_pairs={{0,2},{1,3},{4,6},{5,7},{8,10},{9,11},{12,14},{13,15},{2,0},{3,1},... | collective-permute-start | bytes 393224 | tf_op jit(solution)/shard_map/ppermute | solution.py:23
  4.6 0.7 %collective-permute-start.3 = (bf16[2,256,128]{2,1,0:T(8,128)(2,1)S(1)}, bf16[2,256,128]{2,1,0:T(8,128)(2,1)S(1)}, u32[]{:S(2)}, u32[]{:S(2)}) collective-permute-start(bf16[2,256,128]{2,1,0:T(8,128)(2,1)S(1)} %bitcast.39), channel_id=1, source_target_pairs={{2,8},{3,11},{6,12},{7,15},{8,2},{9,1},{12,6},{13,5},{18,24},{19,2... | collective-permute-start | bytes 393224 | tf_op jit(solution)/shard_map/ppermute | solution.py:23
  5.3 0.9 %slice_bitcast_fusion = (bf16[128,128]{1,0:T(8,128)(2,1)S(1)}, bf16[128,128]{1,0:T(8,128)(2,1)S(1)}, bf16[128,128]{1,0:T(8,128)(2,1)S(1)}, bf16[128,128]{1,0:T(8...) fusion(bf16[9,128,128]{2,1,0:T(8,128)(2,1)} %param.20), kind=kLoop, calls=%fused_computation.39 | loop fusion | bytes 589824 | tf_op jit(solution)/shard_map/squeeze | solution.py:82
  6.5 0.0 copy-start.6
  6.5 0.1 pad_maximum_fusion.w_conv_ref
  6.7 1.4 %collective-permute-done = bf16[2,256,128]{2,1,0:T(8,128)(2,1)S(1)} collective-permute-done((bf16[2,256,128]{2,1,0:T(8,128)(2,1)S(1)}, bf16[2,256,128]{2,1,0:T(8,128)(2,1)S(1)}, u32[]{:S(2)}, u32[]{:S(2)}) %collective-permute-start) | collective-permute-done | bytes 131104 | tf_op jit(solution)/shard_map/ppermute | solution.py:23
  8.1 1.9 %collective-permute-start.1 = (bf16[4,256,128]{2,1,0:T(8,128)(2,1)S(1)}, bf16[4,256,128]{2,1,0:T(8,128)(2,1)S(1)}, u32[]{:S(2)}, u32[]{:S(2)}) collective-permute-start(bf16[4,256,128]{2,1,0:T(8,128)(2,1)S(1)} %pad_maximum_fusion.1), channel_id=1, source_target_pairs={{0,4},{1,5},{2,6},{3,7},{8,12},{9,13},{10,14},{11,15},{4,0},{5,1},... | collective-permute-start | bytes 786440 | tf_op jit(solution)/shard_map/ppermute | solution.py:23
  10.1 0.0 copy-start
  10.1 0.0 copy-start.1
  10.1 0.0 copy-start.2
  10.1 0.0 copy-start.3
  10.1 0.0 copy-start.4
  10.1 0.0 copy-start.5
  10.1 0.0 copy-start.7
  10.1 0.8 %collective-permute-start.2 = (bf16[4,256,128]{2,1,0:T(8,128)(2,1)S(1)}, bf16[4,256,128]{2,1,0:T(8,128)(2,1)S(1)}, u32[]{:S(2)}, u32[]{:S(2)}) collective-permute-start(bf16[4,256,128]{2,1,0:T(8,128)(2,1)S(1)} %pad_maximum_fusion.1), channel_id=1, source_target_pairs={{4,8},{5,9},{6,10},{7,11},{8,4},{9,5},{10,6},{11,7},{20,24},{21,25... | collective-permute-start | bytes 786440 | tf_op jit(solution)/shard_map/ppermute | solution.py:23
  11.0 0.0 collective-permute-done.3
  11.0 0.7 %collective-permute-start.4 = (bf16[2,256,128]{2,1,0:T(8,128)(2,1)S(1)}, bf16[2,256,128]{2,1,0:T(8,128)(2,1)S(1)}, u32[]{:S(2)}, u32[]{:S(2)}) collective-permute-start(bf16[2,256,128]{2,1,0:T(8,128)(2,1)S(1)} %collective-permute-done.3), channel_id=1, source_target_pairs={{0,0},{1,3},{2,2},{3,1},{4,4},{5,7},{6,6},{7,5},{8,8},{9,11},{10,1... | collective-permute-start | bytes 393224 | tf_op jit(solution)/shard_map/ppermute | solution.py:23
  11.7 3.7 %collective-permute-start.5 = (bf16[4,256,128]{2,1,0:T(8,128)(2,1)S(1)}, bf16[4,256,128]{2,1,0:T(8,128)(2,1)S(1)}, u32[]{:S(2)}, u32[]{:S(2)}) collective-permute-start(bf16[4,256,128]{2,1,0:T(8,128)(2,1)S(1)} %pad_maximum_fusion.1), channel_id=1, source_target_pairs={{0,1},{2,3},{4,5},{6,7},{8,9},{10,11},{12,13},{14,15},{1,0},{3,2},... | collective-permute-start | bytes 786440 | tf_op jit(solution)/shard_map/ppermute | solution.py:23
  15.4 0.0 collective-permute-done.4
  15.4 3.7 %collective-permute-start.8 = (bf16[2,256,128]{2,1,0:T(8,128)(2,1)S(1)}, bf16[2,256,128]{2,1,0:T(8,128)(2,1)S(1)}, u32[]{:S(2)}, u32[]{:S(2)}) collective-permute-start(bf16[2,256,128]{2,1,0:T(8,128)(2,1)S(1)} %collective-permute-done.4), channel_id=1, source_target_pairs={{0,1},{2,3},{4,5},{6,7},{8,9},{10,11},{12,13},{14,15},{1,0},{3,2},... | collective-permute-start | bytes 393224 | tf_op jit(solution)/shard_map/ppermute | solution.py:23
  19.1 0.0 collective-permute-done.1
  19.1 0.0 collective-permute-start.6
  19.2 0.6 %collective-permute-start.7 = (bf16[4,256,128]{2,1,0:T(8,128)(2,1)S(1)}, bf16[4,256,128]{2,1,0:T(8,128)(2,1)S(1)}, u32[]{:S(2)}, u32[]{:S(2)}) collective-permute-start(bf16[4,256,128]{2,1,0:T(8,128)(2,1)S(1)} %collective-permute-done.2), channel_id=1, source_target_pairs={{0,1},{2,3},{4,5},{6,7},{8,9},{10,11},{12,13},{14,15},{1,0},{3,2},... | collective-permute-start | bytes 786440 | tf_op jit(solution)/shard_map/ppermute | solution.py:23
  19.8 0.8 %collective-permute-done.6 = bf16[4,256,128]{2,1,0:T(8,128)(2,1)S(1)} collective-permute-done((bf16[4,256,128]{2,1,0:T(8,128)(2,1)S(1)}, bf16[4,256,128]{2,1,0:T(8,128)(2,1)S(1)}, u32[]{:S(2)}, u32[]{:S(2)}) %collective-permute-start.6) | collective-permute-done | bytes 262176 | tf_op jit(solution)/shard_map/ppermute | solution.py:23
  20.7 0.3 collective-permute-done.7
  21.0 0.0 collective-permute-done.8
  21.2 0.0 copy-start.9
  21.2 0.0 copy-start.10
  21.2 7.1 %edge_update.1 = (bf16[24,256,128]{2,1,0:T(8,128)(2,1)}, f32[32,2,256]{2,1,0:T(2,128)S(1)}) custom-call(s32[2,12]{1,0:T(2,128)S(1)} %fusion.4.index_ref, s32[2,12]{1,0:T(2,128)S(1)} %copy-done.6, bf16[2,256,128]{2,1,0:T(8,128)(2,1)S(1)} %copy-done.1, bf16[2,256,128]{2,1,0:T(8,128)(2,1)S(1)} %copy-done.3, bf16[24,256,128]{2,1,0:T(8,128)(2,1)S(1)} %bitcast.35, ...), custom_call_target="tpu_custom_call" | custom-call | tf_op jit(solution)/shard_map/edge_update/pallas_call | solution.py:231
  28.2 11.9 %all_to_all.5 = f32[16,2,2,256]{3,2,1,0:T(2,128)S(1)} all-to-all(f32[16,2,2,256]{3,2,1,0:T(2,128)S(1)} %bitcast.37), channel_id=1, replica_groups=mesh['groups'=2,'edge'=16] {'edge'}, dimensions={0} | all-to-all | bytes 131072 | tf_op jit(solution)/shard_map/all_to_all | solution.py:252
  40.2 0.6 %fusion.1 = f32[2,256]{1,0:T(2,128)} fusion(f32[2,256]{1,0:T(2,128)S(1)} %copy-done.9, f32[2,1,256]{2,1,0:T(1,128)S(1)} %get-tuple-element.30, f32[2,256]{1,0:T(2,128)S(1)} %copy-done.10, f32[2,1,256]{2,1,0:T(1,128)S(1)} %get-tuple-element.29), kind=kLoop, calls=%fused_computation.52 | loop fusion | flops 1536 | bytes 10240 | tf_op jit(solution)/shard_map/add | solution.py:253
  (41 shorter events, 0.6 us)
Async XLA Ops:
  0.6 5.8 %copy-start.8 = (bf16[128,128]{1,0:T(8,128)(2,1)S(1)}, bf16[128,128]{1,0:T(8,128)(2,1)}, u32[]{:S(2)}) copy-start(bf16[128,128]{1,0:T(8,128)(2,1)} %param.21) | copy-start | bytes 98308
  1.6 6.5 %collective-permute-start = (bf16[2,256,128]{2,1,0:T(8,128)(2,1)S(1)}, bf16[2,256,128]{2,1,0:T(8,128)(2,1)S(1)}, u32[]{:S(2)}, u32[]{:S(2)}) collective-permute-start(bf16[2,256,128]{2,1,0:T(8,128)(2,1)S(1)} %bitcast.38), channel_id=1, source_target_pairs={{0,2},{1,3},{4,6},{5,7},{8,10},{9,11},{12,14},{13,15},{2,0},{3,1},... | collective-permute-start | bytes 393224 | tf_op jit(solution)/shard_map/ppermute | solution.py:23
  4.6 6.4 %collective-permute-start.3 = (bf16[2,256,128]{2,1,0:T(8,128)(2,1)S(1)}, bf16[2,256,128]{2,1,0:T(8,128)(2,1)S(1)}, u32[]{:S(2)}, u32[]{:S(2)}) collective-permute-start(bf16[2,256,128]{2,1,0:T(8,128)(2,1)S(1)} %bitcast.39), channel_id=1, source_target_pairs={{2,8},{3,11},{6,12},{7,15},{8,2},{9,1},{12,6},{13,5},{18,24},{19,2... | collective-permute-start | bytes 393224 | tf_op jit(solution)/shard_map/ppermute | solution.py:23
  6.5 3.6 %copy-start.6 = (s32[2,12]{1,0:T(2,128)S(1)}, s32[2,12]{1,0:T(2,128)}, u32[]{:S(2)}) copy-start(s32[2,12]{1,0:T(2,128)} %target_ref.1) | copy-start | bytes 292
  8.1 11.0 %collective-permute-start.1 = (bf16[4,256,128]{2,1,0:T(8,128)(2,1)S(1)}, bf16[4,256,128]{2,1,0:T(8,128)(2,1)S(1)}, u32[]{:S(2)}, u32[]{:S(2)}) collective-permute-start(bf16[4,256,128]{2,1,0:T(8,128)(2,1)S(1)} %pad_maximum_fusion.1), channel_id=1, source_target_pairs={{0,4},{1,5},{2,6},{3,7},{8,12},{9,13},{10,14},{11,15},{4,0},{5,1},... | collective-permute-start | bytes 786440 | tf_op jit(solution)/shard_map/ppermute | solution.py:23
  10.1 11.0 %copy-start = (bf16[2,12,256,128]{3,2,1,0:T(8,128)(2,1)S(1)}, bf16[2,12,256,128]{3,2,1,0:T(8,128)(2,1)}, u32[]{:S(2)}) copy-start(bf16[2,12,256,128]{3,2,1,0:T(8,128)(2,1)} %param.14) | copy-start | bytes 4718596
  10.1 11.0 %copy-start.1 = (bf16[2,256,128]{2,1,0:T(8,128)(2,1)S(1)}, bf16[2,256,128]{2,1,0:T(8,128)(2,1)}, u32[]{:S(2)}) copy-start(bf16[2,256,128]{2,1,0:T(8,128)(2,1)} %feat_ref.1) | copy-start | bytes 393220
  10.1 11.0 %copy-start.2 = (bf16[4,256,49]{2,1,0:T(8,128)(2,1)S(1)}, bf16[4,256,49]{2,1,0:T(8,128)(2,1)}, u32[]{:S(2)}) copy-start(bf16[4,256,49]{2,1,0:T(8,128)(2,1)} %constant.98.clone.picks_ref) | copy-start | bytes 301060
  10.1 11.0 %copy-start.3 = (bf16[2,256,128]{2,1,0:T(8,128)(2,1)S(1)}, bf16[2,256,128]{2,1,0:T(8,128)(2,1)}, u32[]{:S(2)}) copy-start(bf16[2,256,128]{2,1,0:T(8,128)(2,1)} %ctx_ref.1) | copy-start | bytes 393220
  10.1 11.0 %copy-start.4 = (bf16[256,256]{1,0:T(8,128)(2,1)S(1)}, bf16[256,256]{1,0:T(8,128)(2,1)}, u32[]{:S(2)}) copy-start(bf16[256,256]{1,0:T(8,128)(2,1)} %w_gates_ref.1) | copy-start | bytes 393220
  10.1 11.0 %copy-start.5 = (bf16[49,128]{1,0:T(8,128)(2,1)S(1)}, bf16[49,128]{1,0:T(8,128)(2,1)}, u32[]{:S(2)}) copy-start(bf16[49,128]{1,0:T(8,128)(2,1)} %w_corr_ref.1) | copy-start | bytes 37636
  10.1 11.0 %copy-start.7 = (bf16[2,128]{1,0:T(2,128)(2,1)S(1)}, bf16[2,128]{1,0:T(2,128)(2,1)}, u32[]{:S(2)}) copy-start(bf16[2,128]{1,0:T(2,128)(2,1)} %w_heads_ref.1) | copy-start | bytes 1540
  10.1 9.0 %collective-permute-start.2 = (bf16[4,256,128]{2,1,0:T(8,128)(2,1)S(1)}, bf16[4,256,128]{2,1,0:T(8,128)(2,1)S(1)}, u32[]{:S(2)}, u32[]{:S(2)}) collective-permute-start(bf16[4,256,128]{2,1,0:T(8,128)(2,1)S(1)} %pad_maximum_fusion.1), channel_id=1, source_target_pairs={{4,8},{5,9},{6,10},{7,11},{8,4},{9,5},{10,6},{11,7},{20,24},{21,25... | collective-permute-start | bytes 786440 | tf_op jit(solution)/shard_map/ppermute | solution.py:23
  11.0 4.5 %collective-permute-start.4 = (bf16[2,256,128]{2,1,0:T(8,128)(2,1)S(1)}, bf16[2,256,128]{2,1,0:T(8,128)(2,1)S(1)}, u32[]{:S(2)}, u32[]{:S(2)}) collective-permute-start(bf16[2,256,128]{2,1,0:T(8,128)(2,1)S(1)} %collective-permute-done.3), channel_id=1, source_target_pairs={{0,0},{1,3},{2,2},{3,1},{4,4},{5,7},{6,6},{7,5},{8,8},{9,11},{10,1... | collective-permute-start | bytes 393224 | tf_op jit(solution)/shard_map/ppermute | solution.py:23
  11.7 8.1 %collective-permute-start.5 = (bf16[4,256,128]{2,1,0:T(8,128)(2,1)S(1)}, bf16[4,256,128]{2,1,0:T(8,128)(2,1)S(1)}, u32[]{:S(2)}, u32[]{:S(2)}) collective-permute-start(bf16[4,256,128]{2,1,0:T(8,128)(2,1)S(1)} %pad_maximum_fusion.1), channel_id=1, source_target_pairs={{0,1},{2,3},{4,5},{6,7},{8,9},{10,11},{12,13},{14,15},{1,0},{3,2},... | collective-permute-start | bytes 786440 | tf_op jit(solution)/shard_map/ppermute | solution.py:23
  15.4 5.6 %collective-permute-start.8 = (bf16[2,256,128]{2,1,0:T(8,128)(2,1)S(1)}, bf16[2,256,128]{2,1,0:T(8,128)(2,1)S(1)}, u32[]{:S(2)}, u32[]{:S(2)}) collective-permute-start(bf16[2,256,128]{2,1,0:T(8,128)(2,1)S(1)} %collective-permute-done.4), channel_id=1, source_target_pairs={{0,1},{2,3},{4,5},{6,7},{8,9},{10,11},{12,13},{14,15},{1,0},{3,2},... | collective-permute-start | bytes 393224 | tf_op jit(solution)/shard_map/ppermute | solution.py:23
  19.1 1.5 %collective-permute-start.6 = (bf16[4,256,128]{2,1,0:T(8,128)(2,1)S(1)}, bf16[4,256,128]{2,1,0:T(8,128)(2,1)S(1)}, u32[]{:S(2)}, u32[]{:S(2)}) collective-permute-start(bf16[4,256,128]{2,1,0:T(8,128)(2,1)S(1)} %collective-permute-done.1), channel_id=1, source_target_pairs={{0,1},{2,3},{4,5},{6,7},{8,9},{10,11},{12,13},{14,15},{1,0},{3,2},... | collective-permute-start | bytes 786440 | tf_op jit(solution)/shard_map/ppermute | solution.py:23
  19.2 1.9 %collective-permute-start.7 = (bf16[4,256,128]{2,1,0:T(8,128)(2,1)S(1)}, bf16[4,256,128]{2,1,0:T(8,128)(2,1)S(1)}, u32[]{:S(2)}, u32[]{:S(2)}) collective-permute-start(bf16[4,256,128]{2,1,0:T(8,128)(2,1)S(1)} %collective-permute-done.2), channel_id=1, source_target_pairs={{0,1},{2,3},{4,5},{6,7},{8,9},{10,11},{12,13},{14,15},{1,0},{3,2},... | collective-permute-start | bytes 786440 | tf_op jit(solution)/shard_map/ppermute | solution.py:23
  21.2 19.1 %copy-start.9 = (f32[2,256]{1,0:T(2,128)S(1)}, f32[2,256]{1,0:T(2,128)}, u32[]{:S(2)}) copy-start(f32[2,256]{1,0:T(2,128)} %param.16) | copy-start | bytes 6148
  21.2 19.1 %copy-start.10 = (f32[2,256]{1,0:T(2,128)S(1)}, f32[2,256]{1,0:T(2,128)}, u32[]{:S(2)}) copy-start(f32[2,256]{1,0:T(2,128)} %param.17) | copy-start | bytes 6148

commit v6 on v5

--- a/solution.py
+++ b/solution.py
@@ -130,6 +130,8 @@
     length = batch * WIDTH
     quarter = batch // SHARE
     copies = []
+    finished = []
+    all_scores = {}
     for start in range(0, edges, batch):
         these = list(range(start, start + batch))
         scores = []
@@ -143,6 +145,10 @@
                     (((1,), (1,)), ((), ())), preferred_element_type=jnp.float32,
                 )
             )
+        all_scores[start] = scores
+    for start in range(0, edges, batch):
+        these = list(range(start, start + batch))
+        scores = all_scores[start]
         motion, hidden, update_tanh, reset = [], [], [], []
         for y in range(ROWS):
             row = slice(y * WIDTH, (y + 1) * WIDTH)
@@ -194,6 +200,8 @@
                 )
             )
             copies[-1].start()
+        finished.append((start, done))
+    for start, done in finished:
         for i in range(0, batch, 2):
             mine = [
                 jnp.concatenate([n[j * WIDTH : (j + 1) * WIDTH] for n in done], 0)

time: 41.1 us -> 40.7 us (level)
  no operation moved by 1% of the time
where the time goes in v6:
time: 40.7 us; the launch traced here: 40.4 us
  starting transfers between devices  15 us (37%)
  blocking collectives  11.9 us (29%)
  Pallas kernels  6.67 us (16%)
  waiting for transfers between devices  2.56 us (6%)
  local copies, waits for them, and re-layouts  2.29 us (6%)
  between operations  1.09 us (3%)
  other arithmetic  0.9 us (2%)
    ppermute x9, starting transfers between devices, sent(): lax.ppermute(value, 'edge', [(a, b) for a, b in pairs if 0 <= a < count a...  15 us
    all_to_all x1, blocking collectives, on_device(): sums = jnp.sum(lax.all_to_all(sums, 'edge', 0, 0, tiled=True), 0)  11.9 us
    pallas_call x1, Pallas kernels, on_device(): pl.pallas_call(functools.partial(edge_kernel, batch), out_shape=(jax.Shap...  6.67 us
    ppermute x9, waiting for transfers between devices, sent(): lax.ppermute(value, 'edge', [(a, b) for a, b in pairs if 0 <= a < count a...  2.56 us
    rev x1, local copies, waits for them, and re-layouts, on_device(): features.reshape(frames_here, ROWS, WIDTH, chans)[:, :, ::-1]  0.95 us
    squeeze x1, local copies, waits for them, and re-layouts, conv_weights(): w_cand[3 * (r - y + 1) + dx]  0.91 us
  transfers between devices with their start and end apart: 9, of which 3 were waited for; matrix products, arithmetic and copies ran while one was open for 4% of the time, Pallas kernels for 0%

profile of v6, /device:TPU:0, one launch (start us, length us, event | category | flops | bytes accessed | tf_op | source)
XLA Modules:
  0.0 40.4 jit_solution(5750723198482884243)
XLA Ops:
  0.6 1.0 %rev.3 = bf16[2,4,64,128]{3,2,1,0:T(8,128)(2,1)S(1)} reverse(bf16[2,4,64,128]{3,2,1,0:T(8,128)(2,1)} %bitcast.36), dimensions={2} | reverse | bytes 262144 | tf_op jit(solution)/shard_map/rev | solution.py:231
  1.6 3.0 %collective-permute-start = (bf16[2,256,128]{2,1,0:T(8,128)(2,1)S(1)}, bf16[2,256,128]{2,1,0:T(8,128)(2,1)S(1)}, u32[]{:S(2)}, u32[]{:S(2)}) collective-permute-start(bf16[2,256,128]{2,1,0:T(8,128)(2,1)S(1)} %bitcast.38), channel_id=1, source_target_pairs={{0,2},{1,3},{4,6},{5,7},{8,10},{9,11},{12,14},{13,15},{2,0},{3,1},... | collective-permute-start | bytes 393224 | tf_op jit(solution)/shard_map/ppermute | solution.py:23
  4.6 0.7 %collective-permute-start.3 = (bf16[2,256,128]{2,1,0:T(8,128)(2,1)S(1)}, bf16[2,256,128]{2,1,0:T(8,128)(2,1)S(1)}, u32[]{:S(2)}, u32[]{:S(2)}) collective-permute-start(bf16[2,256,128]{2,1,0:T(8,128)(2,1)S(1)} %bitcast.39), channel_id=1, source_target_pairs={{2,8},{3,11},{6,12},{7,15},{8,2},{9,1},{12,6},{13,5},{18,24},{19,2... | collective-permute-start | bytes 393224 | tf_op jit(solution)/shard_map/ppermute | solution.py:23
  5.3 0.9 %slice_bitcast_fusion = (bf16[128,128]{1,0:T(8,128)(2,1)S(1)}, bf16[128,128]{1,0:T(8,128)(2,1)S(1)}, bf16[128,128]{1,0:T(8,128)(2,1)S(1)}, bf16[128,128]{1,0:T(8...) fusion(bf16[9,128,128]{2,1,0:T(8,128)(2,1)} %param.20), kind=kLoop, calls=%fused_computation.39 | loop fusion | bytes 589824 | tf_op jit(solution)/shard_map/squeeze | solution.py:82
  6.5 0.0 copy-start.6
  6.5 0.1 pad_maximum_fusion.w_conv_ref
  6.7 1.4 %collective-permute-done = bf16[2,256,128]{2,1,0:T(8,128)(2,1)S(1)} collective-permute-done((bf16[2,256,128]{2,1,0:T(8,128)(2,1)S(1)}, bf16[2,256,128]{2,1,0:T(8,128)(2,1)S(1)}, u32[]{:S(2)}, u32[]{:S(2)}) %collective-permute-start) | collective-permute-done | bytes 131104 | tf_op jit(solution)/shard_map/ppermute | solution.py:23
  8.1 1.9 %collective-permute-start.1 = (bf16[4,256,128]{2,1,0:T(8,128)(2,1)S(1)}, bf16[4,256,128]{2,1,0:T(8,128)(2,1)S(1)}, u32[]{:S(2)}, u32[]{:S(2)}) collective-permute-start(bf16[4,256,128]{2,1,0:T(8,128)(2,1)S(1)} %pad_maximum_fusion.1), channel_id=1, source_target_pairs={{0,4},{1,5},{2,6},{3,7},{8,12},{9,13},{10,14},{11,15},{4,0},{5,1},... | collective-permute-start | bytes 786440 | tf_op jit(solution)/shard_map/ppermute | solution.py:23
  10.1 0.0 copy-start
  10.1 0.0 copy-start.1
  10.1 0.0 copy-start.2
  10.1 0.0 copy-start.3
  10.1 0.0 copy-start.4
  10.1 0.0 copy-start.5
  10.1 0.0 copy-start.7
  10.1 0.8 %collective-permute-start.2 = (bf16[4,256,128]{2,1,0:T(8,128)(2,1)S(1)}, bf16[4,256,128]{2,1,0:T(8,128)(2,1)S(1)}, u32[]{:S(2)}, u32[]{:S(2)}) collective-permute-start(bf16[4,256,128]{2,1,0:T(8,128)(2,1)S(1)} %pad_maximum_fusion.1), channel_id=1, source_target_pairs={{4,8},{5,9},{6,10},{7,11},{8,4},{9,5},{10,6},{11,7},{20,24},{21,25... | collective-permute-start | bytes 786440 | tf_op jit(solution)/shard_map/ppermute | solution.py:23
  11.0 0.0 collective-permute-done.3
  11.0 0.7 %collective-permute-start.4 = (bf16[2,256,128]{2,1,0:T(8,128)(2,1)S(1)}, bf16[2,256,128]{2,1,0:T(8,128)(2,1)S(1)}, u32[]{:S(2)}, u32[]{:S(2)}) collective-permute-start(bf16[2,256,128]{2,1,0:T(8,128)(2,1)S(1)} %collective-permute-done.3), channel_id=1, source_target_pairs={{0,0},{1,3},{2,2},{3,1},{4,4},{5,7},{6,6},{7,5},{8,8},{9,11},{10,1... | collective-permute-start | bytes 393224 | tf_op jit(solution)/shard_map/ppermute | solution.py:23
  11.7 3.7 %collective-permute-start.5 = (bf16[4,256,128]{2,1,0:T(8,128)(2,1)S(1)}, bf16[4,256,128]{2,1,0:T(8,128)(2,1)S(1)}, u32[]{:S(2)}, u32[]{:S(2)}) collective-permute-start(bf16[4,256,128]{2,1,0:T(8,128)(2,1)S(1)} %pad_maximum_fusion.1), channel_id=1, source_target_pairs={{0,1},{2,3},{4,5},{6,7},{8,9},{10,11},{12,13},{14,15},{1,0},{3,2},... | collective-permute-start | bytes 786440 | tf_op jit(solution)/shard_map/ppermute | solution.py:23
  15.4 0.0 collective-permute-done.4
  15.4 3.7 %collective-permute-start.8 = (bf16[2,256,128]{2,1,0:T(8,128)(2,1)S(1)}, bf16[2,256,128]{2,1,0:T(8,128)(2,1)S(1)}, u32[]{:S(2)}, u32[]{:S(2)}) collective-permute-start(bf16[2,256,128]{2,1,0:T(8,128)(2,1)S(1)} %collective-permute-done.4), channel_id=1, source_target_pairs={{0,1},{2,3},{4,5},{6,7},{8,9},{10,11},{12,13},{14,15},{1,0},{3,2},... | collective-permute-start | bytes 393224 | tf_op jit(solution)/shard_map/ppermute | solution.py:23
  19.1 0.0 collective-permute-done.1
  19.1 0.0 collective-permute-start.6
  19.2 0.6 %collective-permute-start.7 = (bf16[4,256,128]{2,1,0:T(8,128)(2,1)S(1)}, bf16[4,256,128]{2,1,0:T(8,128)(2,1)S(1)}, u32[]{:S(2)}, u32[]{:S(2)}) collective-permute-start(bf16[4,256,128]{2,1,0:T(8,128)(2,1)S(1)} %collective-permute-done.2), channel_id=1, source_target_pairs={{0,1},{2,3},{4,5},{6,7},{8,9},{10,11},{12,13},{14,15},{1,0},{3,2},... | collective-permute-start | bytes 786440 | tf_op jit(solution)/shard_map/ppermute | solution.py:23
  19.8 0.8 %collective-permute-done.6 = bf16[4,256,128]{2,1,0:T(8,128)(2,1)S(1)} collective-permute-done((bf16[4,256,128]{2,1,0:T(8,128)(2,1)S(1)}, bf16[4,256,128]{2,1,0:T(8,128)(2,1)S(1)}, u32[]{:S(2)}, u32[]{:S(2)}) %collective-permute-start.6) | collective-permute-done | bytes 262176 | tf_op jit(solution)/shard_map/ppermute | solution.py:23
  20.7 0.3 collective-permute-done.7
  21.0 0.0 collective-permute-done.8
  21.2 0.0 copy-start.9
  21.2 0.0 copy-start.10
  21.2 6.7 %edge_update.1 = (bf16[24,256,128]{2,1,0:T(8,128)(2,1)}, f32[32,2,256]{2,1,0:T(2,128)S(1)}) custom-call(s32[2,12]{1,0:T(2,128)S(1)} %fusion.4.index_ref, s32[2,12]{1,0:T(2,128)S(1)} %copy-done.6, bf16[2,256,128]{2,1,0:T(8,128)(2,1)S(1)} %copy-done.1, bf16[2,256,128]{2,1,0:T(8,128)(2,1)S(1)} %copy-done.3, bf16[24,256,128]{2,1,0:T(8,128)(2,1)S(1)} %bitcast.35, ...), custom_call_target="tpu_custom_call" | custom-call | tf_op jit(solution)/shard_map/edge_update/pallas_call | solution.py:239
  27.9 11.9 %all_to_all.5 = f32[16,2,2,256]{3,2,1,0:T(2,128)S(1)} all-to-all(f32[16,2,2,256]{3,2,1,0:T(2,128)S(1)} %bitcast.37), channel_id=1, replica_groups=mesh['groups'=2,'edge'=16] {'edge'}, dimensions={0} | all-to-all | bytes 131072 | tf_op jit(solution)/shard_map/all_to_all | solution.py:260
  39.9 0.6 %fusion.1 = f32[2,256]{1,0:T(2,128)} fusion(f32[2,256]{1,0:T(2,128)S(1)} %copy-done.9, f32[2,1,256]{2,1,0:T(1,128)S(1)} %get-tuple-element.30, f32[2,256]{1,0:T(2,128)S(1)} %copy-done.10, f32[2,1,256]{2,1,0:T(1,128)S(1)} %get-tuple-element.29), kind=kLoop, calls=%fused_computation.52 | loop fusion | flops 1536 | bytes 10240 | tf_op jit(solution)/shard_map/add | solution.py:261
  (41 shorter events, 0.6 us)
Async XLA Ops:
  0.6 5.8 %copy-start.8 = (bf16[128,128]{1,0:T(8,128)(2,1)S(1)}, bf16[128,128]{1,0:T(8,128)(2,1)}, u32[]{:S(2)}) copy-start(bf16[128,128]{1,0:T(8,128)(2,1)} %param.21) | copy-start | bytes 98308
  1.6 6.5 %collective-permute-start = (bf16[2,256,128]{2,1,0:T(8,128)(2,1)S(1)}, bf16[2,256,128]{2,1,0:T(8,128)(2,1)S(1)}, u32[]{:S(2)}, u32[]{:S(2)}) collective-permute-start(bf16[2,256,128]{2,1,0:T(8,128)(2,1)S(1)} %bitcast.38), channel_id=1, source_target_pairs={{0,2},{1,3},{4,6},{5,7},{8,10},{9,11},{12,14},{13,15},{2,0},{3,1},... | collective-permute-start | bytes 393224 | tf_op jit(solution)/shard_map/ppermute | solution.py:23
  4.6 6.4 %collective-permute-start.3 = (bf16[2,256,128]{2,1,0:T(8,128)(2,1)S(1)}, bf16[2,256,128]{2,1,0:T(8,128)(2,1)S(1)}, u32[]{:S(2)}, u32[]{:S(2)}) collective-permute-start(bf16[2,256,128]{2,1,0:T(8,128)(2,1)S(1)} %bitcast.39), channel_id=1, source_target_pairs={{2,8},{3,11},{6,12},{7,15},{8,2},{9,1},{12,6},{13,5},{18,24},{19,2... | collective-permute-start | bytes 393224 | tf_op jit(solution)/shard_map/ppermute | solution.py:23
  6.5 3.6 %copy-start.6 = (s32[2,12]{1,0:T(2,128)S(1)}, s32[2,12]{1,0:T(2,128)}, u32[]{:S(2)}) copy-start(s32[2,12]{1,0:T(2,128)} %target_ref.1) | copy-start | bytes 292
  8.1 11.0 %collective-permute-start.1 = (bf16[4,256,128]{2,1,0:T(8,128)(2,1)S(1)}, bf16[4,256,128]{2,1,0:T(8,128)(2,1)S(1)}, u32[]{:S(2)}, u32[]{:S(2)}) collective-permute-start(bf16[4,256,128]{2,1,0:T(8,128)(2,1)S(1)} %pad_maximum_fusion.1), channel_id=1, source_target_pairs={{0,4},{1,5},{2,6},{3,7},{8,12},{9,13},{10,14},{11,15},{4,0},{5,1},... | collective-permute-start | bytes 786440 | tf_op jit(solution)/shard_map/ppermute | solution.py:23
  10.1 11.0 %copy-start = (bf16[2,12,256,128]{3,2,1,0:T(8,128)(2,1)S(1)}, bf16[2,12,256,128]{3,2,1,0:T(8,128)(2,1)}, u32[]{:S(2)}) copy-start(bf16[2,12,256,128]{3,2,1,0:T(8,128)(2,1)} %param.14) | copy-start | bytes 4718596
  10.1 11.0 %copy-start.1 = (bf16[2,256,128]{2,1,0:T(8,128)(2,1)S(1)}, bf16[2,256,128]{2,1,0:T(8,128)(2,1)}, u32[]{:S(2)}) copy-start(bf16[2,256,128]{2,1,0:T(8,128)(2,1)} %feat_ref.1) | copy-start | bytes 393220
  10.1 11.0 %copy-start.2 = (bf16[4,256,49]{2,1,0:T(8,128)(2,1)S(1)}, bf16[4,256,49]{2,1,0:T(8,128)(2,1)}, u32[]{:S(2)}) copy-start(bf16[4,256,49]{2,1,0:T(8,128)(2,1)} %constant.98.clone.picks_ref) | copy-start | bytes 301060
  10.1 11.0 %copy-start.3 = (bf16[2,256,128]{2,1,0:T(8,128)(2,1)S(1)}, bf16[2,256,128]{2,1,0:T(8,128)(2,1)}, u32[]{:S(2)}) copy-start(bf16[2,256,128]{2,1,0:T(8,128)(2,1)} %ctx_ref.1) | copy-start | bytes 393220
  10.1 11.0 %copy-start.4 = (bf16[256,256]{1,0:T(8,128)(2,1)S(1)}, bf16[256,256]{1,0:T(8,128)(2,1)}, u32[]{:S(2)}) copy-start(bf16[256,256]{1,0:T(8,128)(2,1)} %w_gates_ref.1) | copy-start | bytes 393220
  10.1 11.0 %copy-start.5 = (bf16[49,128]{1,0:T(8,128)(2,1)S(1)}, bf16[49,128]{1,0:T(8,128)(2,1)}, u32[]{:S(2)}) copy-start(bf16[49,128]{1,0:T(8,128)(2,1)} %w_corr_ref.1) | copy-start | bytes 37636
  10.1 11.0 %copy-start.7 = (bf16[2,128]{1,0:T(2,128)(2,1)S(1)}, bf16[2,128]{1,0:T(2,128)(2,1)}, u32[]{:S(2)}) copy-start(bf16[2,128]{1,0:T(2,128)(2,1)} %w_heads_ref.1) | copy-start | bytes 1540
  10.1 9.0 %collective-permute-start.2 = (bf16[4,256,128]{2,1,0:T(8,128)(2,1)S(1)}, bf16[4,256,128]{2,1,0:T(8,128)(2,1)S(1)}, u32[]{:S(2)}, u32[]{:S(2)}) collective-permute-start(bf16[4,256,128]{2,1,0:T(8,128)(2,1)S(1)} %pad_maximum_fusion.1), channel_id=1, source_target_pairs={{4,8},{5,9},{6,10},{7,11},{8,4},{9,5},{10,6},{11,7},{20,24},{21,25... | collective-permute-start | bytes 786440 | tf_op jit(solution)/shard_map/ppermute | solution.py:23
  11.0 4.5 %collective-permute-start.4 = (bf16[2,256,128]{2,1,0:T(8,128)(2,1)S(1)}, bf16[2,256,128]{2,1,0:T(8,128)(2,1)S(1)}, u32[]{:S(2)}, u32[]{:S(2)}) collective-permute-start(bf16[2,256,128]{2,1,0:T(8,128)(2,1)S(1)} %collective-permute-done.3), channel_id=1, source_target_pairs={{0,0},{1,3},{2,2},{3,1},{4,4},{5,7},{6,6},{7,5},{8,8},{9,11},{10,1... | collective-permute-start | bytes 393224 | tf_op jit(solution)/shard_map/ppermute | solution.py:23
  11.7 8.1 %collective-permute-start.5 = (bf16[4,256,128]{2,1,0:T(8,128)(2,1)S(1)}, bf16[4,256,128]{2,1,0:T(8,128)(2,1)S(1)}, u32[]{:S(2)}, u32[]{:S(2)}) collective-permute-start(bf16[4,256,128]{2,1,0:T(8,128)(2,1)S(1)} %pad_maximum_fusion.1), channel_id=1, source_target_pairs={{0,1},{2,3},{4,5},{6,7},{8,9},{10,11},{12,13},{14,15},{1,0},{3,2},... | collective-permute-start | bytes 786440 | tf_op jit(solution)/shard_map/ppermute | solution.py:23
  15.4 5.6 %collective-permute-start.8 = (bf16[2,256,128]{2,1,0:T(8,128)(2,1)S(1)}, bf16[2,256,128]{2,1,0:T(8,128)(2,1)S(1)}, u32[]{:S(2)}, u32[]{:S(2)}) collective-permute-start(bf16[2,256,128]{2,1,0:T(8,128)(2,1)S(1)} %collective-permute-done.4), channel_id=1, source_target_pairs={{0,1},{2,3},{4,5},{6,7},{8,9},{10,11},{12,13},{14,15},{1,0},{3,2},... | collective-permute-start | bytes 393224 | tf_op jit(solution)/shard_map/ppermute | solution.py:23
  19.1 1.5 %collective-permute-start.6 = (bf16[4,256,128]{2,1,0:T(8,128)(2,1)S(1)}, bf16[4,256,128]{2,1,0:T(8,128)(2,1)S(1)}, u32[]{:S(2)}, u32[]{:S(2)}) collective-permute-start(bf16[4,256,128]{2,1,0:T(8,128)(2,1)S(1)} %collective-permute-done.1), channel_id=1, source_target_pairs={{0,1},{2,3},{4,5},{6,7},{8,9},{10,11},{12,13},{14,15},{1,0},{3,2},... | collective-permute-start | bytes 786440 | tf_op jit(solution)/shard_map/ppermute | solution.py:23
  19.2 1.9 %collective-permute-start.7 = (bf16[4,256,128]{2,1,0:T(8,128)(2,1)S(1)}, bf16[4,256,128]{2,1,0:T(8,128)(2,1)S(1)}, u32[]{:S(2)}, u32[]{:S(2)}) collective-permute-start(bf16[4,256,128]{2,1,0:T(8,128)(2,1)S(1)} %collective-permute-done.2), channel_id=1, source_target_pairs={{0,1},{2,3},{4,5},{6,7},{8,9},{10,11},{12,13},{14,15},{1,0},{3,2},... | collective-permute-start | bytes 786440 | tf_op jit(solution)/shard_map/ppermute | solution.py:23
  21.2 18.7 %copy-start.9 = (f32[2,256]{1,0:T(2,128)S(1)}, f32[2,256]{1,0:T(2,128)}, u32[]{:S(2)}) copy-start(f32[2,256]{1,0:T(2,128)} %param.16) | copy-start | bytes 6148
  21.2 18.7 %copy-start.10 = (f32[2,256]{1,0:T(2,128)S(1)}, f32[2,256]{1,0:T(2,128)}, u32[]{:S(2)}) copy-start(f32[2,256]{1,0:T(2,128)} %param.17) | copy-start | bytes 6148
